TPU v7x, 256 devices: a whole 4x4x8 slice. The times are simulated.
256 devices in a mesh: dp: 16 (over x, z_hi, core), tensor: 16 (over y, z_lo).
Axes of the slice: x: 4, y: 4, z: 8 (z_hi: 2, z_lo: 4; z = z_hi * 4 + z_lo), core: 2. Of those that a mesh axis runs over, the one named last changes fastest.
Arguments:
- inputs: bfloat16 [16384, 4096], P(('dp', 'tensor')), may hold values from -36 to 36
- out_grad: bfloat16 [16384, 4096], P(('dp', 'tensor')), may hold values from -1.5 to 1.5
- gain: float32 [4096], replicated, may hold values from 0.25 to 1.75
- w_query: bfloat16 [4096, 4096], P(None, 'tensor'), may hold values from -0.09375 to 0.09375
- w_keyval: bfloat16 [2, 4096, 1024], P(None, 'tensor'), may hold values from -0.09375 to 0.09375
- grad_query: bfloat16 [16384, 4096], P('dp', 'tensor'), may hold values from -1.5 to 1.5
- grad_keyval: bfloat16 [2, 16384, 2048], P(None, 'dp', 'tensor'), may hold values from -1.5 to 1.5
Outputs:
- input_grad: float32 [16384, 4096], P(('dp', 'tensor'))
- query_weight_grad: float32 [4096, 4096], P('dp', 'tensor')
- keyval_weight_grad: float32 [2, 4096, 1024], P(None, 'tensor')
All inputs are finite; a program needn't handle non-finite values.
Results may differ from a plain program's by a relative error of at most 0.0029.
Values may be sent and summed in bfloat16 or wider, within the bound.
No kernel may reach another device: no remote copies, remote signals or barrier semaphores. Data moves between devices by JAX's collectives and lax.ppermute only.
A program may use at most 128 MiB of HBM per device.

v0:
```python
import jax
import jax.numpy as jnp
from jax import lax
from jax.sharding import PartitionSpec as P

KVH = 8
HD = 128


EPSILON = 1e-05


def shards(inputs, out_grad, gain, w_query, w_keyval, grad_query, grad_keyval):
    tensor_size = lax.axis_size("tensor")
    copies = tensor_size // KVH
    keyval_rows = w_keyval.shape[1]
    wide_inputs = inputs.astype(jnp.float32)
    rms_inverse = lax.rsqrt(jnp.mean(wide_inputs * wide_inputs, axis=1, keepdims=True) + EPSILON)
    unit_rows = wide_inputs * rms_inverse
    normed_local = (unit_rows * gain).astype(jnp.bfloat16)
    normed = lax.all_gather(normed_local, "tensor", axis=0, tiled=True)
    query_weight_grad = lax.psum_scatter(
        lax.dot_general(
            normed, grad_query, (((0,), (0,)), ((), ())), preferred_element_type=jnp.float32
        ),
        "dp",
        scatter_dimension=0,
        tiled=True,
    )
    weight_heads = w_keyval.reshape(2, keyval_rows, KVH, 1, HD)
    spread_weight = jnp.broadcast_to(weight_heads, (2, keyval_rows, KVH, copies, HD))
    spread_weight = spread_weight.reshape(2, keyval_rows, KVH * copies * HD)
    keyval_columns = lax.all_to_all(
        spread_weight, "tensor", split_axis=2, concat_axis=1, tiled=True
    )
    partial_value = lax.dot_general(
        grad_query, w_query, (((1,), (1,)), ((), ())), preferred_element_type=jnp.float32
    )
    partial_value = partial_value + jnp.einsum(
        "ptj,pdj->td", grad_keyval, keyval_columns, preferred_element_type=jnp.float32
    )
    normed_grad = lax.psum_scatter(partial_value, "tensor", scatter_dimension=0, tiled=True)
    head_grad = jnp.einsum("td,ptj->pdj", normed, grad_keyval, preferred_element_type=jnp.float32)
    returned = lax.all_to_all(head_grad, "tensor", split_axis=1, concat_axis=2, tiled=True)
    keyval_term = jnp.sum(returned.reshape(2, keyval_rows, KVH, copies, HD), axis=3)
    keyval_term = keyval_term.reshape(2, keyval_rows, KVH * HD)
    keyval_weight_grad = lax.psum(keyval_term, "dp")
    scaled = normed_grad * gain
    mean_term = jnp.mean(scaled * unit_rows, axis=1, keepdims=True)
    input_grad = out_grad.astype(jnp.float32) + rms_inverse * (scaled - unit_rows * mean_term)
    return (input_grad, query_weight_grad, keyval_weight_grad)


def solution(mesh):
    placed = (
        P(("dp", "tensor"), None),
        P(("dp", "tensor"), None),
        P(),
        P(None, "tensor"),
        P(None, "tensor", None),
        P("dp", "tensor"),
        P(None, "dp", "tensor"),
    )
    return jax.shard_map(
        shards,
        mesh=mesh,
        in_specs=placed,
        out_specs=(P(("dp", "tensor"), None), P("dp", "tensor"), P(None, "tensor", None)),
        check_vma=False,
    )
```

profile of v0, /device:TPU:17, one launch (start us, length us, event | category | flops | bytes accessed | tf_op | source)
XLA Modules:
  0.0 1084.7 jit_solution(3150637396269902612)
XLA Ops:
  7.2 0.0 copy-start
  7.2 0.0 reduce-scatter.3.cloned.1.call-start
  7.2 2.6 copy.24
  9.9 1.6 broadcast_in_dim.5
  11.5 55.2 %all_to_all.33 = bf16[2,256,2048]{1,0,2:T(2,128)(2,1)S(1)} all-to-all(bf16[2,256,2048]{1,0,2:T(2,128)(2,1)S(1)} %bitcast.34), channel_id=1, replica_groups=mesh['dp'=16,'tensor'=16] {'tensor'}, dimensions={2} | all-to-all | bytes 4194304 | tf_op jit(solution)/shard_map/all_to_all | solution.py:33
  66.7 0.0 copy-start.4
  66.7 1.6 copy.18
  68.3 3.9 copy.19
  72.3 0.0 copy-done.4
  72.3 0.0 copy-start.3
  72.3 9.8 fusion.14
  82.0 0.0 copy-done
  82.0 0.0 copy-done.3
  82.0 13.9 %bitcast_add_fusion = f32[1024,4096]{1,0:T(8,128)} fusion(f32[1024,4096,1]{1,0,2:T(8,128)} %fusion.14, bf16[1024,256]{1,0:T(8,128)(2,1)S(1)} %copy-done.3, bf16[4096,256]{1,0:T(8,128)(2,1)S(1)} %copy-done), kind=kOutput, calls=%fused_computation | convolution fusion | flops 2151677952 | bytes 36175872 | tf_op jit(solution)/shard_map/dot_general | solution.py:36
  95.9 0.0 copy-start.2
  95.9 0.0 copy-start.6
  95.9 0.0 copy-start.5
  95.9 0.0 reduce-scatter.3.cloned.1.call-update
  96.0 0.0 all-gather.2.cloned.1.call-start
  96.0 1.0 copy-done.2
  97.0 0.2 fusion.13
  97.2 353.4 %reduce-scatter.3.cloned.1.call-done = f32[64,4096]{1,0:T(8,128)} async-done(((f32[1024,4096]{1,0:T(8,128)}), f32[64,4096]{1,0:T(8,128)}) %reduce-scatter.3.cloned.1.call-update) | async-done | bytes 1048592 | tf_op jit(solution)/shard_map/reduce_scatter | solution.py:42
  450.6 0.0 copy-done.6
  450.6 1.5 fusion.8
  452.2 0.0 copy-done.5
  452.2 2.8 fusion.12
  454.9 0.0 all-gather.2.cloned.1.call-update
  455.0 0.0 all-reduce.2.cloned.1.call-start
  455.0 187.1 %all-gather.2.cloned.1.call-done = bf16[1024,4096]{1,0:T(8,128)(2,1)} async-done(((bf16[64,4096]{1,0:T(8,128)(2,1)}), bf16[1024,4096]{1,0:T(8,128)(2,1)}) %all-gather.2.cloned.1.call-update) | async-done | bytes 8388624 | tf_op jit(solution)/shard_map/all_gather | solution.py:21
  642.2 6.0 fusion.2
  648.2 15.6 %copy.20 = f32[2,4096,128]{2,0,1:T(2,128)S(1)} copy(f32[2,4096,128]{2,1,0:T(8,128)S(1)} %fusion.2) | data formatting | bytes 8388608 | tf_op jit(solution)/shard_map/td,ptj->pdj/transpose | solution.py:43
  663.8 98.0 %all_to_all.34 = f32[2,4096,128]{2,0,1:T(2,128)} all-to-all(f32[2,4096,128]{2,0,1:T(2,128)S(1)} %copy.20), channel_id=1, replica_groups=mesh['dp'=16,'tensor'=16] {'tensor'}, dimensions={1} | all-to-all | bytes 8388608 | tf_op jit(solution)/shard_map/all_to_all | solution.py:44
  761.8 5.6 reduce
  767.4 2.3 copy.26
  769.7 0.0 all-reduce.2.cloned.1.call-update
  769.7 0.0 reduce-scatter.5.cloned.1.call-start
  769.8 7.8 fusion.15
  777.6 0.0 copy-start.1
  777.6 0.0 reduce-scatter.5.cloned.1.call-update
  777.6 192.2 %all-reduce.2.cloned.1.call-done = f32[2,256,1024]{1,2,0:T(8,128)} async-done(((f32[2,256,1024]{1,2,0:T(8,128)}), f32[2,256,1024]{1,2,0:T(8,128)}) %all-reduce.2.cloned.1.call-update) | async-done | bytes 2097168 | tf_op jit(solution)/shard_map/psum | solution.py:47
  969.8 2.9 copy.23
  972.7 105.5 %reduce-scatter.5.cloned.1.call-done = f32[256,256]{1,0:T(8,128)} async-done(((f32[4096,256]{1,0:T(8,128)}), f32[256,256]{1,0:T(8,128)}) %reduce-scatter.5.cloned.1.call-update) | async-done | bytes 262160 | tf_op jit(solution)/shard_map/reduce_scatter | solution.py:22
  1078.2 0.0 copy-done.1
  (2 shorter events, 0.0 us)
Async XLA Ops:
  7.2 74.9 %copy-start = (bf16[4096,256]{1,0:T(8,128)(2,1)S(1)}, bf16[4096,256]{1,0:T(8,128)(2,1)}, u32[]{:S(2)}) copy-start(bf16[4096,256]{1,0:T(8,128)(2,1)} %param.10) | copy-start | bytes 6291460
  7.2 443.4 %reduce-scatter.3.cloned.1.call-start = ((), (), s32[]{:S(2)}) async-start(), calls=%async_computation.4 | async-start | bytes 17825792 | tf_op jit(solution)/shard_map/reduce_scatter | solution.py:42
  66.7 5.5 copy-start.4
  72.3 9.8 copy-start.3
  95.9 1.0 copy-start.2
  95.9 354.7 %copy-start.6 = (f32[4096]{0:T(1024)S(1)}, f32[4096]{0:T(1024)}, u32[]{:S(2)}) copy-start(f32[4096]{0:T(1024)} %param.9) | copy-start | bytes 49156
  95.9 356.3 %copy-start.5 = (bf16[64,4096]{1,0:T(8,128)(2,1)S(1)}, bf16[64,4096]{1,0:T(8,128)(2,1)}, u32[]{:S(2)}) copy-start(bf16[64,4096]{1,0:T(8,128)(2,1)} %param.8) | copy-start | bytes 1572868
  96.0 546.2 %all-gather.2.cloned.1.call-start = ((), (), s32[]{:S(2)}) async-start(), calls=%async_computation.5 | async-start | bytes 8912896 | tf_op jit(solution)/shard_map/all_gather | solution.py:21
  455.0 514.8 %all-reduce.2.cloned.1.call-start = ((), (), s32[]{:S(2)}) async-start(), calls=%async_computation.7 | async-start | bytes 4194304 | tf_op jit(solution)/shard_map/psum | solution.py:47
  769.7 308.4 %reduce-scatter.5.cloned.1.call-start = ((), (), s32[]{:S(2)}) async-start(), calls=%async_computation.6 | async-start | bytes 4456448 | tf_op jit(solution)/shard_map/reduce_scatter | solution.py:22
  777.6 300.6 %copy-start.1 = (bf16[4096,256]{1,0:T(8,128)(2,1)S(1)}, bf16[4096,256]{1,0:T(8,128)(2,1)}, u32[]{:S(2)}) copy-start(bf16[4096,256]{1,0:T(8,128)(2,1)} %param.10) | copy-start | bytes 6291460
Sparse Core Ops, SparseCore 0:
  96.1 354.5 reduce-scatter.2
  455.1 187.0 all-gather.1
  769.8 199.9 all-reduce.1
  974.6 103.5 reduce-scatter.4
where the time goes:
time: 1090 us; the launch traced here: 1080 us
  waiting for transfers between devices  838 us (77%)
  blocking collectives  153 us (14%)
  matrix products  37.4 us (3%)
  local copies, waits for them, and re-layouts  31.6 us (3%)
  between operations  13.8 us (1%)
    reduce_scatter x1, waiting for transfers between devices, shards(): lax.psum_scatter(partial_value, 'tensor', scatter_dimension=0, tiled=True)  353 us
    psum x1, waiting for transfers between devices, shards(): keyval_weight_grad = lax.psum(keyval_term, 'dp')  192 us
    all_gather x1, waiting for transfers between devices, shards(): normed = lax.all_gather(normed_local, 'tensor', axis=0, tiled=True)  187 us
    reduce_scatter x1, waiting for transfers between devices, shards(): lax.psum_scatter(lax.dot_general(normed, grad_query, (((0,), (0,)), ((),...  105 us
    all_to_all x1, blocking collectives, shards(): lax.all_to_all(head_grad, 'tensor', split_axis=1, concat_axis=2, tiled=True)  98 us
    all_to_all x1, blocking collectives, shards(): lax.all_to_all(spread_weight, 'tensor', split_axis=2, concat_axis=1, tile...  55.2 us
  transfers between devices with their start and end apart: 4, of which 4 were waited for; matrix products, arithmetic and copies ran while one was open for 1% of the time, Pallas kernels for 0%

commit v1 on v0

v1 whole, which is shorter than its diff:
```python
import numpy as np
import jax
import jax.numpy as jnp
from jax import lax
from jax.experimental import pallas as pl
from jax.experimental.pallas import tpu as pltpu
from jax.sharding import PartitionSpec as P

EPSILON = 1e-05
BF = jnp.bfloat16
F32 = jnp.float32

INNER = (0, 1, 4, 5)
OUTER = (0, 2, 12, 14)
HEAD_STEP = (0, 1, 6, 7)


def alpha_of(v):
    return (v ^ (v >> 1)) & 1


def ring_place(alpha, beta):
    return alpha ^ (3 * beta)


def place_table():
    rows = []
    for device in range(256):
        dp, t = divmod(device, 16)
        x, c = dp >> 2, dp & 1
        h = (dp >> 1) & 1
        y, z = divmod(t, 4)
        z0, z1 = z & 1, z >> 1
        base = 4 * alpha_of(y) + z0
        outer = 2 * (y >> 1) + z1
        rows.append(
            (
                base,
                t,
                outer,
                x,
                c,
                c ^ z0,
                alpha_of(x) ^ alpha_of(y),
                x >> 1,
                h,
                base ^ OUTER[x],
                (2 * (y ^ (x >> 1)) + z1),
                x & 1,
                (2 * alpha_of(y)) ^ HEAD_STEP[x],
                0,
                0,
                0,
            )
        )
    return np.array(rows, np.int32)


TABLE = place_table()


def exchange(v, axis, flip):
    return lax.ppermute(v, axis, [(i, i ^ flip) for i in range(16)])


def query_turn():
    pairs = []
    for device in range(256):
        dp, t = divmod(device, 16)
        x, h, c = dp >> 2, (dp >> 1) & 1, dp & 1
        y, z = divmod(t, 4)
        x_to = ring_place(alpha_of(y), x >> 1)
        y_to = ring_place(alpha_of(x), y >> 1)
        z_to, c_to = (z & 2) | c, z & 1
        pairs.append((device, (x_to * 4 + h * 2 + c_to) * 16 + y_to * 4 + z_to))
    return pairs


def keyval_turn():
    pairs = []
    for device in range(256):
        dp, t = divmod(device, 16)
        x = dp >> 2
        y, z = divmod(t, 4)
        x_to = 2 * (y >> 1) + (z >> 1)
        y_to = ring_place(alpha_of(y), x >> 1)
        z_to = 2 * (x & 1) + (z & 1)
        pairs.append((device, (x_to * 4 + (dp & 3)) * 16 + y_to * 4 + z_to))
    return pairs


SMEM = pl.BlockSpec(memory_space=pltpu.SMEM)
VMEM = pl.BlockSpec(memory_space=pltpu.VMEM)
ANY = pl.BlockSpec(memory_space=pl.ANY)


def call(kernel, outs, place, args, scratch=(), flops=0, moved=1 << 20, space=VMEM, limit=40):
    return pl.pallas_call(
        kernel,
        out_shape=[jax.ShapeDtypeStruct(s, d) for s, d in outs],
        in_specs=[SMEM] + [space] * len(args),
        out_specs=[space] * len(outs),
        scratch_shapes=list(scratch),
        compiler_params=pltpu.CompilerParams(vmem_limit_bytes=limit << 20),
        cost_estimate=pl.CostEstimate(flops=flops, bytes_accessed=moved, transcendentals=0),
    )(place, *args)


def block(index, size):
    return pl.ds(pl.multiple_of(index * size, size), size)


def norm_kernel(place, x_ref, gain_ref, o0, o1, o2, o3, scr):
    wide = x_ref[...].astype(F32)
    inverse = lax.rsqrt(jnp.mean(wide * wide, axis=1, keepdims=True) + EPSILON)
    scr[...] = ((wide * inverse) * gain_ref[...]).astype(BF)
    base = place[0]
    for k, out in enumerate((o0, o1, o2, o3)):
        for j in range(4):
            out[:, 256 * j : 256 * (j + 1)] = scr[:, block(base ^ (INNER[k] ^ OUTER[j]), 256)]


def weight_pick_kernel(place, wq, wkv, q0, q1, q2, q3, k0, k1, k2, k3, sem):
    copies = []
    for k, out in enumerate((q0, q1, q2, q3)):
        copies.append(pltpu.make_async_copy(wq.at[block(place[9] ^ INNER[k], 256), :], out, sem.at[k]))
    for j, out in enumerate((k0, k1, k2, k3)):
        head = place[10] ^ HEAD_STEP[j]
        copies.append(pltpu.make_async_copy(wkv.at[place[11], :, block(head, 128)], out, sem.at[4 + j]))
    for copy in copies:
        copy.start()
    for copy in copies:
        copy.wait()


def weight_lay_kernel(place, q0, q1, q2, q3, k0, k1, k2, k3, out):
    x, outer = place[3], place[2]
    for i, ref in enumerate((q0, q1, q2, q3)):
        for k in range(4):
            out[x ^ i, :, 256 * k : 256 * (k + 1)] = ref[k]
    for i, ref in enumerate((k0, k1, k2, k3)):
        lanes = pl.ds(pl.multiple_of(1024 + 128 * (x ^ i), 128), 128)
        for j in range(4):
            out[outer ^ j, :, lanes] = ref[j]


def lay_rows(t, j, g, kv, scr):
    for k in range(4):
        rows = block(t ^ (OUTER[j] ^ INNER[k]), 64)
        here = slice(64 * k, 64 * (k + 1))
        for n in range(4):
            scr[here, 256 * n : 256 * (n + 1)] = g[n][rows, :]
        for a in range(2):
            for p in range(2):
                at = 1024 + 128 * (2 * a + p)
                scr[here, at : at + 128] = kv[a][p, rows, :]


def rows_grad_kernel(which, place, g0, g1, g2, g3, kv0, kv1, w, o0, o1, scr):
    t = place[1]
    for j, out in zip(which, (o0, o1)):
        lay_rows(t, j, (g0, g1, g2, g3), (kv0, kv1), scr)
        left = scr[...]
        for d in range(4):
            value = lax.dot_general(left, w[d], (((1,), (1,)), ((), ())), preferred_element_type=F32)
            out[:, 256 * d : 256 * (d + 1)] = value.astype(out.dtype)


def weight_grad_kernel(place, n0, n1, n2, n3, g0, g1, g2, g3, kv0, kv1, q_keep, q_send, kv_keep, kv_send, right):
    t, c, side = place[1], place[4], place[5]
    q_pairs = ((g0, g1), (g2, g3))
    for half, q_out, kv_out in ((1, q_send, kv_send), (0, q_keep, kv_keep)):
        flip = (side ^ half) == 1
        for j in range(4):
            for k in range(4):
                rows = block(t ^ (OUTER[j] ^ INNER[k]), 64)
                here = slice(256 * j + 64 * k, 256 * j + 64 * (k + 1))
                for a in range(2):
                    right[here, 256 * a : 256 * (a + 1)] = jnp.where(flip, q_pairs[a][1][rows, :], q_pairs[a][0][rows, :])
                    kv = (kv0, kv1)[a]
                    right[here, 512 + 128 * a : 512 + 128 * (a + 1)] = kv[c ^ half, rows, :]
        for d in range(4):
            total = None
            for j, n in enumerate((n0, n1, n2, n3)):
                value = lax.dot_general(
                    n[:, 256 * d : 256 * (d + 1)],
                    right[256 * j : 256 * (j + 1), :],
                    (((0,), (0,)), ((), ())),
                    preferred_element_type=F32,
                )
                total = value if total is None else total + value
            rows = slice(256 * d, 256 * (d + 1))
            q_out[0, rows, :] = total[:, :256]
            q_out[1, rows, :] = total[:, 256:512]
            kv_out[rows, :] = total[:, 512:]


def pair_sum_kernel(place, q_keep, q_got, kv_keep, kv_got, o0, o1, o2, o3):
    for i, out in enumerate((o0, o1, o2, o3)):
        a = place[6] ^ (0, 1, 1, 0)[i]
        rows = block(place[7] ^ (i >> 1), 512)
        out[:512, :] = (q_keep[a, rows, :] + q_got[a, rows, :]).astype(out.dtype)
        rows = block(place[3] ^ i, 256)
        out[512:, :] = (kv_keep[rows, :] + kv_got[rows, :]).astype(out.dtype)


def ring_sum_kernel(place, own, r1, r2, r3, q_keep, q_send, kv):
    h = place[8]

    def total(rows):
        return own[rows, :] + r1[rows, :].astype(F32) + r2[rows, :].astype(F32) + r3[rows, :].astype(F32)

    q_keep[...] = total(block(h, 256))
    q_send[...] = total(block(h ^ 1, 256)).astype(BF)
    kv[...] = total(pl.ds(512, 256))


def keyval_lay_kernel(place, a0, a1, a2, a3, b0, b1, b2, b3, out):
    c, head = place[4], place[12]
    for half, refs in ((0, (a0, a1, a2, a3)), (1, (b0, b1, b2, b3))):
        for i, ref in enumerate(refs):
            for a in range(2):
                lanes = block(head ^ (HEAD_STEP[i] ^ (2 * a)), 128)
                out[c ^ half, :, lanes] = ref[:, 128 * a : 128 * (a + 1)]


def input_grad_kernel(place, x_ref, og_ref, gain_ref, p0, p1, p2, p3, out, scaled):
    base = place[0]
    for k, ref in enumerate((p0, p1, p2, p3)):
        for j in range(4):
            lanes = block(base ^ (INNER[k] ^ OUTER[j]), 256)
            scaled[:, lanes] = ref[:, 256 * j : 256 * (j + 1)].astype(F32) * gain_ref[:, lanes]
    wide = x_ref[...].astype(F32)
    inverse = lax.rsqrt(jnp.mean(wide * wide, axis=1, keepdims=True) + EPSILON)
    unit = wide * inverse
    grad = scaled[...]
    mean_term = jnp.mean(grad * unit, axis=1, keepdims=True)
    out[...] = og_ref[...].astype(F32) + inverse * (grad - unit * mean_term)


def shards(inputs, out_grad, gain, w_query, w_keyval, grad_query, grad_keyval):
    device = lax.axis_index("dp") * 16 + lax.axis_index("tensor")
    place = lax.dynamic_index_in_dim(jnp.asarray(TABLE), device, 0, keepdims=False)
    gain_row = gain.reshape(1, 4096)

    kv_pair = exchange(grad_keyval, "tensor", 1)
    g = [grad_query, exchange(grad_query, "tensor", 1), exchange(grad_query, "tensor", 4)]
    kv_own = (grad_keyval.astype(F32) + kv_pair.astype(F32)).astype(BF)
    kv_far = exchange(kv_own, "tensor", 4)
    g.append(exchange(g[1], "tensor", 4))

    pieces = call(norm_kernel, [((64, 1024), BF)] * 4, place, (inputs, gain_row), [pltpu.VMEM((64, 4096), BF)])
    rows = [pieces[0]] + [exchange(pieces[k], "tensor", INNER[k]) for k in (1, 2, 3)]
    n = [jnp.concatenate(rows, axis=0)]
    n.append(exchange(n[0], "tensor", 2))
    n.append(exchange(n[0], "tensor", 12))
    n.append(exchange(n[1], "tensor", 12))

    picked = call(
        weight_pick_kernel,
        [((256, 256), BF)] * 4 + [((256, 128), BF)] * 4,
        place,
        (w_query, w_keyval),
        [pltpu.SemaphoreType.DMA((8,))],
        space=ANY,
    )
    wq = jnp.stack([picked[0]] + [exchange(picked[k], "tensor", INNER[k]) for k in (1, 2, 3)])
    wkv = jnp.stack([picked[4]] + [exchange(picked[4 + j], "tensor", OUTER[j]) for j in (1, 2, 3)])
    wqs = [wq] + [exchange(wq, "dp", 4 * i) for i in (1, 2, 3)]
    wkvs = [wkv] + [exchange(wkv, "dp", 4 * i) for i in (1, 2, 3)]
    (w,) = call(weight_lay_kernel, [((4, 256, 1536), BF)], place, (*wqs, *wkvs))

    def rows_grad(which, kind):
        return call(
            lambda *refs: rows_grad_kernel(which, *refs),
            [((256, 1024), kind)] * 2,
            place,
            (*g, kv_own, kv_far, w),
            [pltpu.VMEM((256, 1536), BF)],
            flops=2 * 512 * 1024 * 1536,
        )

    both, beta = rows_grad((3, 2), BF)
    both_got = exchange(both, "tensor", 12)
    beta_got = exchange(beta, "tensor", 12)
    side, own = rows_grad((1, 0), F32)
    side_got = exchange((side + both_got.astype(F32)).astype(BF), "tensor", 2)
    own = own + beta_got.astype(F32) + side_got.astype(F32)
    parts = [own[64 * k : 64 * (k + 1)] for k in range(4)]
    parts = [parts[0]] + [exchange(parts[k].astype(BF), "tensor", INNER[k]) for k in (1, 2, 3)]
    (input_grad,) = call(
        input_grad_kernel,
        [((64, 4096), F32)],
        place,
        (inputs, out_grad, gain_row, *parts),
        [pltpu.VMEM((64, 4096), F32)],
    )

    q_keep, q_send, kv_keep, kv_send = call(
        weight_grad_kernel,
        [((2, 1024, 256), F32)] * 2 + [((1024, 256), F32)] * 2,
        place,
        (*n, *g, kv_own, kv_far),
        [pltpu.VMEM((1024, 768), BF)],
        flops=2 * 1024 * 1024 * 1536,
    )
    q_got, kv_got = exchange(q_send, "dp", 1), exchange(kv_send, "dp", 1)
    sums = call(
        pair_sum_kernel,
        [((768, 256), F32)] + [((768, 256), BF)] * 3,
        place,
        (q_keep, q_got, kv_keep, kv_got),
    )
    got = [exchange(sums[i], "dp", 4 * i) for i in (1, 2, 3)]
    q_keep, q_send, kv = call(
        ring_sum_kernel,
        [((256, 256), F32), ((256, 256), BF), ((256, 256), F32)],
        place,
        (sums[0], *got),
    )
    q_block = q_keep + exchange(q_send, "dp", 2).astype(F32)
    query_weight_grad = lax.ppermute(q_block, ("dp", "tensor"), query_turn())
    kv = kv + exchange(kv, "dp", 2)
    kv = lax.ppermute(kv, ("dp", "tensor"), keyval_turn())
    near = [kv] + [exchange(kv, "dp", 4 * i) for i in (1, 2, 3)]
    far = [exchange(v, "dp", 1) for v in near]
    (keyval_weight_grad,) = call(keyval_lay_kernel, [((2, 256, 1024), F32)], place, (*near, *far))
    return (input_grad, query_weight_grad, keyval_weight_grad)


def solution(mesh):
    placed = (
        P(("dp", "tensor"), None),
        P(("dp", "tensor"), None),
        P(),
        P(None, "tensor"),
        P(None, "tensor", None),
        P("dp", "tensor"),
        P(None, "dp", "tensor"),
    )
    return jax.shard_map(
        shards,
        mesh=mesh,
        in_specs=placed,
        out_specs=(P(("dp", "tensor"), None), P("dp", "tensor"), P(None, "tensor", None)),
        check_vma=False,
    )
```

time: 1090 us -> 231 us (0.21)
  waiting for transfers between devices: 838 us -> 110 us
  blocking collectives: 153 us -> 0 us
  starting transfers between devices: 0.16 us -> 93.4 us
  matrix products: 37.4 us -> 0 us
  local copies, waits for them, and re-layouts: 31.6 us -> 3.34 us
  Pallas kernels: 0 us -> 18 us
  between operations: 13.8 us -> 0.92 us
    reduce_scatter x2 -> x0, waiting for transfers between devices: 459 us -> none  [the longest x1 353 us: shards(): lax.psum_scatter(partial_value, 'tensor', scatter_dimension=0, tiled=True)]
    psum x1 -> x0, waiting for transfers between devices: 192 us -> none  [shards(): keyval_weight_grad = lax.psum(keyval_term, 'dp')]
    all_gather x1 -> x0, waiting for transfers between devices: 187 us -> none  [shards(): normed = lax.all_gather(normed_local, 'tensor', axis=0, tiled=True)]
    all_to_all x2 -> x0, blocking collectives: 153 us -> none  [the longest x1 98 us: shards(): lax.all_to_all(head_grad, 'tensor', split_axis=1, concat_axis=2, tiled=True)]
    ppermute x0 -> x45, waiting for transfers between devices: none -> 110 us  [the longest x43 110 us: exchange(): return lax.ppermute(v, axis, [(i, i ^ flip) for i in range(16)])]
    ppermute x0 -> x45, starting transfers between devices: none -> 93.4 us  [the longest x43 89.6 us: exchange(): return lax.ppermute(v, axis, [(i, i ^ flip) for i in range(16)])]
    dot_general x4 -> x0, matrix products: 37.4 us -> none  [the longest x1 13.9 us: shards(): lax.dot_general(grad_query, w_query, (((1,), (1,)), ((), ())), preferred_...]
    pallas_call x0 -> x10, Pallas kernels: none -> 18 us  [call(): pl.pallas_call(kernel, out_shape=[jax.ShapeDtypeStruct(s, d) for s, d in...]
  transfers between devices with their start and end apart: 4 -> 45, of which waited for: 4 -> 19; matrix products, arithmetic and copies ran while one was open for 1% -> 1% of each run, Pallas kernels for 0% -> 5%
where the time goes in v1:
time: 231 us; the launch traced here: 228 us
  waiting for transfers between devices  110 us (48%)
  starting transfers between devices  93.4 us (40%)
  Pallas kernels  18 us (8%)
  local copies, waits for them, and re-layouts  3.34 us (1%)
    ppermute x43, waiting for transfers between devices, exchange(): return lax.ppermute(v, axis, [(i, i ^ flip) for i in range(16)])  110 us
    ppermute x43, starting transfers between devices, exchange(): return lax.ppermute(v, axis, [(i, i ^ flip) for i in range(16)])  89.6 us
    pallas_call x10, Pallas kernels, call(): pl.pallas_call(kernel, out_shape=[jax.ShapeDtypeStruct(s, d) for s, d in...  18 us
  transfers between devices with their start and end apart: 45, of which 19 were waited for; matrix products, arithmetic and copies ran while one was open for 1% of the time, Pallas kernels for 5%

profile of v1, /device:TPU:17, one launch (start us, length us, event | category | flops | bytes accessed | tf_op | source)
XLA Modules:
  0.0 227.5 jit_solution(18322587139356281471)
XLA Ops:
  0.6 0.8 dynamic-slice_bitcast_fusion.place.refs_0_
  1.4 1.0 copy-done.2
  2.4 0.7 copy-done.6
  3.2 0.9 shard_map.108
  4.1 1.7 collective-permute-start.23
  5.8 1.0 collective-permute-start.24
  7.1 1.4 collective-permute-start.3
  8.9 1.0 collective-permute-done.24
  9.9 1.9 collective-permute-done.25
  11.8 3.1 %collective-permute-start.26 = (bf16[256,1024]{1,0:T(8,128)(2,1)S(1)}, bf16[256,1024]{1,0:T(8,128)(2,1)S(1)}, u32[]{:S(2)}, u32[]{:S(2)}) collective-permute-start(bf16[256,1024]{1,0:T(8,128)(2,1)S(1)} %constant_dynamic-update-slice_fusion.n0), channel_id=1, source_target_pairs={{0,2},{1,3},{2,0},{3,1},{4,6},{5,7},{6,4},{7,5},{8,10},{9,11},{10,... | collective-permute-start | bytes 1572872 | tf_op jit(solution)/shard_map/ppermute | solution.py:63
  14.9 0.5 collective-permute-start.1
  15.5 18.1 %collective-permute-done.3 = bf16[2,1024,128]{2,1,0:T(8,128)(2,1)S(1)} collective-permute-done((bf16[2,1024,128]{2,1,0:T(8,128)(2,1)}, bf16[2,1024,128]{2,1,0:T(8,128)(2,1)S(1)}, u32[]{:S(2)}, u32[]{:S(2)}) %collective-permute-start.3) | collective-permute-done | bytes 524320 | tf_op jit(solution)/shard_map/ppermute | solution.py:63
  33.6 1.2 add_convert_fusion.1.refs_5_.kv0
  34.8 1.1 collective-permute-start.4
  35.9 8.9 %collective-permute-done.refs_2_.g1 = bf16[1024,256]{1,0:T(8,128)(2,1)S(1)} collective-permute-done((bf16[1024,256]{1,0:T(8,128)(2,1)}, bf16[1024,256]{1,0:T(8,128)(2,1)S(1)}, u32[]{:S(2)}, u32[]{:S(2)}) %collective-permute-start) | collective-permute-done | bytes 524320 | tf_op jit(solution)/shard_map/ppermute | solution.py:63
  44.8 1.0 collective-permute-start.2
  45.9 0.6 collective-permute-start.28
  46.5 12.4 %collective-permute-done.2.refs_4_.g3 = bf16[1024,256]{1,0:T(8,128)(2,1)S(1)} collective-permute-done((bf16[1024,256]{1,0:T(8,128)(2,1)S(1)}, bf16[1024,256]{1,0:T(8,128)(2,1)S(1)}, u32[]{:S(2)}, u32[]{:S(2)}) %collective-permute-start.2) | collective-permute-done | bytes 524320 | tf_op jit(solution)/shard_map/ppermute | solution.py:63
  58.9 4.1 %shard_map.109 = (f32[2,1024,256]{2,1,0:T(8,128)S(1)}, f32[2,1024,256]{2,1,0:T(8,128)S(1)}, f32[1024,256]{1,0:T(8,128)S(1)}, f32[1024,256]{1,0:T(8,128)S(1)}) custom-call(s32[16]{0:T(128)S(1)} %dynamic-slice_bitcast_fusion.place.refs_0_, bf16[256,1024]{1,0:T(8,128)(2,1)S(1)} %constant_dynamic-update-slice_fusion.n0, ...), custom_call_target="tpu_custom_call" | custom-call | flops 3221225472 | bytes 1048576 | tf_op jit(solution)/shard_map/pallas_call | solution.py:98
  63.0 1.7 collective-permute-start.29
  64.7 1.4 shard_map.103
  66.1 2.8 %collective-permute-start.11 = (bf16[256,128]{1,0:T(8,128)(2,1)S(1)}, bf16[256,128]{1,0:T(8,128)(2,1)S(1)}, u32[]{:S(2)}, u32[]{:S(2)}) collective-permute-start(bf16[256,128]{1,0:T(8,128)(2,1)S(1)} %get-tuple-element.35), channel_id=1, source_target_pairs={{0,2},{1,3},{2,0},{3,1},{4,6},{5,7},{6,4},{7,5},{8,10},{9,11},{10,... | collective-permute-start | bytes 196616 | tf_op jit(solution)/shard_map/ppermute | solution.py:63
  69.1 1.1 collective-permute-start.13
  70.2 1.2 collective-permute-done.11
  71.4 0.7 collective-permute-done.12
  72.0 2.0 collective-permute-done.13
  74.0 1.3 collective-permute-start.14
  75.3 2.2 collective-permute-start.5
  77.5 3.1 %collective-permute-start.6 = (bf16[256,256]{1,0:T(8,128)(2,1)S(1)}, bf16[256,256]{1,0:T(8,128)(2,1)S(1)}, u32[]{:S(2)}, u32[]{:S(2)}) collective-permute-start(bf16[256,256]{1,0:T(8,128)(2,1)S(1)} %get-tuple-element.32), channel_id=1, source_target_pairs={{0,4},{1,5},{2,6},{3,7},{4,0},{5,1},{6,2},{7,3},{8,12},{9,13},{10,... | collective-permute-start | bytes 393224 | tf_op jit(solution)/shard_map/ppermute | solution.py:63
  80.6 2.5 %collective-permute-start.15 = (bf16[4,256,128]{2,1,0:T(8,128)(2,1)S(1)}, bf16[4,256,128]{2,1,0:T(8,128)(2,1)S(1)}, u32[]{:S(2)}, u32[]{:S(2)}) collective-permute-start(bf16[4,256,128]{2,1,0:T(8,128)(2,1)S(1)} %pad_maximum_fusion.1.k0), channel_id=1, source_target_pairs={{0,128},{16,144},{32,160},{48,176},{64,192},{80,208},{96,224},{112... | collective-permute-start | bytes 786440 | tf_op jit(solution)/shard_map/ppermute | solution.py:63
  83.1 0.9 collective-permute-done.6
  84.0 2.5 %collective-permute-done.7 = bf16[256,256]{1,0:T(8,128)(2,1)S(1)} collective-permute-done((bf16[256,256]{1,0:T(8,128)(2,1)S(1)}, bf16[256,256]{1,0:T(8,128)(2,1)S(1)}, u32[]{:S(2)}, u32[]{:S(2)}) %collective-permute-start.7) | collective-permute-done | bytes 131104 | tf_op jit(solution)/shard_map/ppermute | solution.py:63
  86.5 1.9 collective-permute-start.10
  88.7 1.7 collective-permute-start.9
  90.4 1.8 collective-permute-start.16
  92.3 23.5 %collective-permute-done.16.k3 = bf16[4,256,128]{2,1,0:T(8,128)(2,1)S(1)} collective-permute-done((bf16[4,256,128]{2,1,0:T(8,128)(2,1)S(1)}, bf16[4,256,128]{2,1,0:T(8,128)(2,1)S(1)}, u32[]{:S(2)}, u32[]{:S(2)}) %collective-permute-start.16) | collective-permute-done | bytes 262176 | tf_op jit(solution)/shard_map/ppermute | solution.py:63
  115.8 0.9 shard_map.104.refs_7_
  116.7 3.5 %collective-permute-start.30 = (f32[1024,256]{1,0:T(8,128)S(1)}, f32[1024,256]{1,0:T(8,128)S(1)}, u32[]{:S(2)}, u32[]{:S(2)}) collective-permute-start(f32[1024,256]{1,0:T(8,128)S(1)} %get-tuple-element.49), channel_id=1, source_target_pairs={{0,16},{16,0},{32,48},{48,32},{64,80},{80,64},{96,112},{112,96},{1... | collective-permute-start | bytes 3145736 | tf_op jit(solution)/shard_map/ppermute | solution.py:63
  120.2 2.4 %shard_map.106 = (bf16[256,1024]{1,0:T(8,128)(2,1)S(1)}, bf16[256,1024]{1,0:T(8,128)(2,1)S(1)}) custom-call(s32[16]{0:T(128)S(1)} %dynamic-slice_bitcast_fusion.place.refs_0_, bf16[1024,256]{1,0:T(8,128)(2,1)S(1)} %copy-done, bf16[1024,256]{1,0:T(8,128)(2,1)S(1)} %collective-permute-done.refs_2_.g1, bf16[1024,256]{1,0:T(8,128)(2,1)S(1)} %collective-permute-done.1.refs_3_.g2, ...), custom_call_target="tpu_custom_call" | custom-call | flops 1610612736 | bytes 1048576 | tf_op jit(solution)/shard_map/pallas_call | solution.py:98
  122.6 1.4 collective-permute-start.18
  124.2 2.4 %shard_map.105 = (f32[256,1024]{1,0:T(8,128)S(1)}, f32[256,1024]{1,0:T(8,128)S(1)}) custom-call(s32[16]{0:T(128)S(1)} %dynamic-slice_bitcast_fusion.place.refs_0_, bf16[1024,256]{1,0:T(8,128)(2,1)S(1)} %copy-done, bf16[1024,256]{1,0:T(8,128)(2,1)S(1)} %collective-permute-done.refs_2_.g1, bf16[1024,256]{1,0:T(8,128)(2,1)S(1)} %collective-permute-done.1.refs_3_.g2, ...), custom_call_target="tpu_custom_call" | custom-call | flops 1610612736 | bytes 1048576 | tf_op jit(solution)/shard_map/pallas_call | solution.py:98
  126.6 9.6 %collective-permute-done.18 = bf16[256,1024]{1,0:T(8,128)(2,1)S(1)} collective-permute-done((bf16[256,1024]{1,0:T(8,128)(2,1)S(1)}, bf16[256,1024]{1,0:T(8,128)(2,1)S(1)}, u32[]{:S(2)}, u32[]{:S(2)}) %collective-permute-start.18) | collective-permute-done | bytes 524320 | tf_op jit(solution)/shard_map/ppermute | solution.py:63
  136.4 2.9 %collective-permute-start.19 = (bf16[256,1024]{1,0:T(8,128)(2,1)S(1)}, bf16[256,1024]{1,0:T(8,128)(2,1)S(1)}, u32[]{:S(2)}, u32[]{:S(2)}) collective-permute-start(bf16[256,1024]{1,0:T(8,128)(2,1)S(1)} %add_convert_fusion), channel_id=1, source_target_pairs={{0,2},{1,3},{2,0},{3,1},{4,6},{5,7},{6,4},{7,5},{8,10},{9,11},{10,... | collective-permute-start | bytes 1572872 | tf_op jit(solution)/shard_map/ppermute | solution.py:63
  139.3 0.8 shard_map.110
  140.5 2.7 %collective-permute-start.32 = (bf16[768,256]{1,0:T(8,128)(2,1)S(1)}, bf16[768,256]{1,0:T(8,128)(2,1)S(1)}, u32[]{:S(2)}, u32[]{:S(2)}) collective-permute-start(bf16[768,256]{1,0:T(8,128)(2,1)S(1)} %get-tuple-element.52), channel_id=1, source_target_pairs={{0,128},{16,144},{32,160},{48,176},{64,192},{80,208},{96,224},{112... | collective-permute-start | bytes 1179656 | tf_op jit(solution)/shard_map/ppermute | solution.py:63
  143.2 0.9 collective-permute-start.33
  144.1 5.3 %collective-permute-done.31.r1 = bf16[768,256]{1,0:T(8,128)(2,1)S(1)} collective-permute-done((bf16[768,256]{1,0:T(8,128)(2,1)S(1)}, bf16[768,256]{1,0:T(8,128)(2,1)S(1)}, u32[]{:S(2)}, u32[]{:S(2)}) %collective-permute-start.31) | collective-permute-done | bytes 393248 | tf_op jit(solution)/shard_map/ppermute | solution.py:63
  149.3 10.0 %collective-permute-done.32.r2 = bf16[768,256]{1,0:T(8,128)(2,1)S(1)} collective-permute-done((bf16[768,256]{1,0:T(8,128)(2,1)S(1)}, bf16[768,256]{1,0:T(8,128)(2,1)S(1)}, u32[]{:S(2)}, u32[]{:S(2)}) %collective-permute-start.32) | collective-permute-done | bytes 393248 | tf_op jit(solution)/shard_map/ppermute | solution.py:63
  159.4 2.1 collective-permute-done.33.r3
  161.4 0.7 shard_map.111
  162.1 4.6 %collective-permute-start.36 = (f32[256,256]{1,0:T(8,128)S(1)}, f32[256,256]{1,0:T(8,128)S(1)}, u32[]{:S(2)}, u32[]{:S(2)}) collective-permute-start(f32[256,256]{1,0:T(8,128)S(1)} %get-tuple-element.56), channel_id=1, source_target_pairs={{0,32},{16,48},{32,0},{48,16},{64,96},{80,112},{96,64},{112,80},{1... | collective-permute-start | bytes 786440 | tf_op jit(solution)/shard_map/ppermute | solution.py:63
  167.1 4.4 %collective-permute-done.36 = f32[256,256]{1,0:T(8,128)S(1)} collective-permute-done((f32[256,256]{1,0:T(8,128)S(1)}, f32[256,256]{1,0:T(8,128)S(1)}, u32[]{:S(2)}, u32[]{:S(2)}) %collective-permute-start.36) | collective-permute-done | bytes 262176 | tf_op jit(solution)/shard_map/ppermute | solution.py:63
  171.5 1.9 collective-permute-start.37
  173.5 12.4 %collective-permute-start.20 = (bf16[64,1024]{1,0:T(8,128)(2,1)S(1)}, bf16[64,1024]{1,0:T(8,128)(2,1)S(1)}, u32[]{:S(2)}, u32[]{:S(2)}) collective-permute-start(bf16[64,1024]{1,0:T(8,128)(2,1)S(1)} %get-tuple-element.61), channel_id=1, source_target_pairs={{0,1},{1,0},{2,3},{3,2},{4,5},{5,4},{6,7},{7,6},{8,9},{9,8},{10,11... | collective-permute-start | bytes 393224 | tf_op jit(solution)/shard_map/ppermute | solution.py:63
  185.9 17.5 %collective-permute-start.38 = (f32[256,256]{1,0:T(8,128)S(1)}, f32[256,256]{1,0:T(8,128)S(1)}, u32[]{:S(2)}, u32[]{:S(2)}) collective-permute-start(f32[256,256]{1,0:T(8,128)S(1)} %collective-permute-done.37.a0), channel_id=1, source_target_pairs={{0,64},{16,80},{32,96},{48,112},{64,0},{80,16},{96,32},{112,48},{1... | collective-permute-start | bytes 786440 | tf_op jit(solution)/shard_map/ppermute | solution.py:63
  203.4 2.4 %collective-permute-start.40 = (f32[256,256]{1,0:T(8,128)S(1)}, f32[256,256]{1,0:T(8,128)S(1)}, u32[]{:S(2)}, u32[]{:S(2)}) collective-permute-start(f32[256,256]{1,0:T(8,128)S(1)} %collective-permute-done.37.a0), channel_id=1, source_target_pairs={{0,192},{16,208},{32,224},{48,240},{64,128},{80,144},{96,160},{112... | collective-permute-start | bytes 786440 | tf_op jit(solution)/shard_map/ppermute | solution.py:63
  205.8 4.5 %collective-permute-start.21 = (bf16[64,1024]{1,0:T(8,128)(2,1)S(1)}, bf16[64,1024]{1,0:T(8,128)(2,1)S(1)}, u32[]{:S(2)}, u32[]{:S(2)}) collective-permute-start(bf16[64,1024]{1,0:T(8,128)(2,1)S(1)} %get-tuple-element.60), channel_id=1, source_target_pairs={{0,4},{1,5},{2,6},{3,7},{4,0},{5,1},{6,2},{7,3},{8,12},{9,13},{10,... | collective-permute-start | bytes 393224 | tf_op jit(solution)/shard_map/ppermute | solution.py:63
  210.3 4.8 %collective-permute-done.21.p2 = bf16[64,1024]{1,0:T(8,128)(2,1)S(1)} collective-permute-done((bf16[64,1024]{1,0:T(8,128)(2,1)S(1)}, bf16[64,1024]{1,0:T(8,128)(2,1)S(1)}, u32[]{:S(2)}, u32[]{:S(2)}) %collective-permute-start.21) | collective-permute-done | bytes 131104 | tf_op jit(solution)/shard_map/ppermute | solution.py:63
  215.1 1.9 collective-permute-start.35
  217.0 4.2 %collective-permute-start.41 = (f32[256,256]{1,0:T(8,128)S(1)}, f32[256,256]{1,0:T(8,128)S(1)}, u32[]{:S(2)}, u32[]{:S(2)}) collective-permute-start(f32[256,256]{1,0:T(8,128)S(1)} %collective-permute-done.37.a0), channel_id=1, source_target_pairs={{0,16},{16,0},{32,48},{48,32},{64,80},{80,64},{96,112},{112,96},{1... | collective-permute-start | bytes 786440 | tf_op jit(solution)/shard_map/ppermute | solution.py:63
  221.9 2.2 shard_map.107
  224.1 0.6 collective-permute-done.35
  224.7 2.1 shard_map.112
  226.8 0.7 copy.15
  (67 shorter events, 3.3 us)
Async XLA Ops:
  0.6 58.2 %copy-start = (bf16[1024,256]{1,0:T(8,128)(2,1)S(1)}, bf16[1024,256]{1,0:T(8,128)(2,1)}, u32[]{:S(2)}) copy-start(bf16[1024,256]{1,0:T(8,128)(2,1)} %g0.1) | copy-start | bytes 1572868
  1.4 1.0 copy-start.2
  2.4 0.7 copy-start.6
  4.1 4.8 %collective-permute-start.23 = (bf16[64,1024]{1,0:T(8,128)(2,1)S(1)}, bf16[64,1024]{1,0:T(8,128)(2,1)S(1)}, u32[]{:S(2)}, u32[]{:S(2)}) collective-permute-start(bf16[64,1024]{1,0:T(8,128)(2,1)S(1)} %get-tuple-element.43), channel_id=1, source_target_pairs={{0,1},{1,0},{2,3},{3,2},{4,5},{5,4},{6,7},{7,6},{8,9},{9,8},{10,11... | collective-permute-start | bytes 393224 | tf_op jit(solution)/shard_map/ppermute | solution.py:63
  5.8 4.1 %collective-permute-start.24 = (bf16[64,1024]{1,0:T(8,128)(2,1)S(1)}, bf16[64,1024]{1,0:T(8,128)(2,1)S(1)}, u32[]{:S(2)}, u32[]{:S(2)}) collective-permute-start(bf16[64,1024]{1,0:T(8,128)(2,1)S(1)} %get-tuple-element.44), channel_id=1, source_target_pairs={{0,4},{1,5},{2,6},{3,7},{4,0},{5,1},{6,2},{7,3},{8,12},{9,13},{10,... | collective-permute-start | bytes 393224 | tf_op jit(solution)/shard_map/ppermute | solution.py:63
  6.8 5.0 %collective-permute-start.25 = (bf16[64,1024]{1,0:T(8,128)(2,1)S(1)}, bf16[64,1024]{1,0:T(8,128)(2,1)S(1)}, u32[]{:S(2)}, u32[]{:S(2)}) collective-permute-start(bf16[64,1024]{1,0:T(8,128)(2,1)S(1)} %get-tuple-element.45), channel_id=1, source_target_pairs={{0,5},{1,4},{2,7},{3,6},{4,1},{5,0},{6,3},{7,2},{8,13},{9,12},{10,... | collective-permute-start | bytes 393224 | tf_op jit(solution)/shard_map/ppermute | solution.py:63
  7.1 26.5 %collective-permute-start.3 = (bf16[2,1024,128]{2,1,0:T(8,128)(2,1)}, bf16[2,1024,128]{2,1,0:T(8,128)(2,1)S(1)}, u32[]{:S(2)}, u32[]{:S(2)}) collective-permute-start(bf16[2,1024,128]{2,1,0:T(8,128)(2,1)} %param.14), channel_id=1, source_target_pairs={{0,1},{1,0},{2,3},{3,2},{4,5},{5,4},{6,7},{7,6},{8,9},{9,8},{10,11... | collective-permute-start | bytes 1572872 | tf_op jit(solution)/shard_map/ppermute | solution.py:63
  8.4 36.4 %collective-permute-start = (bf16[1024,256]{1,0:T(8,128)(2,1)}, bf16[1024,256]{1,0:T(8,128)(2,1)S(1)}, u32[]{:S(2)}, u32[]{:S(2)}) collective-permute-start(bf16[1024,256]{1,0:T(8,128)(2,1)} %g0.1), channel_id=1, source_target_pairs={{0,1},{1,0},{2,3},{3,2},{4,5},{5,4},{6,7},{7,6},{8,9},{9,8},{10,11... | collective-permute-start | bytes 1572872 | tf_op jit(solution)/shard_map/ppermute | solution.py:63
  11.8 34.1 %collective-permute-start.26 = (bf16[256,1024]{1,0:T(8,128)(2,1)S(1)}, bf16[256,1024]{1,0:T(8,128)(2,1)S(1)}, u32[]{:S(2)}, u32[]{:S(2)}) collective-permute-start(bf16[256,1024]{1,0:T(8,128)(2,1)S(1)} %constant_dynamic-update-slice_fusion.n0), channel_id=1, source_target_pairs={{0,2},{1,3},{2,0},{3,1},{4,6},{5,7},{6,4},{7,5},{8,10},{9,11},{10,... | collective-permute-start | bytes 1572872 | tf_op jit(solution)/shard_map/ppermute | solution.py:63
  14.9 31.6 %collective-permute-start.1 = (bf16[1024,256]{1,0:T(8,128)(2,1)}, bf16[1024,256]{1,0:T(8,128)(2,1)S(1)}, u32[]{:S(2)}, u32[]{:S(2)}) collective-permute-start(bf16[1024,256]{1,0:T(8,128)(2,1)} %g0.1), channel_id=1, source_target_pairs={{0,4},{1,5},{2,6},{3,7},{4,0},{5,1},{6,2},{7,3},{8,12},{9,13},{10,... | collective-permute-start | bytes 1572872 | tf_op jit(solution)/shard_map/ppermute | solution.py:63
  15.3 31.2 %collective-permute-start.27 = (bf16[256,1024]{1,0:T(8,128)(2,1)S(1)}, bf16[256,1024]{1,0:T(8,128)(2,1)S(1)}, u32[]{:S(2)}, u32[]{:S(2)}) collective-permute-start(bf16[256,1024]{1,0:T(8,128)(2,1)S(1)} %constant_dynamic-update-slice_fusion.n0), channel_id=1, source_target_pairs={{0,12},{1,13},{2,14},{3,15},{4,8},{5,9},{6,10},{7,11},{8,4},{9,5},... | collective-permute-start | bytes 1572872 | tf_op jit(solution)/shard_map/ppermute | solution.py:63
  34.8 29.9 %copy-start.1 = (bf16[4096,256]{1,0:T(8,128)(2,1)S(1)}, bf16[4096,256]{1,0:T(8,128)(2,1)}, u32[]{:S(2)}) copy-start(bf16[4096,256]{1,0:T(8,128)(2,1)} %wq.1) | copy-start | bytes 6291460
  34.8 29.9 %copy-start.4 = (bf16[2,256,1024]{2,1,0:T(8,128)(2,1)S(1)}, bf16[2,256,1024]{2,1,0:T(8,128)(2,1)}, u32[]{:S(2)}) copy-start(bf16[2,256,1024]{2,1,0:T(8,128)(2,1)} %wkv.1) | copy-start | bytes 3145732
  34.8 11.7 %collective-permute-start.4 = (bf16[2,1024,128]{2,1,0:T(8,128)(2,1)S(1)}, bf16[2,1024,128]{2,1,0:T(8,128)(2,1)S(1)}, u32[]{:S(2)}, u32[]{:S(2)}) collective-permute-start(bf16[2,1024,128]{2,1,0:T(8,128)(2,1)S(1)} %add_convert_fusion.1.refs_5_.kv0), channel_id=1, source_target_pairs={{0,4},{1,5},{2,6},{3,7},{4,0},{5,1},{6,2},{7,3},{8,12},{9,13},{10,... | collective-permute-start | bytes 1572872 | tf_op jit(solution)/shard_map/ppermute | solution.py:63
  44.8 14.0 %collective-permute-start.2 = (bf16[1024,256]{1,0:T(8,128)(2,1)S(1)}, bf16[1024,256]{1,0:T(8,128)(2,1)S(1)}, u32[]{:S(2)}, u32[]{:S(2)}) collective-permute-start(bf16[1024,256]{1,0:T(8,128)(2,1)S(1)} %collective-permute-done.refs_2_.g1), channel_id=1, source_target_pairs={{0,4},{1,5},{2,6},{3,7},{4,0},{5,1},{6,2},{7,3},{8,12},{9,13},{10,... | collective-permute-start | bytes 1572872 | tf_op jit(solution)/shard_map/ppermute | solution.py:63
  45.9 13.0 %collective-permute-start.28 = (bf16[256,1024]{1,0:T(8,128)(2,1)S(1)}, bf16[256,1024]{1,0:T(8,128)(2,1)S(1)}, u32[]{:S(2)}, u32[]{:S(2)}) collective-permute-start(bf16[256,1024]{1,0:T(8,128)(2,1)S(1)} %collective-permute-done.26.n1), channel_id=1, source_target_pairs={{0,12},{1,13},{2,14},{3,15},{4,8},{5,9},{6,10},{7,11},{8,4},{9,5},... | collective-permute-start | bytes 1572872 | tf_op jit(solution)/shard_map/ppermute | solution.py:63
  63.0 76.3 %collective-permute-start.29 = (f32[2,1024,256]{2,1,0:T(8,128)S(1)}, f32[2,1024,256]{2,1,0:T(8,128)S(1)}, u32[]{:S(2)}, u32[]{:S(2)}) collective-permute-start(f32[2,1024,256]{2,1,0:T(8,128)S(1)} %get-tuple-element.47), channel_id=1, source_target_pairs={{0,16},{16,0},{32,48},{48,32},{64,80},{80,64},{96,112},{112,96},{1... | collective-permute-start | bytes 6291464 | tf_op jit(solution)/shard_map/ppermute | solution.py:63
  66.1 5.2 %collective-permute-start.11 = (bf16[256,128]{1,0:T(8,128)(2,1)S(1)}, bf16[256,128]{1,0:T(8,128)(2,1)S(1)}, u32[]{:S(2)}, u32[]{:S(2)}) collective-permute-start(bf16[256,128]{1,0:T(8,128)(2,1)S(1)} %get-tuple-element.35), channel_id=1, source_target_pairs={{0,2},{1,3},{2,0},{3,1},{4,6},{5,7},{6,4},{7,5},{8,10},{9,11},{10,... | collective-permute-start | bytes 196616 | tf_op jit(solution)/shard_map/ppermute | solution.py:63
  68.9 3.1 %collective-permute-start.12 = (bf16[256,128]{1,0:T(8,128)(2,1)S(1)}, bf16[256,128]{1,0:T(8,128)(2,1)S(1)}, u32[]{:S(2)}, u32[]{:S(2)}) collective-permute-start(bf16[256,128]{1,0:T(8,128)(2,1)S(1)} %get-tuple-element.36), channel_id=1, source_target_pairs={{0,12},{1,13},{2,14},{3,15},{4,8},{5,9},{6,10},{7,11},{8,4},{9,5},... | collective-permute-start | bytes 196616 | tf_op jit(solution)/shard_map/ppermute | solution.py:63
  69.1 4.9 %collective-permute-start.13 = (bf16[256,128]{1,0:T(8,128)(2,1)S(1)}, bf16[256,128]{1,0:T(8,128)(2,1)S(1)}, u32[]{:S(2)}, u32[]{:S(2)}) collective-permute-start(bf16[256,128]{1,0:T(8,128)(2,1)S(1)} %get-tuple-element.37), channel_id=1, source_target_pairs={{0,14},{1,15},{2,12},{3,13},{4,10},{5,11},{6,8},{7,9},{8,6},{9,7},... | collective-permute-start | bytes 196616 | tf_op jit(solution)/shard_map/ppermute | solution.py:63
  74.0 14.7 %collective-permute-start.14 = (bf16[4,256,128]{2,1,0:T(8,128)(2,1)S(1)}, bf16[4,256,128]{2,1,0:T(8,128)(2,1)S(1)}, u32[]{:S(2)}, u32[]{:S(2)}) collective-permute-start(bf16[4,256,128]{2,1,0:T(8,128)(2,1)S(1)} %pad_maximum_fusion.1.k0), channel_id=1, source_target_pairs={{0,64},{16,80},{32,96},{48,112},{64,0},{80,16},{96,32},{112,48},{1... | collective-permute-start | bytes 786440 | tf_op jit(solution)/shard_map/ppermute | solution.py:63
  75.3 5.3 %collective-permute-start.5 = (bf16[256,256]{1,0:T(8,128)(2,1)S(1)}, bf16[256,256]{1,0:T(8,128)(2,1)S(1)}, u32[]{:S(2)}, u32[]{:S(2)}) collective-permute-start(bf16[256,256]{1,0:T(8,128)(2,1)S(1)} %get-tuple-element.31), channel_id=1, source_target_pairs={{0,1},{1,0},{2,3},{3,2},{4,5},{5,4},{6,7},{7,6},{8,9},{9,8},{10,11... | collective-permute-start | bytes 393224 | tf_op jit(solution)/shard_map/ppermute | solution.py:63
  77.5 6.4 %collective-permute-start.6 = (bf16[256,256]{1,0:T(8,128)(2,1)S(1)}, bf16[256,256]{1,0:T(8,128)(2,1)S(1)}, u32[]{:S(2)}, u32[]{:S(2)}) collective-permute-start(bf16[256,256]{1,0:T(8,128)(2,1)S(1)} %get-tuple-element.32), channel_id=1, source_target_pairs={{0,4},{1,5},{2,6},{3,7},{4,0},{5,1},{6,2},{7,3},{8,12},{9,13},{10,... | collective-permute-start | bytes 393224 | tf_op jit(solution)/shard_map/ppermute | solution.py:63
  80.6 5.8 %collective-permute-start.7 = (bf16[256,256]{1,0:T(8,128)(2,1)S(1)}, bf16[256,256]{1,0:T(8,128)(2,1)S(1)}, u32[]{:S(2)}, u32[]{:S(2)}) collective-permute-start(bf16[256,256]{1,0:T(8,128)(2,1)S(1)} %get-tuple-element.33), channel_id=1, source_target_pairs={{0,5},{1,4},{2,7},{3,6},{4,1},{5,0},{6,3},{7,2},{8,13},{9,12},{10,... | collective-permute-start | bytes 393224 | tf_op jit(solution)/shard_map/ppermute | solution.py:63
  80.6 9.8 %collective-permute-start.15 = (bf16[4,256,128]{2,1,0:T(8,128)(2,1)S(1)}, bf16[4,256,128]{2,1,0:T(8,128)(2,1)S(1)}, u32[]{:S(2)}, u32[]{:S(2)}) collective-permute-start(bf16[4,256,128]{2,1,0:T(8,128)(2,1)S(1)} %pad_maximum_fusion.1.k0), channel_id=1, source_target_pairs={{0,128},{16,144},{32,160},{48,176},{64,192},{80,208},{96,224},{112... | collective-permute-start | bytes 786440 | tf_op jit(solution)/shard_map/ppermute | solution.py:63
  86.5 29.3 %collective-permute-start.10 = (bf16[4,256,256]{2,1,0:T(8,128)(2,1)S(1)}, bf16[4,256,256]{2,1,0:T(8,128)(2,1)S(1)}, u32[]{:S(2)}, u32[]{:S(2)}) collective-permute-start(bf16[4,256,256]{2,1,0:T(8,128)(2,1)S(1)} %pad_maximum_fusion.q0), channel_id=1, source_target_pairs={{0,192},{16,208},{32,224},{48,240},{64,128},{80,144},{96,160},{112... | collective-permute-start | bytes 1572872 | tf_op jit(solution)/shard_map/ppermute | solution.py:63
  88.4 27.4 %collective-permute-start.8 = (bf16[4,256,256]{2,1,0:T(8,128)(2,1)S(1)}, bf16[4,256,256]{2,1,0:T(8,128)(2,1)S(1)}, u32[]{:S(2)}, u32[]{:S(2)}) collective-permute-start(bf16[4,256,256]{2,1,0:T(8,128)(2,1)S(1)} %pad_maximum_fusion.q0), channel_id=1, source_target_pairs={{0,64},{16,80},{32,96},{48,112},{64,0},{80,16},{96,32},{112,48},{1... | collective-permute-start | bytes 1572872 | tf_op jit(solution)/shard_map/ppermute | solution.py:63
  88.7 27.1 %collective-permute-start.9 = (bf16[4,256,256]{2,1,0:T(8,128)(2,1)S(1)}, bf16[4,256,256]{2,1,0:T(8,128)(2,1)S(1)}, u32[]{:S(2)}, u32[]{:S(2)}) collective-permute-start(bf16[4,256,256]{2,1,0:T(8,128)(2,1)S(1)} %pad_maximum_fusion.q0), channel_id=1, source_target_pairs={{0,128},{16,144},{32,160},{48,176},{64,192},{80,208},{96,224},{112... | collective-permute-start | bytes 1572872 | tf_op jit(solution)/shard_map/ppermute | solution.py:63
  90.4 25.4 %collective-permute-start.16 = (bf16[4,256,128]{2,1,0:T(8,128)(2,1)S(1)}, bf16[4,256,128]{2,1,0:T(8,128)(2,1)S(1)}, u32[]{:S(2)}, u32[]{:S(2)}) collective-permute-start(bf16[4,256,128]{2,1,0:T(8,128)(2,1)S(1)} %pad_maximum_fusion.1.k0), channel_id=1, source_target_pairs={{0,192},{16,208},{32,224},{48,240},{64,128},{80,144},{96,160},{112... | collective-permute-start | bytes 786440 | tf_op jit(solution)/shard_map/ppermute | solution.py:63
  116.7 22.6 %collective-permute-start.30 = (f32[1024,256]{1,0:T(8,128)S(1)}, f32[1024,256]{1,0:T(8,128)S(1)}, u32[]{:S(2)}, u32[]{:S(2)}) collective-permute-start(f32[1024,256]{1,0:T(8,128)S(1)} %get-tuple-element.49), channel_id=1, source_target_pairs={{0,16},{16,0},{32,48},{48,32},{64,80},{80,64},{96,112},{112,96},{1... | collective-permute-start | bytes 3145736 | tf_op jit(solution)/shard_map/ppermute | solution.py:63
  122.6 13.6 %collective-permute-start.18 = (bf16[256,1024]{1,0:T(8,128)(2,1)S(1)}, bf16[256,1024]{1,0:T(8,128)(2,1)S(1)}, u32[]{:S(2)}, u32[]{:S(2)}) collective-permute-start(bf16[256,1024]{1,0:T(8,128)(2,1)S(1)} %get-tuple-element.41), channel_id=1, source_target_pairs={{0,12},{1,13},{2,14},{3,15},{4,8},{5,9},{6,10},{7,11},{8,4},{9,5},... | collective-permute-start | bytes 1572872 | tf_op jit(solution)/shard_map/ppermute | solution.py:63
  124.0 42.8 %collective-permute-start.17 = (bf16[256,1024]{1,0:T(8,128)(2,1)S(1)}, bf16[256,1024]{1,0:T(8,128)(2,1)S(1)}, u32[]{:S(2)}, u32[]{:S(2)}) collective-permute-start(bf16[256,1024]{1,0:T(8,128)(2,1)S(1)} %get-tuple-element.39), channel_id=1, source_target_pairs={{0,12},{1,13},{2,14},{3,15},{4,8},{5,9},{6,10},{7,11},{8,4},{9,5},... | collective-permute-start | bytes 1572872 | tf_op jit(solution)/shard_map/ppermute | solution.py:63
  136.4 30.3 %collective-permute-start.19 = (bf16[256,1024]{1,0:T(8,128)(2,1)S(1)}, bf16[256,1024]{1,0:T(8,128)(2,1)S(1)}, u32[]{:S(2)}, u32[]{:S(2)}) collective-permute-start(bf16[256,1024]{1,0:T(8,128)(2,1)S(1)} %add_convert_fusion), channel_id=1, source_target_pairs={{0,2},{1,3},{2,0},{3,1},{4,6},{5,7},{6,4},{7,5},{8,10},{9,11},{10,... | collective-permute-start | bytes 1572872 | tf_op jit(solution)/shard_map/ppermute | solution.py:63
  140.1 9.2 %collective-permute-start.31 = (bf16[768,256]{1,0:T(8,128)(2,1)S(1)}, bf16[768,256]{1,0:T(8,128)(2,1)S(1)}, u32[]{:S(2)}, u32[]{:S(2)}) collective-permute-start(bf16[768,256]{1,0:T(8,128)(2,1)S(1)} %get-tuple-element.51), channel_id=1, source_target_pairs={{0,64},{16,80},{32,96},{48,112},{64,0},{80,16},{96,32},{112,48},{1... | collective-permute-start | bytes 1179656 | tf_op jit(solution)/shard_map/ppermute | solution.py:63
  140.5 18.9 %collective-permute-start.32 = (bf16[768,256]{1,0:T(8,128)(2,1)S(1)}, bf16[768,256]{1,0:T(8,128)(2,1)S(1)}, u32[]{:S(2)}, u32[]{:S(2)}) collective-permute-start(bf16[768,256]{1,0:T(8,128)(2,1)S(1)} %get-tuple-element.52), channel_id=1, source_target_pairs={{0,128},{16,144},{32,160},{48,176},{64,192},{80,208},{96,224},{112... | collective-permute-start | bytes 1179656 | tf_op jit(solution)/shard_map/ppermute | solution.py:63
  143.2 18.2 %collective-permute-start.33 = (bf16[768,256]{1,0:T(8,128)(2,1)S(1)}, bf16[768,256]{1,0:T(8,128)(2,1)S(1)}, u32[]{:S(2)}, u32[]{:S(2)}) collective-permute-start(bf16[768,256]{1,0:T(8,128)(2,1)S(1)} %get-tuple-element.53), channel_id=1, source_target_pairs={{0,192},{16,208},{32,224},{48,240},{64,128},{80,144},{96,160},{112... | collective-permute-start | bytes 1179656 | tf_op jit(solution)/shard_map/ppermute | solution.py:63
  162.1 9.3 %collective-permute-start.36 = (f32[256,256]{1,0:T(8,128)S(1)}, f32[256,256]{1,0:T(8,128)S(1)}, u32[]{:S(2)}, u32[]{:S(2)}) collective-permute-start(f32[256,256]{1,0:T(8,128)S(1)} %get-tuple-element.56), channel_id=1, source_target_pairs={{0,32},{16,48},{32,0},{48,16},{64,96},{80,112},{96,64},{112,80},{1... | collective-permute-start | bytes 786440 | tf_op jit(solution)/shard_map/ppermute | solution.py:63
  167.1 54.9 %copy-start.3 = (bf16[64,4096]{1,0:T(8,128)(2,1)S(1)}, bf16[64,4096]{1,0:T(8,128)(2,1)}, u32[]{:S(2)}) copy-start(bf16[64,4096]{1,0:T(8,128)(2,1)} %x_ref.3) | copy-start | bytes 1572868
  167.1 54.9 %copy-start.5 = (bf16[64,4096]{1,0:T(8,128)(2,1)S(1)}, bf16[64,4096]{1,0:T(8,128)(2,1)}, u32[]{:S(2)}) copy-start(bf16[64,4096]{1,0:T(8,128)(2,1)} %og_ref.1) | copy-start | bytes 1572868
  167.1 54.9 %copy-start.7 = (f32[4096]{0:T(1024)S(1)}, f32[4096]{0:T(1024)}, u32[]{:S(2)}) copy-start(f32[4096]{0:T(1024)} %param.10) | copy-start | bytes 49156
  171.5 14.4 %collective-permute-start.37 = (f32[256,256]{1,0:T(8,128)S(1)}, f32[256,256]{1,0:T(8,128)S(1)}, u32[]{:S(2)}, u32[]{:S(2)}) collective-permute-start(f32[256,256]{1,0:T(8,128)S(1)} %add.32), channel_id=1, source_target_pairs={{0,0},{1,1},{2,64},{3,65},{4,4},{5,5},{6,68},{7,69},{8,132},{9,133... | collective-permute-start | bytes 786440 | tf_op jit(solution)/shard_map/ppermute | solution.py:324
  173.5 32.3 %collective-permute-start.20 = (bf16[64,1024]{1,0:T(8,128)(2,1)S(1)}, bf16[64,1024]{1,0:T(8,128)(2,1)S(1)}, u32[]{:S(2)}, u32[]{:S(2)}) collective-permute-start(bf16[64,1024]{1,0:T(8,128)(2,1)S(1)} %get-tuple-element.61), channel_id=1, source_target_pairs={{0,1},{1,0},{2,3},{3,2},{4,5},{5,4},{6,7},{7,6},{8,9},{9,8},{10,11... | collective-permute-start | bytes 393224 | tf_op jit(solution)/shard_map/ppermute | solution.py:63
  185.9 24.4 %collective-permute-start.34 = (bf16[256,256]{1,0:T(8,128)(2,1)S(1)}, bf16[256,256]{1,0:T(8,128)(2,1)S(1)}, u32[]{:S(2)}, u32[]{:S(2)}) collective-permute-start(bf16[256,256]{1,0:T(8,128)(2,1)S(1)} %get-tuple-element.55), channel_id=1, source_target_pairs={{0,32},{16,48},{32,0},{48,16},{64,96},{80,112},{96,64},{112,80},{1... | collective-permute-start | bytes 393224 | tf_op jit(solution)/shard_map/ppermute | solution.py:63
  185.9 35.4 %collective-permute-start.38 = (f32[256,256]{1,0:T(8,128)S(1)}, f32[256,256]{1,0:T(8,128)S(1)}, u32[]{:S(2)}, u32[]{:S(2)}) collective-permute-start(f32[256,256]{1,0:T(8,128)S(1)} %collective-permute-done.37.a0), channel_id=1, source_target_pairs={{0,64},{16,80},{32,96},{48,112},{64,0},{80,16},{96,32},{112,48},{1... | collective-permute-start | bytes 786440 | tf_op jit(solution)/shard_map/ppermute | solution.py:63
  203.4 18.0 %collective-permute-start.39 = (f32[256,256]{1,0:T(8,128)S(1)}, f32[256,256]{1,0:T(8,128)S(1)}, u32[]{:S(2)}, u32[]{:S(2)}) collective-permute-start(f32[256,256]{1,0:T(8,128)S(1)} %collective-permute-done.37.a0), channel_id=1, source_target_pairs={{0,128},{16,144},{32,160},{48,176},{64,192},{80,208},{96,224},{112... | collective-permute-start | bytes 786440 | tf_op jit(solution)/shard_map/ppermute | solution.py:63
  203.4 18.4 %collective-permute-start.40 = (f32[256,256]{1,0:T(8,128)S(1)}, f32[256,256]{1,0:T(8,128)S(1)}, u32[]{:S(2)}, u32[]{:S(2)}) collective-permute-start(f32[256,256]{1,0:T(8,128)S(1)} %collective-permute-done.37.a0), channel_id=1, source_target_pairs={{0,192},{16,208},{32,224},{48,240},{64,128},{80,144},{96,160},{112... | collective-permute-start | bytes 786440 | tf_op jit(solution)/shard_map/ppermute | solution.py:63
  205.8 9.3 %collective-permute-start.21 = (bf16[64,1024]{1,0:T(8,128)(2,1)S(1)}, bf16[64,1024]{1,0:T(8,128)(2,1)S(1)}, u32[]{:S(2)}, u32[]{:S(2)}) collective-permute-start(bf16[64,1024]{1,0:T(8,128)(2,1)S(1)} %get-tuple-element.60), channel_id=1, source_target_pairs={{0,4},{1,5},{2,6},{3,7},{4,0},{5,1},{6,2},{7,3},{8,12},{9,13},{10,... | collective-permute-start | bytes 393224 | tf_op jit(solution)/shard_map/ppermute | solution.py:63
  210.3 6.7 %collective-permute-start.22 = (bf16[64,1024]{1,0:T(8,128)(2,1)S(1)}, bf16[64,1024]{1,0:T(8,128)(2,1)S(1)}, u32[]{:S(2)}, u32[]{:S(2)}) collective-permute-start(bf16[64,1024]{1,0:T(8,128)(2,1)S(1)} %get-tuple-element.59), channel_id=1, source_target_pairs={{0,5},{1,4},{2,7},{3,6},{4,1},{5,0},{6,3},{7,2},{8,13},{9,12},{10,... | collective-permute-start | bytes 393224 | tf_op jit(solution)/shard_map/ppermute | solution.py:63
  215.1 9.6 %collective-permute-start.35 = (f32[256,256]{1,0:T(8,128)S(1)}, f32[256,256]{1,0:T(8,128)S(1)}, u32[]{:S(2)}, u32[]{:S(2)}) collective-permute-start(f32[256,256]{1,0:T(8,128)S(1)} %convert_add_fusion.1), channel_id=1, source_target_pairs={{0,0},{1,16},{2,2},{3,18},{4,64},{5,80},{6,66},{7,82},{8,76},{9,92... | collective-permute-start | bytes 786440 | tf_op jit(solution)/shard_map/ppermute | solution.py:322
  217.0 7.7 %collective-permute-start.41 = (f32[256,256]{1,0:T(8,128)S(1)}, f32[256,256]{1,0:T(8,128)S(1)}, u32[]{:S(2)}, u32[]{:S(2)}) collective-permute-start(f32[256,256]{1,0:T(8,128)S(1)} %collective-permute-done.37.a0), channel_id=1, source_target_pairs={{0,16},{16,0},{32,48},{48,32},{64,80},{80,64},{96,112},{112,96},{1... | collective-permute-start | bytes 786440 | tf_op jit(solution)/shard_map/ppermute | solution.py:63
  221.3 3.4 %collective-permute-start.42 = (f32[256,256]{1,0:T(8,128)S(1)}, f32[256,256]{1,0:T(8,128)S(1)}, u32[]{:S(2)}, u32[]{:S(2)}) collective-permute-start(f32[256,256]{1,0:T(8,128)S(1)} %collective-permute-done.38.a1), channel_id=1, source_target_pairs={{0,16},{16,0},{32,48},{48,32},{64,80},{80,64},{96,112},{112,96},{1... | collective-permute-start | bytes 786440 | tf_op jit(solution)/shard_map/ppermute | solution.py:63
  221.4 3.3 %collective-permute-start.43 = (f32[256,256]{1,0:T(8,128)S(1)}, f32[256,256]{1,0:T(8,128)S(1)}, u32[]{:S(2)}, u32[]{:S(2)}) collective-permute-start(f32[256,256]{1,0:T(8,128)S(1)} %collective-permute-done.39.a2), channel_id=1, source_target_pairs={{0,16},{16,0},{32,48},{48,32},{64,80},{80,64},{96,112},{112,96},{1... | collective-permute-start | bytes 786440 | tf_op jit(solution)/shard_map/ppermute | solution.py:63
  221.8 2.9 %collective-permute-start.44 = (f32[256,256]{1,0:T(8,128)S(1)}, f32[256,256]{1,0:T(8,128)S(1)}, u32[]{:S(2)}, u32[]{:S(2)}) collective-permute-start(f32[256,256]{1,0:T(8,128)S(1)} %collective-permute-done.40.a3), channel_id=1, source_target_pairs={{0,16},{16,0},{32,48},{48,32},{64,80},{80,64},{96,112},{112,96},{1... | collective-permute-start | bytes 786440 | tf_op jit(solution)/shard_map/ppermute | solution.py:63

commit v2 on v1

v2 whole, which is shorter than its diff:
```python
import numpy as np
import jax
import jax.numpy as jnp
from jax import lax
from jax.experimental import pallas as pl
from jax.experimental.pallas import tpu as pltpu
from jax.sharding import PartitionSpec as P

EPSILON = 1e-05
BF = jnp.bfloat16
F32 = jnp.float32

INNER = (0, 1, 4, 5)
OUTER = (0, 2, 12, 14)
HEAD_STEP = (0, 1, 6, 7)


def alpha_of(v):
    return (v ^ (v >> 1)) & 1


def ring_place(alpha, beta):
    return alpha ^ (3 * beta)


def place_table():
    rows = []
    for device in range(256):
        dp, t = divmod(device, 16)
        x, c = dp >> 2, dp & 1
        h = (dp >> 1) & 1
        y, z = divmod(t, 4)
        z0, z1 = z & 1, z >> 1
        base = 4 * alpha_of(y) + z0
        outer = 2 * (y >> 1) + z1
        rows.append(
            (
                base,
                t,
                outer,
                x,
                c,
                c ^ z0,
                alpha_of(x) ^ alpha_of(y),
                x >> 1,
                h,
                base ^ OUTER[2 * (x & 1)],
                2 * y + z1,
                x & 1,
                (2 * alpha_of(y)) ^ HEAD_STEP[x],
                0,
                0,
                0,
            )
        )
    return np.array(rows, np.int32)


TABLE = place_table()


def exchange(v, axis, flip):
    return lax.ppermute(v, axis, [(i, i ^ flip) for i in range(16)])


def query_turn(over):
    pairs = []
    for device in range(256):
        dp, t = divmod(device, 16)
        x, h, c = dp >> 2, (dp >> 1) & 1, dp & 1
        y, z = divmod(t, 4)
        x_to = ring_place(alpha_of(y), x >> 1)
        y_to = ring_place(alpha_of(x), y >> 1)
        z_to, c_to = (z & 2) | c, z & 1
        pairs.append((device, (x_to * 4 + (h ^ over) * 2 + c_to) * 16 + y_to * 4 + z_to))
    return pairs


def keyval_turn(over):
    pairs = []
    for device in range(256):
        dp, t = divmod(device, 16)
        x = dp >> 2
        y, z = divmod(t, 4)
        x_to = 2 * (y >> 1) + (z >> 1)
        y_to = ring_place(alpha_of(y), x >> 1)
        z_to = 2 * (x & 1) + (z & 1)
        pairs.append((device, (x_to * 4 + ((dp & 3) ^ (2 * over))) * 16 + y_to * 4 + z_to))
    return pairs


SMEM = pl.BlockSpec(memory_space=pltpu.SMEM)
VMEM = pl.BlockSpec(memory_space=pltpu.VMEM)
ANY = pl.BlockSpec(memory_space=pl.ANY)
HBM = pl.BlockSpec(memory_space=pltpu.HBM)


def call(kernel, outs, place, args, scratch=(), spaces=None, limit=40):
    return pl.pallas_call(
        kernel,
        out_shape=[jax.ShapeDtypeStruct(s, d) for s, d in outs],
        in_specs=[SMEM] + list(spaces or [VMEM] * len(args)),
        out_specs=[VMEM] * len(outs),
        scratch_shapes=list(scratch),
        compiler_params=pltpu.CompilerParams(vmem_limit_bytes=limit << 20),
        cost_estimate=pl.CostEstimate(flops=0, bytes_accessed=1, transcendentals=0),
    )(place, *args)


def block(index, size):
    return pl.ds(pl.multiple_of(index * size, size), size)


def prepare_kernel(place, x_any, gain_any, wq, wkv, *refs):
    inner, k0, k1, k2, x_ref, gain_ref, scr, sem = refs[:4], *refs[4:]
    base, c = place[0], place[4]
    first = [
        pltpu.make_async_copy(x_any, x_ref, sem.at[0]),
        pltpu.make_async_copy(gain_any, gain_ref, sem.at[1]),
    ]
    copies = []
    for k in range(4):
        for m in range(2):
            rows = block(2 * (place[9] ^ (INNER[k] ^ OUTER[m])) + c, 128)
            to = inner[k].at[256 + 128 * m : 384 + 128 * m, :]
            copies.append(pltpu.make_async_copy(wq.at[rows, :], to, sem.at[2 + 2 * k + m]))
    for j, out in enumerate((k0, k1.at[0], k2, k1.at[1])):
        for a in range(2):
            head = block(place[10] ^ (HEAD_STEP[j] ^ (2 * a)), 128)
            to = out.at[:, 128 * a : 128 * (a + 1)]
            copies.append(pltpu.make_async_copy(wkv.at[place[11], block(c, 128), head], to, sem.at[10 + 2 * j + a]))
    for copy in first + copies:
        copy.start()
    for copy in first:
        copy.wait()
    wide = x_ref[...].astype(F32)
    inverse = lax.rsqrt(jnp.mean(wide * wide, axis=1, keepdims=True) + EPSILON)
    scr[...] = ((wide * inverse) * gain_ref[...]).astype(BF)
    for k in range(4):
        for j in range(4):
            inner[k][64 * j : 64 * (j + 1), :] = scr[:, block(base ^ (INNER[k] ^ OUTER[j]), 256)]
    for copy in copies:
        copy.wait()


def gather_rows_kernel(place, m0, m1, m2, m3, gkv, n, gkv_out, sem):
    copy = pltpu.make_async_copy(gkv, gkv_out, sem)
    copy.start()
    for k, ref in enumerate((m0, m1, m2, m3)):
        for j in range(4):
            n[64 * k : 64 * (k + 1), 256 * j : 256 * (j + 1)] = ref[64 * j : 64 * (j + 1), :]
    copy.wait()


def relay_kernel(place, k1, k2, out):
    out[0] = k2[...]
    out[1] = k1[1]


def gather_weights_kernel(place, m0, m1, m2, m3, k0, k1, k23, after, w):
    for k, ref in enumerate((m0, m1, m2, m3)):
        w[k, :256, :] = ref[256:, :]
    for j, piece in enumerate((k0[...], k1[0], k23[0], k23[1])):
        w[j, 256:, :] = piece


def near_kernel(place, own, got, a0, a1, a2, out):
    out[...] = (own[...].astype(F32) + got[...].astype(F32)).astype(BF)


def weight_lay_kernel(place, w0, w1, a0, a1, a2, a3, out):
    outer = place[2]
    for i, ref in enumerate((w0, w1)):
        part = place[11] ^ i
        for k in range(4):
            for m in range(2):
                out[2 * part + m, :, 256 * k : 256 * (k + 1)] = ref[k, 128 * m : 128 * (m + 1), :]
                lanes = pl.ds(pl.multiple_of(1024 + 256 * m + 128 * part, 128), 128)
                out[outer ^ k, :, lanes] = ref[k, 256:, 128 * m : 128 * (m + 1)]


def weight_join_kernel(place, mine, other, out):
    c = place[4]
    for half, ref in ((0, mine), (1, other)):
        for d in range(4):
            out[d, block(c ^ half, 128), :] = ref[d]


def rows_grad_kernel(which, place, g0, g1, g2, g3, kv0, kv1, w, after, o0, o1, scr):
    t = place[1]
    for j, out in zip(which, (o0, o1)):
        for k in range(4):
            rows = block(t ^ (OUTER[j] ^ INNER[k]), 64)
            here = slice(64 * k, 64 * (k + 1))
            for n, g in enumerate((g0, g1, g2, g3)):
                scr[here, 256 * n : 256 * (n + 1)] = g[rows, :]
            for a, kv in enumerate((kv0, kv1)):
                for p in range(2):
                    at = 1024 + 128 * (2 * a + p)
                    scr[here, at : at + 128] = kv[p, rows, :]
        left = scr[...]
        for d in range(4):
            value = lax.dot_general(left, w[d], (((1,), (1,)), ((), ())), preferred_element_type=F32)
            out[:, 256 * d : 256 * (d + 1)] = value.astype(out.dtype)


def rows_product(ns, d, right):
    total = None
    for j, n in enumerate(ns):
        value = lax.dot_general(
            n[:, 256 * d : 256 * (d + 1)],
            right[256 * j : 256 * (j + 1), :],
            (((0,), (0,)), ((), ())),
            preferred_element_type=F32,
        )
        total = value if total is None else total + value
    return total


def keyval_grad_kernel(place, n0, n1, n2, n3, kv0, kv1, after, keep, send, right):
    t, c = place[1], place[4]
    for j in range(4):
        for k in range(4):
            rows = block(t ^ (OUTER[j] ^ INNER[k]), 64)
            here = slice(256 * j + 64 * k, 256 * j + 64 * (k + 1))
            for half in range(2):
                for a, kv in enumerate((kv0, kv1)):
                    at = 256 * half + 128 * a
                    right[here, at : at + 128] = kv[c ^ half, rows, :]
    for d in range(4):
        total = rows_product((n0, n1, n2, n3), d, right)
        keep[256 * d : 256 * (d + 1), :] = total[:, :256]
        send[256 * d : 256 * (d + 1), :] = total[:, 256:]


def query_grad_kernel(place, n0, n1, n2, n3, g0, g1, g2, g3, after, keep, send, right):
    t = place[1]
    flip = place[5] == 1
    for j in range(4):
        for k in range(4):
            rows = block(t ^ (OUTER[j] ^ INNER[k]), 64)
            here = slice(256 * j + 64 * k, 256 * j + 64 * (k + 1))
            for a, (near, far) in enumerate(((g0, g1), (g2, g3))):
                right[here, 256 * a : 256 * (a + 1)] = jnp.where(flip, far[rows, :], near[rows, :])
                right[here, 512 + 256 * a : 768 + 256 * a] = jnp.where(flip, near[rows, :], far[rows, :])
    for d in range(4):
        total = rows_product((n0, n1, n2, n3), d, right)
        for a in range(2):
            keep[a, 256 * d : 256 * (d + 1), :] = total[:, 256 * a : 256 * (a + 1)]
            send[a, 256 * d : 256 * (d + 1), :] = total[:, 512 + 256 * a : 768 + 256 * a]


def keyval_pair_kernel(place, keep, got, o0, o1, o2, o3):
    for i, out in enumerate((o0, o1, o2, o3)):
        rows = block(place[3] ^ i, 256)
        out[...] = (keep[rows, :] + got[rows, :]).astype(out.dtype)


def query_pair_kernel(place, keep, got, after, o0, o1, o2, o3):
    for i, out in enumerate((o0, o1, o2, o3)):
        a = place[6] ^ (0, 1, 1, 0)[i]
        rows = block(place[7] ^ (i >> 1), 512)
        out[...] = (keep[a, rows, :] + got[a, rows, :]).astype(out.dtype)


def query_ring_kernel(place, own, r1, r2, r3, after, q_keep, q_send):
    h = place[8]

    def total(rows):
        return own[rows, :] + r1[rows, :].astype(F32) + r2[rows, :].astype(F32) + r3[rows, :].astype(F32)

    q_keep[...] = total(block(h, 256))
    q_send[...] = total(block(h ^ 1, 256)).astype(BF)


def keyval_ring_kernel(place, own, r1, r2, r3, after, out):
    out[...] = (own[...] + r1[...] + r2[...] + r3[...]).astype(BF)


def keyval_lay_kernel(place, a0, a1, a2, a3, b0, b1, b2, b3, out):
    c, head = place[4], place[12]
    for half, refs in ((0, (a0, a1, a2, a3)), (1, (b0, b1, b2, b3))):
        for i, ref in enumerate(refs):
            for a in range(2):
                lanes = block(head ^ (HEAD_STEP[i] ^ (2 * a)), 128)
                out[c ^ half, :, lanes] = ref[:, 128 * a : 128 * (a + 1)]


def owner_sum_kernel(place, own, beta, side, o0, o1, o2, o3):
    for k, out in enumerate((o0, o1, o2, o3)):
        rows = slice(64 * k, 64 * (k + 1))
        out[...] = (own[rows, :] + beta[rows, :].astype(F32) + side[rows, :].astype(F32)).astype(out.dtype)


def input_grad_kernel(place, x_ref, og_ref, gain_ref, p0, p1, p2, p3, out, scaled):
    base = place[0]
    for k, ref in enumerate((p0, p1, p2, p3)):
        for j in range(4):
            lanes = block(base ^ (INNER[k] ^ OUTER[j]), 256)
            scaled[:, lanes] = ref[:, 256 * j : 256 * (j + 1)].astype(F32) * gain_ref[:, lanes]
    wide = x_ref[...].astype(F32)
    inverse = lax.rsqrt(jnp.mean(wide * wide, axis=1, keepdims=True) + EPSILON)
    unit = wide * inverse
    grad = scaled[...]
    mean_term = jnp.mean(grad * unit, axis=1, keepdims=True)
    out[...] = og_ref[...].astype(F32) + inverse * (grad - unit * mean_term)


def shards(inputs, out_grad, gain, w_query, w_keyval, grad_query, grad_keyval):
    device = lax.axis_index("dp") * 16 + lax.axis_index("tensor")
    place = lax.dynamic_index_in_dim(jnp.asarray(TABLE), device, 0, keepdims=False)
    gain_row = gain.reshape(1, 4096)

    *inner, k0, k1, k2 = call(
        prepare_kernel,
        [((512, 256), BF)] * 4 + [((128, 256), BF), ((2, 128, 256), BF), ((128, 256), BF)],
        place,
        (inputs, gain_row, w_query, w_keyval),
        [
            pltpu.VMEM((64, 4096), BF),
            pltpu.VMEM((1, 4096), F32),
            pltpu.VMEM((64, 4096), BF),
            pltpu.SemaphoreType.DMA((18,)),
        ],
        spaces=[HBM] * 4,
        limit=60,
    )
    inner = [inner[0]] + [exchange(inner[k], "tensor", INNER[k]) for k in (1, 2, 3)]
    k1 = exchange(k1, "tensor", 2)
    g1, g2 = exchange(grad_query, "tensor", 1), exchange(grad_query, "tensor", 4)
    g = (grad_query, g1, g2, exchange(g1, "tensor", 4))
    n0, gkv = call(
        gather_rows_kernel,
        [((256, 1024), BF), ((2, 1024, 128), BF)],
        place,
        (*inner, grad_keyval),
        [pltpu.SemaphoreType.DMA],
        spaces=[VMEM] * 4 + [HBM],
    )
    (k23,) = call(relay_kernel, [((2, 128, 256), BF)], place, (k1, k2))
    k23 = exchange(k23, "tensor", 12)
    n1 = exchange(n0, "tensor", 2)
    n = (n0, n1, exchange(n0, "tensor", 12), exchange(n1, "tensor", 12))
    (w0,) = call(
        gather_weights_kernel,
        [((4, 384, 256), BF)],
        place,
        (*inner, k0, k1, k23, g1),
        spaces=[VMEM] * 7 + [ANY],

    )
    (kv_own,) = call(
        near_kernel,
        [((2, 1024, 128), BF)],
        place,
        (gkv, exchange(gkv, "tensor", 1), w0, n1, n[2]),
        spaces=[VMEM] * 2 + [ANY] * 3,
    )
    kv_far = exchange(kv_own, "tensor", 4)
    (half,) = call(
        weight_lay_kernel,
        [((4, 128, 1536), BF)],
        place,
        (w0, exchange(w0, "dp", 4), kv_far, g[3], g2, n[3]),
        spaces=[VMEM] * 2 + [ANY] * 4,
    )
    (w,) = call(weight_join_kernel, [((4, 256, 1536), BF)], place, (half, exchange(half, "dp", 1)))

    kv_keep, kv_send = call(
        keyval_grad_kernel,
        [((1024, 256), F32)] * 2,
        place,
        (*n, kv_own, kv_far, half),
        [pltpu.VMEM((1024, 512), BF)],
        spaces=[VMEM] * 6 + [ANY],
    )

    kv = call(
        keyval_pair_kernel,
        [((256, 256), F32)] * 4,
        place,
        (kv_keep, exchange(kv_send, "dp", 1)),
    )

    def rows_grad(which, kind, after):
        return call(
            lambda *refs: rows_grad_kernel(which, *refs),
            [((256, 1024), kind)] * 2,
            place,
            (*g, kv_own, kv_far, w, after),
            [pltpu.VMEM((256, 1536), BF)],
            spaces=[VMEM] * 7 + [ANY],
        )

    both, beta = rows_grad((3, 2), BF, kv[0])
    both_got = exchange(both, "tensor", 12)
    beta_got = exchange(beta, "tensor", 12)
    q_keep, q_send = call(
        query_grad_kernel,
        [((2, 1024, 256), F32)] * 2,
        place,
        (*n, *g, both),
        [pltpu.VMEM((1024, 1024), BF)],
        spaces=[VMEM] * 8 + [ANY],
    )
    q_got = exchange(q_send, "dp", 1)
    q = call(
        query_pair_kernel,
        [((512, 256), F32)] + [((512, 256), BF)] * 3,
        place,
        (q_keep, q_got, kv[0]),
        spaces=[VMEM] * 2 + [ANY],
    )
    side, own = rows_grad((1, 0), F32, q[0])
    side = (side + both_got.astype(F32)).astype(BF)
    side_got = exchange(side, "tensor", 2)

    everywhere = ("dp", "tensor")
    (kv,) = call(
        keyval_ring_kernel,
        [((256, 256), BF)],
        place,
        (kv[0], *(exchange(kv[i], "dp", 4 * i) for i in (1, 2, 3)), side),
        spaces=[VMEM] * 4 + [ANY],
    )
    kv = [lax.ppermute(kv, everywhere, keyval_turn(over)).astype(F32) for over in (0, 1)]
    kv = kv[0] + kv[1]
    near = [kv] + [exchange(kv, "dp", 4 * i) for i in (1, 2, 3)]
    far = [exchange(v, "dp", 1) for v in near]
    (keyval_weight_grad,) = call(keyval_lay_kernel, [((2, 256, 1024), F32)], place, (*near, *far))

    parts = call(
        owner_sum_kernel, [((64, 1024), F32)] + [((64, 1024), BF)] * 3, place, (own, beta_got, side_got)
    )
    parts = [parts[0]] + [exchange(parts[k], "tensor", INNER[k]) for k in (1, 2, 3)]
    (input_grad,) = call(
        input_grad_kernel,
        [((64, 4096), F32)],
        place,
        (inputs, out_grad, gain_row, *parts),
        [pltpu.VMEM((64, 4096), F32)],
    )

    q_keep, q_send = call(
        query_ring_kernel,
        [((256, 256), F32), ((256, 256), BF)],
        place,
        (q[0], *(exchange(q[i], "dp", 4 * i) for i in (1, 2, 3)), parts[0]),
        spaces=[VMEM] * 4 + [ANY],
    )
    query_weight_grad = lax.ppermute(q_keep, everywhere, query_turn(0)) + lax.ppermute(
        q_send, everywhere, query_turn(1)
    ).astype(F32)
    return (input_grad, query_weight_grad, keyval_weight_grad)


def solution(mesh):
    placed = (
        P(("dp", "tensor"), None),
        P(("dp", "tensor"), None),
        P(),
        P(None, "tensor"),
        P(None, "tensor", None),
        P("dp", "tensor"),
        P(None, "dp", "tensor"),
    )
    return jax.shard_map(
        shards,
        mesh=mesh,
        in_specs=placed,
        out_specs=(P(("dp", "tensor"), None), P("dp", "tensor"), P(None, "tensor", None)),
        check_vma=False,
    )
```

time: 231 us -> 189 us (0.82)
  the two profiles are of different devices: /device:TPU:17 before, /device:TPU:5 now
where the time goes in v2:
time: 189 us
  starting transfers between devices  89.3 us (47%)
  waiting for transfers between devices  68.3 us (36%)
  Pallas kernels  24.6 us (13%)
  local copies, waits for them, and re-layouts  4.96 us (3%)
    ppermute x36, starting transfers between devices, exchange(): return lax.ppermute(v, axis, [(i, i ^ flip) for i in range(16)])  60.3 us
    ppermute x36, waiting for transfers between devices, exchange(): return lax.ppermute(v, axis, [(i, i ^ flip) for i in range(16)])  59.2 us
    pallas_call x18, Pallas kernels, call(): pl.pallas_call(kernel, out_shape=[jax.ShapeDtypeStruct(s, d) for s, d in...  24.6 us
    ppermute x2, starting transfers between devices, shards(): lax.ppermute(kv, everywhere, keyval_turn(over)).astype(F32)  13 us
    ppermute x1, starting transfers between devices, shards(): lax.ppermute(q_send, everywhere, query_turn(1)).astype(F32)  8.71 us
    ppermute x1, starting transfers between devices, shards(): lax.ppermute(q_keep, everywhere, query_turn(0))  7.35 us
    ppermute x2, waiting for transfers between devices, shards(): lax.ppermute(kv, everywhere, keyval_turn(over)).astype(F32)  7.11 us
  transfers between devices with their start and end apart: 40, of which 15 were waited for; matrix products, arithmetic and copies ran while one was open for 0% of the time, Pallas kernels for 8%

profile of v2, /device:TPU:5, one launch (start us, length us, event | category | flops | bytes accessed | tf_op | source)
XLA Modules:
  0.0 189.0 jit_solution(4473246426548630912)
XLA Ops:
  0.7 1.4 dynamic-slice_bitcast_fusion.place.refs_0_
  2.0 3.3 %shard_map.103 = (bf16[512,256]{1,0:T(8,128)(2,1)}, bf16[512,256]{1,0:T(8,128)(2,1)}, bf16[512,256]{1,0:T(8,128)(2,1)}, bf16[512,256]{1,0:T(8,128)(2,1)}, bf16[1...) custom-call(s32[16]{0:T(128)} %dynamic-slice_bitcast_fusion.place.refs_0_, ...), custom_call_target="tpu_custom_call" | custom-call | bytes 1 | tf_op jit(solution)/shard_map/pallas_call | solution.py:99
  5.3 1.7 collective-permute-start.3
  7.1 1.3 collective-permute-start.4
  8.4 1.3 collective-permute-start
  9.7 3.0 %collective-permute-start.7 = (bf16[2,128,256]{2,1,0:T(8,128)(2,1)}, bf16[2,128,256]{2,1,0:T(8,128)(2,1)S(1)}, u32[]{:S(2)}, u32[]{:S(2)}) collective-permute-start(bf16[2,128,256]{2,1,0:T(8,128)(2,1)} %get-tuple-element.40), channel_id=1, source_target_pairs={{0,2},{1,3},{2,0},{3,1},{4,6},{5,7},{6,4},{7,5},{8,10},{9,11},{10,... | collective-permute-start | bytes 393224 | tf_op jit(solution)/shard_map/ppermute | solution.py:63
  13.2 0.9 collective-permute-done.4.m2
  14.1 8.5 %collective-permute-done.5.m3 = bf16[512,256]{1,0:T(8,128)(2,1)S(1)} collective-permute-done((bf16[512,256]{1,0:T(8,128)(2,1)}, bf16[512,256]{1,0:T(8,128)(2,1)S(1)}, u32[]{:S(2)}, u32[]{:S(2)}) %collective-permute-start.5) | collective-permute-done | bytes 262176 | tf_op jit(solution)/shard_map/ppermute | solution.py:63
  22.6 0.9 copy-done.2
  23.6 0.6 shard_map.104
  24.3 4.2 %collective-permute-start.9 = (bf16[256,1024]{1,0:T(8,128)(2,1)S(1)}, bf16[256,1024]{1,0:T(8,128)(2,1)S(1)}, u32[]{:S(2)}, u32[]{:S(2)}) collective-permute-start(bf16[256,1024]{1,0:T(8,128)(2,1)S(1)} %get-tuple-element.42.n0), channel_id=1, source_target_pairs={{0,2},{1,3},{2,0},{3,1},{4,6},{5,7},{6,4},{7,5},{8,10},{9,11},{10,... | collective-permute-start | bytes 1572872 | tf_op jit(solution)/shard_map/ppermute | solution.py:63
  28.6 1.9 %collective-permute-start.10 = (bf16[256,1024]{1,0:T(8,128)(2,1)S(1)}, bf16[256,1024]{1,0:T(8,128)(2,1)S(1)}, u32[]{:S(2)}, u32[]{:S(2)}) collective-permute-start(bf16[256,1024]{1,0:T(8,128)(2,1)S(1)} %get-tuple-element.42.n0), channel_id=1, source_target_pairs={{0,12},{1,13},{2,14},{3,15},{4,8},{5,9},{6,10},{7,11},{8,4},{9,5},... | collective-permute-start | bytes 1572872 | tf_op jit(solution)/shard_map/ppermute | solution.py:63
  30.5 1.6 collective-permute-done.7.k1
  32.1 0.8 copy-done.9
  33.5 2.8 %collective-permute-start.8 = (bf16[2,128,256]{2,1,0:T(8,128)(2,1)S(1)}, bf16[2,128,256]{2,1,0:T(8,128)(2,1)S(1)}, u32[]{:S(2)}, u32[]{:S(2)}) collective-permute-start(bf16[2,128,256]{2,1,0:T(8,128)(2,1)S(1)} %shard_map.105), channel_id=1, source_target_pairs={{0,12},{1,13},{2,14},{3,15},{4,8},{5,9},{6,10},{7,11},{8,4},{9,5},... | collective-permute-start | bytes 393224 | tf_op jit(solution)/shard_map/ppermute | solution.py:63
  36.2 6.5 %collective-permute-done.8.k23 = bf16[2,128,256]{2,1,0:T(8,128)(2,1)S(1)} collective-permute-done((bf16[2,128,256]{2,1,0:T(8,128)(2,1)S(1)}, bf16[2,128,256]{2,1,0:T(8,128)(2,1)S(1)}, u32[]{:S(2)}, u32[]{:S(2)}) %collective-permute-start.8) | collective-permute-done | bytes 131104 | tf_op jit(solution)/shard_map/ppermute | solution.py:63
  42.8 1.3 collective-permute-done.after.refs_2_.g1
  44.1 0.9 copy-done.3
  45.0 0.8 copy-done.8
  45.9 0.6 shard_map.106.a0.w0
  46.5 1.0 collective-permute-start.12
  47.5 1.3 collective-permute-start.1
  48.8 6.5 %collective-permute-done.6.got = bf16[2,1024,128]{2,1,0:T(8,128)(2,1)S(1)} collective-permute-done((bf16[2,1024,128]{2,1,0:T(8,128)(2,1)S(1)}, bf16[2,1024,128]{2,1,0:T(8,128)(2,1)S(1)}, u32[]{:S(2)}, u32[]{:S(2)}) %collective-permute-start.6) | collective-permute-done | bytes 524320 | tf_op jit(solution)/shard_map/ppermute | solution.py:63
  55.3 1.3 collective-permute-start.2
  56.6 0.7 shard_map.107.kv0.refs_5_
  57.6 2.7 %collective-permute-start.13 = (bf16[256,1024]{1,0:T(8,128)(2,1)S(1)}, bf16[256,1024]{1,0:T(8,128)(2,1)S(1)}, u32[]{:S(2)}, u32[]{:S(2)}) collective-permute-start(bf16[256,1024]{1,0:T(8,128)(2,1)S(1)} %collective-permute-done.9.a1.n1), channel_id=1, source_target_pairs={{0,12},{1,13},{2,14},{3,15},{4,8},{5,9},{6,10},{7,11},{8,4},{9,5},... | collective-permute-start | bytes 1572872 | tf_op jit(solution)/shard_map/ppermute | solution.py:63
  60.3 9.0 %collective-permute-done.2.a1.refs_4_.g3 = bf16[1024,256]{1,0:T(8,128)(2,1)S(1)} collective-permute-done((bf16[1024,256]{1,0:T(8,128)(2,1)S(1)}, bf16[1024,256]{1,0:T(8,128)(2,1)S(1)}, u32[]{:S(2)}, u32[]{:S(2)}) %collective-permute-start.2) | collective-permute-done | bytes 524320 | tf_op jit(solution)/shard_map/ppermute | solution.py:63
  69.3 11.2 %collective-permute-done.11.a0.kv1.refs_6_ = bf16[2,1024,128]{2,1,0:T(8,128)(2,1)S(1)} collective-permute-done((bf16[2,1024,128]{2,1,0:T(8,128)(2,1)S(1)}, bf16[2,1024,128]{2,1,0:T(8,128)(2,1)S(1)}, u32[]{:S(2)}, u32[]{:S(2)}) %collective-permute-start.11) | collective-permute-done | bytes 524320 | tf_op jit(solution)/shard_map/ppermute | solution.py:63
  80.6 0.7 shard_map.108.mine.after
  81.3 3.8 %collective-permute-start.14 = (bf16[4,128,1536]{2,1,0:T(8,128)(2,1)S(1)}, bf16[4,128,1536]{2,1,0:T(8,128)(2,1)S(1)}, u32[]{:S(2)}, u32[]{:S(2)}) collective-permute-start(bf16[4,128,1536]{2,1,0:T(8,128)(2,1)S(1)} %shard_map.108.mine.after), channel_id=1, source_target_pairs={{0,16},{16,0},{32,48},{48,32},{64,80},{80,64},{96,112},{112,96},{1... | collective-permute-start | bytes 4718600 | tf_op jit(solution)/shard_map/ppermute | solution.py:63
  85.1 1.9 %shard_map.110 = (f32[1024,256]{1,0:T(8,128)S(1)}, f32[1024,256]{1,0:T(8,128)S(1)}) custom-call(s32[16]{0:T(128)S(1)} %copy-done.6, bf16[256,1024]{1,0:T(8,128)(2,1)S(1)} %get-tuple-element.42.n0, bf16[256,1024]{1,0:T(8,128)(2,1)S(1)} %collective-permute-done.9.a1.n1, bf16[256,1024]{1,0:T(8,128)(2,1)S(1)} %collective-permute-done.10.a2.n2, ...), custom_call_target="tpu_custom_call" | custom-call | bytes 1 | tf_op jit(solution)/shard_map/pallas_call | solution.py:99
  87.3 2.6 %collective-permute-done.15.got = f32[1024,256]{1,0:T(8,128)S(1)} collective-permute-done((f32[1024,256]{1,0:T(8,128)S(1)}, f32[1024,256]{1,0:T(8,128)S(1)}, u32[]{:S(2)}, u32[]{:S(2)}) %collective-permute-start.15) | collective-permute-done | bytes 1048608 | tf_op jit(solution)/shard_map/ppermute | solution.py:63
  89.9 0.7 shard_map.111
  90.6 0.7 shard_map.109.refs_7_
  91.4 2.4 %shard_map.112 = (bf16[256,1024]{1,0:T(8,128)(2,1)S(1)}, bf16[256,1024]{1,0:T(8,128)(2,1)S(1)}) custom-call(s32[16]{0:T(128)S(1)} %copy-done.6, bf16[1024,256]{1,0:T(8,128)(2,1)S(1)} %copy-done, bf16[1024,256]{1,0:T(8,128)(2,1)S(1)} %collective-permute-done.after.refs_2_.g1, bf16[1024,256]{1,0:T(8,128)(2,1)S(1)} %collective-permute-done.1.a2.refs_3_.g2, ...), custom_call_target="tpu_custom_call" | custom-call | bytes 1 | tf_op jit(solution)/shard_map/pallas_call | solution.py:99
  93.8 3.0 %shard_map.113 = (f32[2,1024,256]{2,1,0:T(8,128)S(1)}, f32[2,1024,256]{2,1,0:T(8,128)S(1)}) custom-call(s32[16]{0:T(128)S(1)} %copy-done.6, bf16[256,1024]{1,0:T(8,128)(2,1)S(1)} %get-tuple-element.42.n0, bf16[256,1024]{1,0:T(8,128)(2,1)S(1)} %collective-permute-done.9.a1.n1, bf16[256,1024]{1,0:T(8,128)(2,1)S(1)} %collective-permute-done.10.a2.n2, ...), custom_call_target="tpu_custom_call" | custom-call | bytes 1 | tf_op jit(solution)/shard_map/pallas_call | solution.py:99
  97.0 2.7 %collective-permute-start.18 = (bf16[256,1024]{1,0:T(8,128)(2,1)S(1)}, bf16[256,1024]{1,0:T(8,128)(2,1)S(1)}, u32[]{:S(2)}, u32[]{:S(2)}) collective-permute-start(bf16[256,1024]{1,0:T(8,128)(2,1)S(1)} %get-tuple-element.46.after), channel_id=1, source_target_pairs={{0,12},{1,13},{2,14},{3,15},{4,8},{5,9},{6,10},{7,11},{8,4},{9,5},... | collective-permute-start | bytes 1572872 | tf_op jit(solution)/shard_map/ppermute | solution.py:63
  100.6 1.9 collective-permute-start.30
  102.4 1.4 collective-permute-start.17
  103.8 0.7 shard_map.114
  104.6 2.4 %shard_map.115 = (f32[256,1024]{1,0:T(8,128)S(1)}, f32[256,1024]{1,0:T(8,128)S(1)}) custom-call(s32[16]{0:T(128)S(1)} %copy-done.6, bf16[1024,256]{1,0:T(8,128)(2,1)S(1)} %copy-done, bf16[1024,256]{1,0:T(8,128)(2,1)S(1)} %collective-permute-done.after.refs_2_.g1, bf16[1024,256]{1,0:T(8,128)(2,1)S(1)} %collective-permute-done.1.a2.refs_3_.g2, ...), custom_call_target="tpu_custom_call" | custom-call | bytes 1 | tf_op jit(solution)/shard_map/pallas_call | solution.py:99
  107.0 4.5 %collective-permute-done.18 = bf16[256,1024]{1,0:T(8,128)(2,1)S(1)} collective-permute-done((bf16[256,1024]{1,0:T(8,128)(2,1)S(1)}, bf16[256,1024]{1,0:T(8,128)(2,1)S(1)}, u32[]{:S(2)}, u32[]{:S(2)}) %collective-permute-start.18) | collective-permute-done | bytes 524320 | tf_op jit(solution)/shard_map/ppermute | solution.py:63
  111.7 2.1 %collective-permute-start.19 = (bf16[256,1024]{1,0:T(8,128)(2,1)S(1)}, bf16[256,1024]{1,0:T(8,128)(2,1)S(1)}, u32[]{:S(2)}, u32[]{:S(2)}) collective-permute-start(bf16[256,1024]{1,0:T(8,128)(2,1)S(1)} %add_convert_fusion.after), channel_id=1, source_target_pairs={{0,2},{1,3},{2,0},{3,1},{4,6},{5,7},{6,4},{7,5},{8,10},{9,11},{10,... | collective-permute-start | bytes 1572872 | tf_op jit(solution)/shard_map/ppermute | solution.py:63
  113.8 0.6 shard_map.119
  114.4 9.2 %collective-permute-start.32 = (bf16[256,256]{1,0:T(8,128)(2,1)S(1)}, bf16[256,256]{1,0:T(8,128)(2,1)S(1)}, u32[]{:S(2)}, u32[]{:S(2)}) collective-permute-start(bf16[256,256]{1,0:T(8,128)(2,1)S(1)} %shard_map.119), channel_id=1, source_target_pairs={{0,32},{1,33},{2,96},{3,97},{4,36},{5,37},{6,100},{7,101},{8,164},... | collective-permute-start | bytes 393224 | tf_op jit(solution)/shard_map/ppermute | solution.py:426
  123.6 3.8 %collective-permute-start.31 = (bf16[256,256]{1,0:T(8,128)(2,1)S(1)}, bf16[256,256]{1,0:T(8,128)(2,1)S(1)}, u32[]{:S(2)}, u32[]{:S(2)}) collective-permute-start(bf16[256,256]{1,0:T(8,128)(2,1)S(1)} %shard_map.119), channel_id=1, source_target_pairs={{0,0},{1,1},{2,64},{3,65},{4,4},{5,5},{6,68},{7,69},{8,132},{9,133... | collective-permute-start | bytes 393224 | tf_op jit(solution)/shard_map/ppermute | solution.py:426
  127.4 2.1 %collective-permute-start.23 = (bf16[512,256]{1,0:T(8,128)(2,1)S(1)}, bf16[512,256]{1,0:T(8,128)(2,1)S(1)}, u32[]{:S(2)}, u32[]{:S(2)}) collective-permute-start(bf16[512,256]{1,0:T(8,128)(2,1)S(1)} %get-tuple-element.57), channel_id=1, source_target_pairs={{0,64},{16,80},{32,96},{48,112},{64,0},{80,16},{96,32},{112,48},{1... | collective-permute-start | bytes 786440 | tf_op jit(solution)/shard_map/ppermute | solution.py:63
  129.5 7.1 %collective-permute-done.32 = bf16[256,256]{1,0:T(8,128)(2,1)S(1)} collective-permute-done((bf16[256,256]{1,0:T(8,128)(2,1)S(1)}, bf16[256,256]{1,0:T(8,128)(2,1)S(1)}, u32[]{:S(2)}, u32[]{:S(2)}) %collective-permute-start.32) | collective-permute-done | bytes 131104 | tf_op jit(solution)/shard_map/ppermute | solution.py:426
  136.6 8.1 %collective-permute-start.25 = (bf16[512,256]{1,0:T(8,128)(2,1)S(1)}, bf16[512,256]{1,0:T(8,128)(2,1)S(1)}, u32[]{:S(2)}, u32[]{:S(2)}) collective-permute-start(bf16[512,256]{1,0:T(8,128)(2,1)S(1)} %get-tuple-element.59), channel_id=1, source_target_pairs={{0,192},{16,208},{32,224},{48,240},{64,128},{80,144},{96,160},{112... | collective-permute-start | bytes 786440 | tf_op jit(solution)/shard_map/ppermute | solution.py:63
  144.7 3.2 %collective-permute-start.33 = (f32[256,256]{1,0:T(8,128)S(1)}, f32[256,256]{1,0:T(8,128)S(1)}, u32[]{:S(2)}, u32[]{:S(2)}) collective-permute-start(f32[256,256]{1,0:T(8,128)S(1)} %convert_add_fusion.a0), channel_id=1, source_target_pairs={{0,64},{16,80},{32,96},{48,112},{64,0},{80,16},{96,32},{112,48},{1... | collective-permute-start | bytes 786440 | tf_op jit(solution)/shard_map/ppermute | solution.py:63
  148.0 1.9 collective-permute-start.34
  150.1 3.3 %collective-permute-start.36 = (f32[256,256]{1,0:T(8,128)S(1)}, f32[256,256]{1,0:T(8,128)S(1)}, u32[]{:S(2)}, u32[]{:S(2)}) collective-permute-start(f32[256,256]{1,0:T(8,128)S(1)} %convert_add_fusion.a0), channel_id=1, source_target_pairs={{0,16},{16,0},{32,48},{48,32},{64,80},{80,64},{96,112},{112,96},{1... | collective-permute-start | bytes 786440 | tf_op jit(solution)/shard_map/ppermute | solution.py:63
  153.5 0.7 shard_map.116
  154.4 0.7 shard_map.118
  155.0 3.9 %collective-permute-done.34.a2 = f32[256,256]{1,0:T(8,128)S(1)} collective-permute-done((f32[256,256]{1,0:T(8,128)S(1)}, f32[256,256]{1,0:T(8,128)S(1)}, u32[]{:S(2)}, u32[]{:S(2)}) %collective-permute-start.34) | collective-permute-done | bytes 262176 | tf_op jit(solution)/shard_map/ppermute | solution.py:63
  158.9 3.8 %collective-permute-start.37 = (f32[256,256]{1,0:T(8,128)S(1)}, f32[256,256]{1,0:T(8,128)S(1)}, u32[]{:S(2)}, u32[]{:S(2)}) collective-permute-start(f32[256,256]{1,0:T(8,128)S(1)} %collective-permute-done.33.a1), channel_id=1, source_target_pairs={{0,16},{16,0},{32,48},{48,32},{64,80},{80,64},{96,112},{112,96},{1... | collective-permute-start | bytes 786440 | tf_op jit(solution)/shard_map/ppermute | solution.py:63
  162.7 1.9 %collective-permute-done.35.a3 = f32[256,256]{1,0:T(8,128)S(1)} collective-permute-done((f32[256,256]{1,0:T(8,128)S(1)}, f32[256,256]{1,0:T(8,128)S(1)}, u32[]{:S(2)}, u32[]{:S(2)}) %collective-permute-start.35) | collective-permute-done | bytes 262176 | tf_op jit(solution)/shard_map/ppermute | solution.py:63
  164.6 1.2 collective-permute-start.38
  166.0 7.3 %collective-permute-start.26 = (f32[256,256]{1,0:T(8,128)S(1)}, f32[256,256]{1,0:T(8,128)S(1)}, u32[]{:S(2)}, u32[]{:S(2)}) collective-permute-start(f32[256,256]{1,0:T(8,128)S(1)} %get-tuple-element.60), channel_id=1, source_target_pairs={{0,0},{1,16},{2,2},{3,18},{4,64},{5,80},{6,66},{7,82},{8,76},{9,92... | collective-permute-start | bytes 786440 | tf_op jit(solution)/shard_map/ppermute | solution.py:451
  173.3 8.7 %collective-permute-start.27 = (bf16[256,256]{1,0:T(8,128)(2,1)S(1)}, bf16[256,256]{1,0:T(8,128)(2,1)S(1)}, u32[]{:S(2)}, u32[]{:S(2)}) collective-permute-start(bf16[256,256]{1,0:T(8,128)(2,1)S(1)} %get-tuple-element.61), channel_id=1, source_target_pairs={{0,32},{1,48},{2,34},{3,50},{4,96},{5,112},{6,98},{7,114},{8,108},... | collective-permute-start | bytes 393224 | tf_op jit(solution)/shard_map/ppermute | solution.py:451
  182.0 2.2 %shard_map.117 = f32[64,4096]{1,0:T(8,128)} custom-call(s32[16]{0:T(128)S(1)} %copy-done.6, bf16[64,4096]{1,0:T(8,128)(2,1)S(1)} %copy-done.1, bf16[64,4096]{1,0:T(8,128)(2,1)S(1)} %copy-done.5, f32[1,4096]{1,0:T(1,128)S(1)} %bitcast.4, f32[64,1024]{1,0:T(8,128)S(1)} %get-tuple-element.53.p0.after, bf16[64,1024]{1,0:T(8,128)(2,1)S(1)} %collective-permute-done.20.p1, ...), custom_call_target="tpu_custom_call" | custom-call | bytes 1 | tf_op jit(solution)/shard_map/pallas_call | solution.py:99
  184.2 2.1 %shard_map.120 = f32[2,256,1024]{2,1,0:T(8,128)} custom-call(s32[16]{0:T(128)S(1)} %copy-done.6, f32[256,256]{1,0:T(8,128)S(1)} %convert_add_fusion.a0, f32[256,256]{1,0:T(8,128)S(1)} %collective-permute-done.33.a1, f32[256,256]{1,0:T(8,128)S(1)} %collective-permute-done.34.a2, f32[256,256]{1,0:T(8,128)S(1)} %collective-permute-done.35.a3, ...), custom_call_target="tpu_custom_call" | custom-call | bytes 1 | tf_op jit(solution)/shard_map/pallas_call | solution.py:99
  186.3 1.9 %collective-permute-done.27 = bf16[256,256]{1,0:T(8,128)(2,1)S(1)} collective-permute-done((bf16[256,256]{1,0:T(8,128)(2,1)S(1)}, bf16[256,256]{1,0:T(8,128)(2,1)S(1)}, u32[]{:S(2)}, u32[]{:S(2)}) %collective-permute-start.27) | collective-permute-done | bytes 131104 | tf_op jit(solution)/shard_map/ppermute | solution.py:451
  188.3 0.7 convert_add_fusion.1
  (58 shorter events, 3.5 us)
Async XLA Ops:
  0.6 7.7 %copy-start = (bf16[1024,256]{1,0:T(8,128)(2,1)S(1)}, bf16[1024,256]{1,0:T(8,128)(2,1)}, u32[]{:S(2)}) copy-start(bf16[1024,256]{1,0:T(8,128)(2,1)} %refs_1_.3) | copy-start | bytes 1572868
  0.6 22.0 %copy-start.4 = (bf16[2,1024,128]{2,1,0:T(8,128)(2,1)S(1)}, bf16[2,1024,128]{2,1,0:T(8,128)(2,1)}, u32[]{:S(2)}) copy-start(bf16[2,1024,128]{2,1,0:T(8,128)(2,1)} %gkv.1) | copy-start | bytes 1572868
  2.0 20.6 %copy-start.6 = (s32[16]{0:T(128)S(1)}, s32[16]{0:T(128)}, u32[]{:S(2)}) copy-start(s32[16]{0:T(128)} %dynamic-slice_bitcast_fusion.place.refs_0_) | copy-start | bytes 196
  5.3 7.8 %collective-permute-start.3 = (bf16[512,256]{1,0:T(8,128)(2,1)}, bf16[512,256]{1,0:T(8,128)(2,1)S(1)}, u32[]{:S(2)}, u32[]{:S(2)}) collective-permute-start(bf16[512,256]{1,0:T(8,128)(2,1)} %get-tuple-element.35), channel_id=1, source_target_pairs={{0,1},{1,0},{2,3},{3,2},{4,5},{5,4},{6,7},{7,6},{8,9},{9,8},{10,11... | collective-permute-start | bytes 786440 | tf_op jit(solution)/shard_map/ppermute | solution.py:63
  7.1 7.1 %collective-permute-start.4 = (bf16[512,256]{1,0:T(8,128)(2,1)}, bf16[512,256]{1,0:T(8,128)(2,1)S(1)}, u32[]{:S(2)}, u32[]{:S(2)}) collective-permute-start(bf16[512,256]{1,0:T(8,128)(2,1)} %get-tuple-element.36), channel_id=1, source_target_pairs={{0,4},{1,5},{2,6},{3,7},{4,0},{5,1},{6,2},{7,3},{8,12},{9,13},{10,... | collective-permute-start | bytes 786440 | tf_op jit(solution)/shard_map/ppermute | solution.py:63
  8.4 14.3 %collective-permute-start.5 = (bf16[512,256]{1,0:T(8,128)(2,1)}, bf16[512,256]{1,0:T(8,128)(2,1)S(1)}, u32[]{:S(2)}, u32[]{:S(2)}) collective-permute-start(bf16[512,256]{1,0:T(8,128)(2,1)} %get-tuple-element.37), channel_id=1, source_target_pairs={{0,5},{1,4},{2,7},{3,6},{4,1},{5,0},{6,3},{7,2},{8,13},{9,12},{10,... | collective-permute-start | bytes 786440 | tf_op jit(solution)/shard_map/ppermute | solution.py:63
  8.4 35.7 %collective-permute-start = (bf16[1024,256]{1,0:T(8,128)(2,1)S(1)}, bf16[1024,256]{1,0:T(8,128)(2,1)S(1)}, u32[]{:S(2)}, u32[]{:S(2)}) collective-permute-start(bf16[1024,256]{1,0:T(8,128)(2,1)S(1)} %copy-done), channel_id=1, source_target_pairs={{0,1},{1,0},{2,3},{3,2},{4,5},{5,4},{6,7},{7,6},{8,9},{9,8},{10,11... | collective-permute-start | bytes 1572872 | tf_op jit(solution)/shard_map/ppermute | solution.py:63
  9.7 22.3 %collective-permute-start.7 = (bf16[2,128,256]{2,1,0:T(8,128)(2,1)}, bf16[2,128,256]{2,1,0:T(8,128)(2,1)S(1)}, u32[]{:S(2)}, u32[]{:S(2)}) collective-permute-start(bf16[2,128,256]{2,1,0:T(8,128)(2,1)} %get-tuple-element.40), channel_id=1, source_target_pairs={{0,2},{1,3},{2,0},{3,1},{4,6},{5,7},{6,4},{7,5},{8,10},{9,11},{10,... | collective-permute-start | bytes 393224 | tf_op jit(solution)/shard_map/ppermute | solution.py:63
  22.6 1.0 copy-start.2
  24.2 31.1 %collective-permute-start.6 = (bf16[2,1024,128]{2,1,0:T(8,128)(2,1)S(1)}, bf16[2,1024,128]{2,1,0:T(8,128)(2,1)S(1)}, u32[]{:S(2)}, u32[]{:S(2)}) collective-permute-start(bf16[2,1024,128]{2,1,0:T(8,128)(2,1)S(1)} %get-tuple-element.38.own), channel_id=1, source_target_pairs={{0,1},{1,0},{2,3},{3,2},{4,5},{5,4},{6,7},{7,6},{8,9},{9,8},{10,11... | collective-permute-start | bytes 1572872 | tf_op jit(solution)/shard_map/ppermute | solution.py:63
  24.3 32.3 %collective-permute-start.9 = (bf16[256,1024]{1,0:T(8,128)(2,1)S(1)}, bf16[256,1024]{1,0:T(8,128)(2,1)S(1)}, u32[]{:S(2)}, u32[]{:S(2)}) collective-permute-start(bf16[256,1024]{1,0:T(8,128)(2,1)S(1)} %get-tuple-element.42.n0), channel_id=1, source_target_pairs={{0,2},{1,3},{2,0},{3,1},{4,6},{5,7},{6,4},{7,5},{8,10},{9,11},{10,... | collective-permute-start | bytes 1572872 | tf_op jit(solution)/shard_map/ppermute | solution.py:63
  28.6 28.1 %collective-permute-start.10 = (bf16[256,1024]{1,0:T(8,128)(2,1)S(1)}, bf16[256,1024]{1,0:T(8,128)(2,1)S(1)}, u32[]{:S(2)}, u32[]{:S(2)}) collective-permute-start(bf16[256,1024]{1,0:T(8,128)(2,1)S(1)} %get-tuple-element.42.n0), channel_id=1, source_target_pairs={{0,12},{1,13},{2,14},{3,15},{4,8},{5,9},{6,10},{7,11},{8,4},{9,5},... | collective-permute-start | bytes 1572872 | tf_op jit(solution)/shard_map/ppermute | solution.py:63
  32.1 0.8 copy-start.9
  33.5 9.3 %collective-permute-start.8 = (bf16[2,128,256]{2,1,0:T(8,128)(2,1)S(1)}, bf16[2,128,256]{2,1,0:T(8,128)(2,1)S(1)}, u32[]{:S(2)}, u32[]{:S(2)}) collective-permute-start(bf16[2,128,256]{2,1,0:T(8,128)(2,1)S(1)} %shard_map.105), channel_id=1, source_target_pairs={{0,12},{1,13},{2,14},{3,15},{4,8},{5,9},{6,10},{7,11},{8,4},{9,5},... | collective-permute-start | bytes 393224 | tf_op jit(solution)/shard_map/ppermute | solution.py:63
  44.1 1.0 copy-start.3
  45.0 0.8 copy-start.8
  46.5 34.1 %collective-permute-start.12 = (bf16[4,384,256]{2,1,0:T(8,128)(2,1)S(1)}, bf16[4,384,256]{2,1,0:T(8,128)(2,1)S(1)}, u32[]{:S(2)}, u32[]{:S(2)}) collective-permute-start(bf16[4,384,256]{2,1,0:T(8,128)(2,1)S(1)} %shard_map.106.a0.w0), channel_id=1, source_target_pairs={{0,64},{16,80},{32,96},{48,112},{64,0},{80,16},{96,32},{112,48},{1... | collective-permute-start | bytes 2359304 | tf_op jit(solution)/shard_map/ppermute | solution.py:63
  47.5 12.8 %collective-permute-start.1 = (bf16[1024,256]{1,0:T(8,128)(2,1)S(1)}, bf16[1024,256]{1,0:T(8,128)(2,1)S(1)}, u32[]{:S(2)}, u32[]{:S(2)}) collective-permute-start(bf16[1024,256]{1,0:T(8,128)(2,1)S(1)} %copy-done), channel_id=1, source_target_pairs={{0,4},{1,5},{2,6},{3,7},{4,0},{5,1},{6,2},{7,3},{8,12},{9,13},{10,... | collective-permute-start | bytes 1572872 | tf_op jit(solution)/shard_map/ppermute | solution.py:63
  55.3 14.0 %collective-permute-start.2 = (bf16[1024,256]{1,0:T(8,128)(2,1)S(1)}, bf16[1024,256]{1,0:T(8,128)(2,1)S(1)}, u32[]{:S(2)}, u32[]{:S(2)}) collective-permute-start(bf16[1024,256]{1,0:T(8,128)(2,1)S(1)} %collective-permute-done.after.refs_2_.g1), channel_id=1, source_target_pairs={{0,4},{1,5},{2,6},{3,7},{4,0},{5,1},{6,2},{7,3},{8,12},{9,13},{10,... | collective-permute-start | bytes 1572872 | tf_op jit(solution)/shard_map/ppermute | solution.py:63
  57.3 23.3 %collective-permute-start.11 = (bf16[2,1024,128]{2,1,0:T(8,128)(2,1)S(1)}, bf16[2,1024,128]{2,1,0:T(8,128)(2,1)S(1)}, u32[]{:S(2)}, u32[]{:S(2)}) collective-permute-start(bf16[2,1024,128]{2,1,0:T(8,128)(2,1)S(1)} %shard_map.107.kv0.refs_5_), channel_id=1, source_target_pairs={{0,4},{1,5},{2,6},{3,7},{4,0},{5,1},{6,2},{7,3},{8,12},{9,13},{10,... | collective-permute-start | bytes 1572872 | tf_op jit(solution)/shard_map/ppermute | solution.py:63
  57.6 23.0 %collective-permute-start.13 = (bf16[256,1024]{1,0:T(8,128)(2,1)S(1)}, bf16[256,1024]{1,0:T(8,128)(2,1)S(1)}, u32[]{:S(2)}, u32[]{:S(2)}) collective-permute-start(bf16[256,1024]{1,0:T(8,128)(2,1)S(1)} %collective-permute-done.9.a1.n1), channel_id=1, source_target_pairs={{0,12},{1,13},{2,14},{3,15},{4,8},{5,9},{6,10},{7,11},{8,4},{9,5},... | collective-permute-start | bytes 1572872 | tf_op jit(solution)/shard_map/ppermute | solution.py:63
  81.3 9.3 %collective-permute-start.14 = (bf16[4,128,1536]{2,1,0:T(8,128)(2,1)S(1)}, bf16[4,128,1536]{2,1,0:T(8,128)(2,1)S(1)}, u32[]{:S(2)}, u32[]{:S(2)}) collective-permute-start(bf16[4,128,1536]{2,1,0:T(8,128)(2,1)S(1)} %shard_map.108.mine.after), channel_id=1, source_target_pairs={{0,16},{16,0},{32,48},{48,32},{64,80},{80,64},{96,112},{112,96},{1... | collective-permute-start | bytes 4718600 | tf_op jit(solution)/shard_map/ppermute | solution.py:63
  87.0 2.9 %collective-permute-start.15 = (f32[1024,256]{1,0:T(8,128)S(1)}, f32[1024,256]{1,0:T(8,128)S(1)}, u32[]{:S(2)}, u32[]{:S(2)}) collective-permute-start(f32[1024,256]{1,0:T(8,128)S(1)} %get-tuple-element.44), channel_id=1, source_target_pairs={{0,16},{16,0},{32,48},{48,32},{64,80},{80,64},{96,112},{112,96},{1... | collective-permute-start | bytes 3145736 | tf_op jit(solution)/shard_map/ppermute | solution.py:63
  96.8 5.6 %collective-permute-start.16 = (f32[2,1024,256]{2,1,0:T(8,128)S(1)}, f32[2,1024,256]{2,1,0:T(8,128)S(1)}, u32[]{:S(2)}, u32[]{:S(2)}) collective-permute-start(f32[2,1024,256]{2,1,0:T(8,128)S(1)} %get-tuple-element.48), channel_id=1, source_target_pairs={{0,16},{16,0},{32,48},{48,32},{64,80},{80,64},{96,112},{112,96},{1... | collective-permute-start | bytes 6291464 | tf_op jit(solution)/shard_map/ppermute | solution.py:63
  97.0 14.5 %collective-permute-start.18 = (bf16[256,1024]{1,0:T(8,128)(2,1)S(1)}, bf16[256,1024]{1,0:T(8,128)(2,1)S(1)}, u32[]{:S(2)}, u32[]{:S(2)}) collective-permute-start(bf16[256,1024]{1,0:T(8,128)(2,1)S(1)} %get-tuple-element.46.after), channel_id=1, source_target_pairs={{0,12},{1,13},{2,14},{3,15},{4,8},{5,9},{6,10},{7,11},{8,4},{9,5},... | collective-permute-start | bytes 1572872 | tf_op jit(solution)/shard_map/ppermute | solution.py:63
  99.8 14.0 %collective-permute-start.28 = (f32[256,256]{1,0:T(8,128)S(1)}, f32[256,256]{1,0:T(8,128)S(1)}, u32[]{:S(2)}, u32[]{:S(2)}) collective-permute-start(f32[256,256]{1,0:T(8,128)S(1)} %get-tuple-element.62), channel_id=1, source_target_pairs={{0,64},{16,80},{32,96},{48,112},{64,0},{80,16},{96,32},{112,48},{1... | collective-permute-start | bytes 786440 | tf_op jit(solution)/shard_map/ppermute | solution.py:63
  100.3 13.5 %collective-permute-start.29 = (f32[256,256]{1,0:T(8,128)S(1)}, f32[256,256]{1,0:T(8,128)S(1)}, u32[]{:S(2)}, u32[]{:S(2)}) collective-permute-start(f32[256,256]{1,0:T(8,128)S(1)} %get-tuple-element.63), channel_id=1, source_target_pairs={{0,128},{16,144},{32,160},{48,176},{64,192},{80,208},{96,224},{112... | collective-permute-start | bytes 786440 | tf_op jit(solution)/shard_map/ppermute | solution.py:63
  100.6 13.2 %collective-permute-start.30 = (f32[256,256]{1,0:T(8,128)S(1)}, f32[256,256]{1,0:T(8,128)S(1)}, u32[]{:S(2)}, u32[]{:S(2)}) collective-permute-start(f32[256,256]{1,0:T(8,128)S(1)} %get-tuple-element.64), channel_id=1, source_target_pairs={{0,192},{16,208},{32,224},{48,240},{64,128},{80,144},{96,160},{112... | collective-permute-start | bytes 786440 | tf_op jit(solution)/shard_map/ppermute | solution.py:63
  102.4 42.3 %collective-permute-start.17 = (bf16[256,1024]{1,0:T(8,128)(2,1)S(1)}, bf16[256,1024]{1,0:T(8,128)(2,1)S(1)}, u32[]{:S(2)}, u32[]{:S(2)}) collective-permute-start(bf16[256,1024]{1,0:T(8,128)(2,1)S(1)} %get-tuple-element.51), channel_id=1, source_target_pairs={{0,12},{1,13},{2,14},{3,15},{4,8},{5,9},{6,10},{7,11},{8,4},{9,5},... | collective-permute-start | bytes 1572872 | tf_op jit(solution)/shard_map/ppermute | solution.py:63
  111.7 38.4 %collective-permute-start.19 = (bf16[256,1024]{1,0:T(8,128)(2,1)S(1)}, bf16[256,1024]{1,0:T(8,128)(2,1)S(1)}, u32[]{:S(2)}, u32[]{:S(2)}) collective-permute-start(bf16[256,1024]{1,0:T(8,128)(2,1)S(1)} %add_convert_fusion.after), channel_id=1, source_target_pairs={{0,2},{1,3},{2,0},{3,1},{4,6},{5,7},{6,4},{7,5},{8,10},{9,11},{10,... | collective-permute-start | bytes 1572872 | tf_op jit(solution)/shard_map/ppermute | solution.py:63
  114.4 22.2 %collective-permute-start.32 = (bf16[256,256]{1,0:T(8,128)(2,1)S(1)}, bf16[256,256]{1,0:T(8,128)(2,1)S(1)}, u32[]{:S(2)}, u32[]{:S(2)}) collective-permute-start(bf16[256,256]{1,0:T(8,128)(2,1)S(1)} %shard_map.119), channel_id=1, source_target_pairs={{0,32},{1,33},{2,96},{3,97},{4,36},{5,37},{6,100},{7,101},{8,164},... | collective-permute-start | bytes 393224 | tf_op jit(solution)/shard_map/ppermute | solution.py:426
  123.6 13.0 %collective-permute-start.31 = (bf16[256,256]{1,0:T(8,128)(2,1)S(1)}, bf16[256,256]{1,0:T(8,128)(2,1)S(1)}, u32[]{:S(2)}, u32[]{:S(2)}) collective-permute-start(bf16[256,256]{1,0:T(8,128)(2,1)S(1)} %shard_map.119), channel_id=1, source_target_pairs={{0,0},{1,1},{2,64},{3,65},{4,4},{5,5},{6,68},{7,69},{8,132},{9,133... | collective-permute-start | bytes 393224 | tf_op jit(solution)/shard_map/ppermute | solution.py:426
  127.4 20.6 %collective-permute-start.23 = (bf16[512,256]{1,0:T(8,128)(2,1)S(1)}, bf16[512,256]{1,0:T(8,128)(2,1)S(1)}, u32[]{:S(2)}, u32[]{:S(2)}) collective-permute-start(bf16[512,256]{1,0:T(8,128)(2,1)S(1)} %get-tuple-element.57), channel_id=1, source_target_pairs={{0,64},{16,80},{32,96},{48,112},{64,0},{80,16},{96,32},{112,48},{1... | collective-permute-start | bytes 786440 | tf_op jit(solution)/shard_map/ppermute | solution.py:63
  136.6 13.3 %collective-permute-start.24 = (bf16[512,256]{1,0:T(8,128)(2,1)S(1)}, bf16[512,256]{1,0:T(8,128)(2,1)S(1)}, u32[]{:S(2)}, u32[]{:S(2)}) collective-permute-start(bf16[512,256]{1,0:T(8,128)(2,1)S(1)} %get-tuple-element.58), channel_id=1, source_target_pairs={{0,128},{16,144},{32,160},{48,176},{64,192},{80,208},{96,224},{112... | collective-permute-start | bytes 786440 | tf_op jit(solution)/shard_map/ppermute | solution.py:63
  136.6 45.4 %copy-start.1 = (bf16[64,4096]{1,0:T(8,128)(2,1)S(1)}, bf16[64,4096]{1,0:T(8,128)(2,1)}, u32[]{:S(2)}) copy-start(bf16[64,4096]{1,0:T(8,128)(2,1)} %x_ref.1) | copy-start | bytes 1572868
  136.6 45.4 %copy-start.5 = (bf16[64,4096]{1,0:T(8,128)(2,1)S(1)}, bf16[64,4096]{1,0:T(8,128)(2,1)}, u32[]{:S(2)}) copy-start(bf16[64,4096]{1,0:T(8,128)(2,1)} %og_ref.1) | copy-start | bytes 1572868
  136.6 45.4 %copy-start.7 = (f32[4096]{0:T(1024)S(1)}, f32[4096]{0:T(1024)}, u32[]{:S(2)}) copy-start(f32[4096]{0:T(1024)} %param.10) | copy-start | bytes 49156
  136.6 17.5 %collective-permute-start.25 = (bf16[512,256]{1,0:T(8,128)(2,1)S(1)}, bf16[512,256]{1,0:T(8,128)(2,1)S(1)}, u32[]{:S(2)}, u32[]{:S(2)}) collective-permute-start(bf16[512,256]{1,0:T(8,128)(2,1)S(1)} %get-tuple-element.59), channel_id=1, source_target_pairs={{0,192},{16,208},{32,224},{48,240},{64,128},{80,144},{96,160},{112... | collective-permute-start | bytes 786440 | tf_op jit(solution)/shard_map/ppermute | solution.py:63
  144.7 9.5 %collective-permute-start.33 = (f32[256,256]{1,0:T(8,128)S(1)}, f32[256,256]{1,0:T(8,128)S(1)}, u32[]{:S(2)}, u32[]{:S(2)}) collective-permute-start(f32[256,256]{1,0:T(8,128)S(1)} %convert_add_fusion.a0), channel_id=1, source_target_pairs={{0,64},{16,80},{32,96},{48,112},{64,0},{80,16},{96,32},{112,48},{1... | collective-permute-start | bytes 786440 | tf_op jit(solution)/shard_map/ppermute | solution.py:63
  148.0 10.9 %collective-permute-start.34 = (f32[256,256]{1,0:T(8,128)S(1)}, f32[256,256]{1,0:T(8,128)S(1)}, u32[]{:S(2)}, u32[]{:S(2)}) collective-permute-start(f32[256,256]{1,0:T(8,128)S(1)} %convert_add_fusion.a0), channel_id=1, source_target_pairs={{0,128},{16,144},{32,160},{48,176},{64,192},{80,208},{96,224},{112... | collective-permute-start | bytes 786440 | tf_op jit(solution)/shard_map/ppermute | solution.py:63
  149.9 14.8 %collective-permute-start.35 = (f32[256,256]{1,0:T(8,128)S(1)}, f32[256,256]{1,0:T(8,128)S(1)}, u32[]{:S(2)}, u32[]{:S(2)}) collective-permute-start(f32[256,256]{1,0:T(8,128)S(1)} %convert_add_fusion.a0), channel_id=1, source_target_pairs={{0,192},{16,208},{32,224},{48,240},{64,128},{80,144},{96,160},{112... | collective-permute-start | bytes 786440 | tf_op jit(solution)/shard_map/ppermute | solution.py:63
  150.1 15.7 %collective-permute-start.36 = (f32[256,256]{1,0:T(8,128)S(1)}, f32[256,256]{1,0:T(8,128)S(1)}, u32[]{:S(2)}, u32[]{:S(2)}) collective-permute-start(f32[256,256]{1,0:T(8,128)S(1)} %convert_add_fusion.a0), channel_id=1, source_target_pairs={{0,16},{16,0},{32,48},{48,32},{64,80},{80,64},{96,112},{112,96},{1... | collective-permute-start | bytes 786440 | tf_op jit(solution)/shard_map/ppermute | solution.py:63
  154.2 11.7 %collective-permute-start.20 = (bf16[64,1024]{1,0:T(8,128)(2,1)S(1)}, bf16[64,1024]{1,0:T(8,128)(2,1)S(1)}, u32[]{:S(2)}, u32[]{:S(2)}) collective-permute-start(bf16[64,1024]{1,0:T(8,128)(2,1)S(1)} %get-tuple-element.54), channel_id=1, source_target_pairs={{0,1},{1,0},{2,3},{3,2},{4,5},{5,4},{6,7},{7,6},{8,9},{9,8},{10,11... | collective-permute-start | bytes 393224 | tf_op jit(solution)/shard_map/ppermute | solution.py:63
  154.3 11.7 %collective-permute-start.21 = (bf16[64,1024]{1,0:T(8,128)(2,1)S(1)}, bf16[64,1024]{1,0:T(8,128)(2,1)S(1)}, u32[]{:S(2)}, u32[]{:S(2)}) collective-permute-start(bf16[64,1024]{1,0:T(8,128)(2,1)S(1)} %get-tuple-element.55), channel_id=1, source_target_pairs={{0,4},{1,5},{2,6},{3,7},{4,0},{5,1},{6,2},{7,3},{8,12},{9,13},{10,... | collective-permute-start | bytes 393224 | tf_op jit(solution)/shard_map/ppermute | solution.py:63
  158.9 25.3 %collective-permute-start.37 = (f32[256,256]{1,0:T(8,128)S(1)}, f32[256,256]{1,0:T(8,128)S(1)}, u32[]{:S(2)}, u32[]{:S(2)}) collective-permute-start(f32[256,256]{1,0:T(8,128)S(1)} %collective-permute-done.33.a1), channel_id=1, source_target_pairs={{0,16},{16,0},{32,48},{48,32},{64,80},{80,64},{96,112},{112,96},{1... | collective-permute-start | bytes 786440 | tf_op jit(solution)/shard_map/ppermute | solution.py:63
  164.6 19.6 %collective-permute-start.38 = (f32[256,256]{1,0:T(8,128)S(1)}, f32[256,256]{1,0:T(8,128)S(1)}, u32[]{:S(2)}, u32[]{:S(2)}) collective-permute-start(f32[256,256]{1,0:T(8,128)S(1)} %collective-permute-done.34.a2), channel_id=1, source_target_pairs={{0,16},{16,0},{32,48},{48,32},{64,80},{80,64},{96,112},{112,96},{1... | collective-permute-start | bytes 786440 | tf_op jit(solution)/shard_map/ppermute | solution.py:63
  165.8 7.5 %collective-permute-start.22 = (bf16[64,1024]{1,0:T(8,128)(2,1)S(1)}, bf16[64,1024]{1,0:T(8,128)(2,1)S(1)}, u32[]{:S(2)}, u32[]{:S(2)}) collective-permute-start(bf16[64,1024]{1,0:T(8,128)(2,1)S(1)} %get-tuple-element.56), channel_id=1, source_target_pairs={{0,5},{1,4},{2,7},{3,6},{4,1},{5,0},{6,3},{7,2},{8,13},{9,12},{10,... | collective-permute-start | bytes 393224 | tf_op jit(solution)/shard_map/ppermute | solution.py:63
  165.8 18.4 %collective-permute-start.39 = (f32[256,256]{1,0:T(8,128)S(1)}, f32[256,256]{1,0:T(8,128)S(1)}, u32[]{:S(2)}, u32[]{:S(2)}) collective-permute-start(f32[256,256]{1,0:T(8,128)S(1)} %collective-permute-done.35.a3), channel_id=1, source_target_pairs={{0,16},{16,0},{32,48},{48,32},{64,80},{80,64},{96,112},{112,96},{1... | collective-permute-start | bytes 786440 | tf_op jit(solution)/shard_map/ppermute | solution.py:63
  166.0 22.3 %collective-permute-start.26 = (f32[256,256]{1,0:T(8,128)S(1)}, f32[256,256]{1,0:T(8,128)S(1)}, u32[]{:S(2)}, u32[]{:S(2)}) collective-permute-start(f32[256,256]{1,0:T(8,128)S(1)} %get-tuple-element.60), channel_id=1, source_target_pairs={{0,0},{1,16},{2,2},{3,18},{4,64},{5,80},{6,66},{7,82},{8,76},{9,92... | collective-permute-start | bytes 786440 | tf_op jit(solution)/shard_map/ppermute | solution.py:451
  173.3 14.9 %collective-permute-start.27 = (bf16[256,256]{1,0:T(8,128)(2,1)S(1)}, bf16[256,256]{1,0:T(8,128)(2,1)S(1)}, u32[]{:S(2)}, u32[]{:S(2)}) collective-permute-start(bf16[256,256]{1,0:T(8,128)(2,1)S(1)} %get-tuple-element.61), channel_id=1, source_target_pairs={{0,32},{1,48},{2,34},{3,50},{4,96},{5,112},{6,98},{7,114},{8,108},... | collective-permute-start | bytes 393224 | tf_op jit(solution)/shard_map/ppermute | solution.py:451

commit v3 on v2

--- a/solution.py
+++ b/solution.py
@@ -95,7 +95,7 @@
 HBM = pl.BlockSpec(memory_space=pltpu.HBM)
 
 
-def call(kernel, outs, place, args, scratch=(), spaces=None, limit=40):
+def call(kernel, outs, place, args, scratch=(), spaces=None, limit=40, cost=0):
     return pl.pallas_call(
         kernel,
         out_shape=[jax.ShapeDtypeStruct(s, d) for s, d in outs],
@@ -103,7 +103,7 @@
         out_specs=[VMEM] * len(outs),
         scratch_shapes=list(scratch),
         compiler_params=pltpu.CompilerParams(vmem_limit_bytes=limit << 20),
-        cost_estimate=pl.CostEstimate(flops=0, bytes_accessed=1, transcendentals=0),
+        cost_estimate=pl.CostEstimate(flops=cost, bytes_accessed=1, transcendentals=0),
     )(place, *args)
 
 
@@ -143,18 +143,15 @@
         copy.wait()
 
 
-def gather_rows_kernel(place, m0, m1, m2, m3, gkv, n, gkv_out, sem):
+def gather_rows_kernel(place, m0, m1, m2, m3, k1, k2, gkv, n, k23, gkv_out, sem):
     copy = pltpu.make_async_copy(gkv, gkv_out, sem)
     copy.start()
     for k, ref in enumerate((m0, m1, m2, m3)):
         for j in range(4):
             n[64 * k : 64 * (k + 1), 256 * j : 256 * (j + 1)] = ref[64 * j : 64 * (j + 1), :]
+    k23[0] = k2[...]
+    k23[1] = k1[1]
     copy.wait()
-
-
-def relay_kernel(place, k1, k2, out):
-    out[0] = k2[...]
-    out[1] = k1[1]
 
 
 def gather_weights_kernel(place, m0, m1, m2, m3, k0, k1, k23, after, w):
@@ -168,7 +165,7 @@
     out[...] = (own[...].astype(F32) + got[...].astype(F32)).astype(BF)
 
 
-def weight_lay_kernel(place, w0, w1, a0, a1, a2, a3, out):
+def weight_lay_kernel(place, w0, w1, a0, a1, a2, out):
     outer = place[2]
     for i, ref in enumerate((w0, w1)):
         part = place[11] ^ i
@@ -329,15 +326,14 @@
     k1 = exchange(k1, "tensor", 2)
     g1, g2 = exchange(grad_query, "tensor", 1), exchange(grad_query, "tensor", 4)
     g = (grad_query, g1, g2, exchange(g1, "tensor", 4))
-    n0, gkv = call(
+    n0, k23, gkv = call(
         gather_rows_kernel,
-        [((256, 1024), BF), ((2, 1024, 128), BF)],
-        place,
-        (*inner, grad_keyval),
+        [((256, 1024), BF), ((2, 128, 256), BF), ((2, 1024, 128), BF)],
+        place,
+        (*inner, k1, k2, grad_keyval),
         [pltpu.SemaphoreType.DMA],
-        spaces=[VMEM] * 4 + [HBM],
-    )
-    (k23,) = call(relay_kernel, [((2, 128, 256), BF)], place, (k1, k2))
+        spaces=[VMEM] * 6 + [HBM],
+    )
     k23 = exchange(k23, "tensor", 12)
     n1 = exchange(n0, "tensor", 2)
     n = (n0, n1, exchange(n0, "tensor", 12), exchange(n1, "tensor", 12))
@@ -345,7 +341,7 @@
         gather_weights_kernel,
         [((4, 384, 256), BF)],
         place,
-        (*inner, k0, k1, k23, g1),
+        (*inner, k0, k1, k23, g2),
         spaces=[VMEM] * 7 + [ANY],
 
     )
@@ -361,8 +357,8 @@
         weight_lay_kernel,
         [((4, 128, 1536), BF)],
         place,
-        (w0, exchange(w0, "dp", 4), kv_far, g[3], g2, n[3]),
-        spaces=[VMEM] * 2 + [ANY] * 4,
+        (w0, exchange(w0, "dp", 4), kv_far, g1, n[3]),
+        spaces=[VMEM] * 2 + [ANY] * 3,
     )
     (w,) = call(weight_join_kernel, [((4, 256, 1536), BF)], place, (half, exchange(half, "dp", 1)))
 
@@ -392,7 +388,8 @@
             spaces=[VMEM] * 7 + [ANY],
         )
 
-    both, beta = rows_grad((3, 2), BF, kv[0])
+    kv_got = [exchange(kv[i], "dp", 4 * i) for i in (1, 2, 3)]
+    both, beta = rows_grad((3, 2), BF, kv_got[0])
     both_got = exchange(both, "tensor", 12)
     beta_got = exchange(beta, "tensor", 12)
     q_keep, q_send = call(
@@ -420,7 +417,7 @@
         keyval_ring_kernel,
         [((256, 256), BF)],
         place,
-        (kv[0], *(exchange(kv[i], "dp", 4 * i) for i in (1, 2, 3)), side),
+        (kv[0], *kv_got, side),
         spaces=[VMEM] * 4 + [ANY],
     )
     kv = [lax.ppermute(kv, everywhere, keyval_turn(over)).astype(F32) for over in (0, 1)]
@@ -439,6 +436,7 @@
         place,
         (inputs, out_grad, gain_row, *parts),
         [pltpu.VMEM((64, 4096), F32)],
+        cost=10**11,
     )
 
     q_keep, q_send = call(

time: 189 us -> 179 us (0.947)
  the two profiles are of different devices: /device:TPU:5 before, /device:TPU:17 now
where the time goes in v3:
time: 179 us; the launch traced here: 178 us
  starting transfers between devices  81.1 us (45%)
  waiting for transfers between devices  67.4 us (38%)
  Pallas kernels  24.1 us (13%)
  local copies, waits for them, and re-layouts  4.01 us (2%)
    ppermute x36, starting transfers between devices, exchange(): return lax.ppermute(v, axis, [(i, i ^ flip) for i in range(16)])  60.2 us
    ppermute x36, waiting for transfers between devices, exchange(): return lax.ppermute(v, axis, [(i, i ^ flip) for i in range(16)])  51.3 us
    pallas_call x17, Pallas kernels, call(): pl.pallas_call(kernel, out_shape=[jax.ShapeDtypeStruct(s, d) for s, d in...  24.1 us
    ppermute x2, waiting for transfers between devices, shards(): lax.ppermute(kv, everywhere, keyval_turn(over)).astype(F32)  12.2 us
    ppermute x2, starting transfers between devices, shards(): lax.ppermute(kv, everywhere, keyval_turn(over)).astype(F32)  10.1 us
    ppermute x1, starting transfers between devices, shards(): lax.ppermute(q_keep, everywhere, query_turn(0))  7.65 us
    ppermute x1, waiting for transfers between devices, shards(): lax.ppermute(q_send, everywhere, query_turn(1)).astype(F32)  3.86 us
  transfers between devices with their start and end apart: 40, of which 13 were waited for; matrix products, arithmetic and copies ran while one was open for 0% of the time, Pallas kernels for 8%

profile of v3, /device:TPU:17, one launch (start us, length us, event | category | flops | bytes accessed | tf_op | source)
XLA Modules:
  0.0 178.3 jit_solution(3420205201140276531)
XLA Ops:
  0.7 1.4 dynamic-slice_bitcast_fusion.place.refs_0_
  2.0 3.3 %shard_map.103 = (bf16[512,256]{1,0:T(8,128)(2,1)}, bf16[512,256]{1,0:T(8,128)(2,1)}, bf16[512,256]{1,0:T(8,128)(2,1)}, bf16[512,256]{1,0:T(8,128)(2,1)}, bf16[1...) custom-call(s32[16]{0:T(128)} %dynamic-slice_bitcast_fusion.place.refs_0_, ...), custom_call_target="tpu_custom_call" | custom-call | bytes 1 | tf_op jit(solution)/shard_map/pallas_call | solution.py:99
  5.4 1.7 collective-permute-start.3
  7.1 1.0 collective-permute-start.4
  8.4 1.0 collective-permute-start.1
  9.4 3.0 %collective-permute-start.6 = (bf16[2,128,256]{2,1,0:T(8,128)(2,1)}, bf16[2,128,256]{2,1,0:T(8,128)(2,1)S(1)}, u32[]{:S(2)}, u32[]{:S(2)}) collective-permute-start(bf16[2,128,256]{2,1,0:T(8,128)(2,1)} %get-tuple-element.39), channel_id=1, source_target_pairs={{0,2},{1,3},{2,0},{3,1},{4,6},{5,7},{6,4},{7,5},{8,10},{9,11},{10,... | collective-permute-start | bytes 393224 | tf_op jit(solution)/shard_map/ppermute | solution.py:63
  12.4 8.5 %collective-permute-done.6.k1 = bf16[2,128,256]{2,1,0:T(8,128)(2,1)S(1)} collective-permute-done((bf16[2,128,256]{2,1,0:T(8,128)(2,1)}, bf16[2,128,256]{2,1,0:T(8,128)(2,1)S(1)}, u32[]{:S(2)}, u32[]{:S(2)}) %collective-permute-start.6) | collective-permute-done | bytes 131104 | tf_op jit(solution)/shard_map/ppermute | solution.py:63
  20.8 1.5 collective-permute-done.5.m3
  22.4 0.9 copy-done.1
  23.4 0.8 copy-done.6
  24.2 0.6 shard_map.104
  24.8 2.4 %collective-permute-start.7 = (bf16[2,1024,128]{2,1,0:T(8,128)(2,1)S(1)}, bf16[2,1024,128]{2,1,0:T(8,128)(2,1)S(1)}, u32[]{:S(2)}, u32[]{:S(2)}) collective-permute-start(bf16[2,1024,128]{2,1,0:T(8,128)(2,1)S(1)} %get-tuple-element.41.own), channel_id=1, source_target_pairs={{0,1},{1,0},{2,3},{3,2},{4,5},{5,4},{6,7},{7,6},{8,9},{9,8},{10,11... | collective-permute-start | bytes 1572872 | tf_op jit(solution)/shard_map/ppermute | solution.py:63
  27.2 2.0 %collective-permute-start.9 = (bf16[256,1024]{1,0:T(8,128)(2,1)S(1)}, bf16[256,1024]{1,0:T(8,128)(2,1)S(1)}, u32[]{:S(2)}, u32[]{:S(2)}) collective-permute-start(bf16[256,1024]{1,0:T(8,128)(2,1)S(1)} %get-tuple-element.44.n0), channel_id=1, source_target_pairs={{0,2},{1,3},{2,0},{3,1},{4,6},{5,7},{6,4},{7,5},{8,10},{9,11},{10,... | collective-permute-start | bytes 1572872 | tf_op jit(solution)/shard_map/ppermute | solution.py:63
  29.2 1.5 collective-permute-start.8
  30.6 12.6 %collective-permute-done.8.k23 = bf16[2,128,256]{2,1,0:T(8,128)(2,1)S(1)} collective-permute-done((bf16[2,128,256]{2,1,0:T(8,128)(2,1)S(1)}, bf16[2,128,256]{2,1,0:T(8,128)(2,1)S(1)}, u32[]{:S(2)}, u32[]{:S(2)}) %collective-permute-start.8) | collective-permute-done | bytes 131104 | tf_op jit(solution)/shard_map/ppermute | solution.py:63
  43.2 0.8 copy-done.5
  44.1 0.6 shard_map.105.a0.w0
  44.7 1.3 collective-permute-start.12
  46.4 2.3 %collective-permute-done.7.got = bf16[2,1024,128]{2,1,0:T(8,128)(2,1)S(1)} collective-permute-done((bf16[2,1024,128]{2,1,0:T(8,128)(2,1)S(1)}, bf16[2,1024,128]{2,1,0:T(8,128)(2,1)S(1)}, u32[]{:S(2)}, u32[]{:S(2)}) %collective-permute-start.7) | collective-permute-done | bytes 524320 | tf_op jit(solution)/shard_map/ppermute | solution.py:63
  48.7 0.7 shard_map.106.kv0.refs_5_
  49.4 0.8 collective-permute-start.11
  50.1 10.4 %collective-permute-done.a1.refs_2_.g1 = bf16[1024,256]{1,0:T(8,128)(2,1)S(1)} collective-permute-done((bf16[1024,256]{1,0:T(8,128)(2,1)S(1)}, bf16[1024,256]{1,0:T(8,128)(2,1)S(1)}, u32[]{:S(2)}, u32[]{:S(2)}) %collective-permute-start) | collective-permute-done | bytes 524320 | tf_op jit(solution)/shard_map/ppermute | solution.py:63
  60.7 0.7 shard_map.107.mine.after
  61.4 4.1 %collective-permute-start.14 = (bf16[4,128,1536]{2,1,0:T(8,128)(2,1)S(1)}, bf16[4,128,1536]{2,1,0:T(8,128)(2,1)S(1)}, u32[]{:S(2)}, u32[]{:S(2)}) collective-permute-start(bf16[4,128,1536]{2,1,0:T(8,128)(2,1)S(1)} %shard_map.107.mine.after), channel_id=1, source_target_pairs={{0,16},{16,0},{32,48},{48,32},{64,80},{80,64},{96,112},{112,96},{1... | collective-permute-start | bytes 4718600 | tf_op jit(solution)/shard_map/ppermute | solution.py:63
  65.5 1.9 %shard_map.109 = (f32[1024,256]{1,0:T(8,128)S(1)}, f32[1024,256]{1,0:T(8,128)S(1)}) custom-call(s32[16]{0:T(128)S(1)} %copy-done.4, bf16[256,1024]{1,0:T(8,128)(2,1)S(1)} %get-tuple-element.44.n0, bf16[256,1024]{1,0:T(8,128)(2,1)S(1)} %collective-permute-done.9.a1.n1, bf16[256,1024]{1,0:T(8,128)(2,1)S(1)} %collective-permute-done.10.a2.n2, ...), custom_call_target="tpu_custom_call" | custom-call | bytes 1 | tf_op jit(solution)/shard_map/pallas_call | solution.py:99
  67.5 1.8 %collective-permute-start.2 = (bf16[1024,256]{1,0:T(8,128)(2,1)S(1)}, bf16[1024,256]{1,0:T(8,128)(2,1)S(1)}, u32[]{:S(2)}, u32[]{:S(2)}) collective-permute-start(bf16[1024,256]{1,0:T(8,128)(2,1)S(1)} %collective-permute-done.a1.refs_2_.g1), channel_id=1, source_target_pairs={{0,4},{1,5},{2,6},{3,7},{4,0},{5,1},{6,2},{7,3},{8,12},{9,13},{10,... | collective-permute-start | bytes 1572872 | tf_op jit(solution)/shard_map/ppermute | solution.py:63
  69.4 0.8 collective-permute-done.15.got
  70.2 0.7 shard_map.110
  70.8 1.5 collective-permute-start.16
  72.3 0.7 shard_map.108.refs_7_
  73.1 8.3 %collective-permute-done.2.refs_4_.g3 = bf16[1024,256]{1,0:T(8,128)(2,1)S(1)} collective-permute-done((bf16[1024,256]{1,0:T(8,128)(2,1)S(1)}, bf16[1024,256]{1,0:T(8,128)(2,1)S(1)}, u32[]{:S(2)}, u32[]{:S(2)}) %collective-permute-start.2) | collective-permute-done | bytes 524320 | tf_op jit(solution)/shard_map/ppermute | solution.py:63
  81.3 2.4 %shard_map.111 = (bf16[256,1024]{1,0:T(8,128)(2,1)S(1)}, bf16[256,1024]{1,0:T(8,128)(2,1)S(1)}) custom-call(s32[16]{0:T(128)S(1)} %copy-done.4, bf16[1024,256]{1,0:T(8,128)(2,1)S(1)} %copy-done, bf16[1024,256]{1,0:T(8,128)(2,1)S(1)} %collective-permute-done.a1.refs_2_.g1, bf16[1024,256]{1,0:T(8,128)(2,1)S(1)} %collective-permute-done.1.after.refs_3_.g2, ...), custom_call_target="tpu_custom_call" | custom-call | bytes 1 | tf_op jit(solution)/shard_map/pallas_call | solution.py:99
  83.8 3.0 %shard_map.112 = (f32[2,1024,256]{2,1,0:T(8,128)S(1)}, f32[2,1024,256]{2,1,0:T(8,128)S(1)}) custom-call(s32[16]{0:T(128)S(1)} %copy-done.4, bf16[256,1024]{1,0:T(8,128)(2,1)S(1)} %get-tuple-element.44.n0, bf16[256,1024]{1,0:T(8,128)(2,1)S(1)} %collective-permute-done.9.a1.n1, bf16[256,1024]{1,0:T(8,128)(2,1)S(1)} %collective-permute-done.10.a2.n2, ...), custom_call_target="tpu_custom_call" | custom-call | bytes 1 | tf_op jit(solution)/shard_map/pallas_call | solution.py:99
  86.8 1.0 collective-permute-start.17
  87.9 2.7 %collective-permute-start.29 = (f32[256,256]{1,0:T(8,128)S(1)}, f32[256,256]{1,0:T(8,128)S(1)}, u32[]{:S(2)}, u32[]{:S(2)}) collective-permute-start(f32[256,256]{1,0:T(8,128)S(1)} %get-tuple-element.65), channel_id=1, source_target_pairs={{0,128},{16,144},{32,160},{48,176},{64,192},{80,208},{96,224},{112... | collective-permute-start | bytes 786440 | tf_op jit(solution)/shard_map/ppermute | solution.py:63
  90.6 0.9 collective-permute-start.30
  91.5 1.4 collective-permute-start.18
  92.9 0.7 shard_map.113
  93.6 2.4 %shard_map.114 = (f32[256,1024]{1,0:T(8,128)S(1)}, f32[256,1024]{1,0:T(8,128)S(1)}) custom-call(s32[16]{0:T(128)S(1)} %copy-done.4, bf16[1024,256]{1,0:T(8,128)(2,1)S(1)} %copy-done, bf16[1024,256]{1,0:T(8,128)(2,1)S(1)} %collective-permute-done.a1.refs_2_.g1, bf16[1024,256]{1,0:T(8,128)(2,1)S(1)} %collective-permute-done.1.after.refs_3_.g2, ...), custom_call_target="tpu_custom_call" | custom-call | bytes 1 | tf_op jit(solution)/shard_map/pallas_call | solution.py:99
  96.1 5.2 %collective-permute-done.19 = bf16[256,1024]{1,0:T(8,128)(2,1)S(1)} collective-permute-done((bf16[256,1024]{1,0:T(8,128)(2,1)S(1)}, bf16[256,1024]{1,0:T(8,128)(2,1)S(1)}, u32[]{:S(2)}, u32[]{:S(2)}) %collective-permute-start.19) | collective-permute-done | bytes 524320 | tf_op jit(solution)/shard_map/ppermute | solution.py:63
  101.4 2.8 %collective-permute-start.20 = (bf16[256,1024]{1,0:T(8,128)(2,1)S(1)}, bf16[256,1024]{1,0:T(8,128)(2,1)S(1)}, u32[]{:S(2)}, u32[]{:S(2)}) collective-permute-start(bf16[256,1024]{1,0:T(8,128)(2,1)S(1)} %add_convert_fusion.after), channel_id=1, source_target_pairs={{0,2},{1,3},{2,0},{3,1},{4,6},{5,7},{6,4},{7,5},{8,10},{9,11},{10,... | collective-permute-start | bytes 1572872 | tf_op jit(solution)/shard_map/ppermute | solution.py:63
  104.3 0.6 shard_map.118
  104.9 7.0 %collective-permute-start.32 = (bf16[256,256]{1,0:T(8,128)(2,1)S(1)}, bf16[256,256]{1,0:T(8,128)(2,1)S(1)}, u32[]{:S(2)}, u32[]{:S(2)}) collective-permute-start(bf16[256,256]{1,0:T(8,128)(2,1)S(1)} %shard_map.118), channel_id=1, source_target_pairs={{0,32},{1,33},{2,96},{3,97},{4,36},{5,37},{6,100},{7,101},{8,164},... | collective-permute-start | bytes 393224 | tf_op jit(solution)/shard_map/ppermute | solution.py:423
  111.9 3.1 %collective-permute-start.31 = (bf16[256,256]{1,0:T(8,128)(2,1)S(1)}, bf16[256,256]{1,0:T(8,128)(2,1)S(1)}, u32[]{:S(2)}, u32[]{:S(2)}) collective-permute-start(bf16[256,256]{1,0:T(8,128)(2,1)S(1)} %shard_map.118), channel_id=1, source_target_pairs={{0,0},{1,1},{2,64},{3,65},{4,4},{5,5},{6,68},{7,69},{8,132},{9,133... | collective-permute-start | bytes 393224 | tf_op jit(solution)/shard_map/ppermute | solution.py:423
  115.1 12.2 %collective-permute-done.32 = bf16[256,256]{1,0:T(8,128)(2,1)S(1)} collective-permute-done((bf16[256,256]{1,0:T(8,128)(2,1)S(1)}, bf16[256,256]{1,0:T(8,128)(2,1)S(1)}, u32[]{:S(2)}, u32[]{:S(2)}) %collective-permute-start.32) | collective-permute-done | bytes 131104 | tf_op jit(solution)/shard_map/ppermute | solution.py:423
  127.3 0.4 collective-permute-start.25
  127.7 9.6 %collective-permute-start.26 = (bf16[512,256]{1,0:T(8,128)(2,1)S(1)}, bf16[512,256]{1,0:T(8,128)(2,1)S(1)}, u32[]{:S(2)}, u32[]{:S(2)}) collective-permute-start(bf16[512,256]{1,0:T(8,128)(2,1)S(1)} %get-tuple-element.62), channel_id=1, source_target_pairs={{0,192},{16,208},{32,224},{48,240},{64,128},{80,144},{96,160},{112... | collective-permute-start | bytes 786440 | tf_op jit(solution)/shard_map/ppermute | solution.py:63
  137.4 1.4 collective-permute-start.34
  138.8 2.5 %collective-permute-start.35 = (f32[256,256]{1,0:T(8,128)S(1)}, f32[256,256]{1,0:T(8,128)S(1)}, u32[]{:S(2)}, u32[]{:S(2)}) collective-permute-start(f32[256,256]{1,0:T(8,128)S(1)} %convert_add_fusion.a0), channel_id=1, source_target_pairs={{0,192},{16,208},{32,224},{48,240},{64,128},{80,144},{96,160},{112... | collective-permute-start | bytes 786440 | tf_op jit(solution)/shard_map/ppermute | solution.py:63
  141.3 3.5 %collective-permute-start.36 = (f32[256,256]{1,0:T(8,128)S(1)}, f32[256,256]{1,0:T(8,128)S(1)}, u32[]{:S(2)}, u32[]{:S(2)}) collective-permute-start(f32[256,256]{1,0:T(8,128)S(1)} %convert_add_fusion.a0), channel_id=1, source_target_pairs={{0,16},{16,0},{32,48},{48,32},{64,80},{80,64},{96,112},{112,96},{1... | collective-permute-start | bytes 786440 | tf_op jit(solution)/shard_map/ppermute | solution.py:63
  144.8 0.7 shard_map.115
  145.6 2.8 %collective-permute-start.22 = (bf16[64,1024]{1,0:T(8,128)(2,1)S(1)}, bf16[64,1024]{1,0:T(8,128)(2,1)S(1)}, u32[]{:S(2)}, u32[]{:S(2)}) collective-permute-start(bf16[64,1024]{1,0:T(8,128)(2,1)S(1)} %get-tuple-element.58), channel_id=1, source_target_pairs={{0,4},{1,5},{2,6},{3,7},{4,0},{5,1},{6,2},{7,3},{8,12},{9,13},{10,... | collective-permute-start | bytes 393224 | tf_op jit(solution)/shard_map/ppermute | solution.py:63
  148.4 0.5 collective-permute-done.34.a2
  148.8 4.7 %collective-permute-start.23 = (bf16[64,1024]{1,0:T(8,128)(2,1)S(1)}, bf16[64,1024]{1,0:T(8,128)(2,1)S(1)}, u32[]{:S(2)}, u32[]{:S(2)}) collective-permute-start(bf16[64,1024]{1,0:T(8,128)(2,1)S(1)} %get-tuple-element.59), channel_id=1, source_target_pairs={{0,5},{1,4},{2,7},{3,6},{4,1},{5,0},{6,3},{7,2},{8,13},{9,12},{10,... | collective-permute-start | bytes 393224 | tf_op jit(solution)/shard_map/ppermute | solution.py:63
  153.5 0.7 shard_map.117
  154.2 1.0 collective-permute-done.35.a3
  155.1 1.9 %collective-permute-start.37 = (f32[256,256]{1,0:T(8,128)S(1)}, f32[256,256]{1,0:T(8,128)S(1)}, u32[]{:S(2)}, u32[]{:S(2)}) collective-permute-start(f32[256,256]{1,0:T(8,128)S(1)} %collective-permute-done.33.a1), channel_id=1, source_target_pairs={{0,16},{16,0},{32,48},{48,32},{64,80},{80,64},{96,112},{112,96},{1... | collective-permute-start | bytes 786440 | tf_op jit(solution)/shard_map/ppermute | solution.py:63
  157.2 1.5 collective-permute-start.39
  158.7 7.7 %collective-permute-start.27 = (f32[256,256]{1,0:T(8,128)S(1)}, f32[256,256]{1,0:T(8,128)S(1)}, u32[]{:S(2)}, u32[]{:S(2)}) collective-permute-start(f32[256,256]{1,0:T(8,128)S(1)} %get-tuple-element.63), channel_id=1, source_target_pairs={{0,0},{1,16},{2,2},{3,18},{4,64},{5,80},{6,66},{7,82},{8,76},{9,92... | collective-permute-start | bytes 786440 | tf_op jit(solution)/shard_map/ppermute | solution.py:449
  166.3 3.1 %collective-permute-start.28 = (bf16[256,256]{1,0:T(8,128)(2,1)S(1)}, bf16[256,256]{1,0:T(8,128)(2,1)S(1)}, u32[]{:S(2)}, u32[]{:S(2)}) collective-permute-start(bf16[256,256]{1,0:T(8,128)(2,1)S(1)} %get-tuple-element.64), channel_id=1, source_target_pairs={{0,32},{1,48},{2,34},{3,50},{4,96},{5,112},{6,98},{7,114},{8,108},... | collective-permute-start | bytes 393224 | tf_op jit(solution)/shard_map/ppermute | solution.py:449
  169.4 2.2 %shard_map.116 = f32[64,4096]{1,0:T(8,128)} custom-call(s32[16]{0:T(128)S(1)} %copy-done.4, bf16[64,4096]{1,0:T(8,128)(2,1)S(1)} %copy-done.3, bf16[64,4096]{1,0:T(8,128)(2,1)S(1)} %copy-done.8, f32[1,4096]{1,0:T(1,128)S(1)} %bitcast.4, f32[64,1024]{1,0:T(8,128)S(1)} %get-tuple-element.56.p0.after, bf16[64,1024]{1,0:T(8,128)(2,1)S(1)} %collective-permute-done.21.p1, ...), custom_call_target="tpu_custom_call" | custom-call | flops 99999997952 | bytes 1 | tf_op jit(solution)/shard_map/pallas_call | solution.py:99
  171.6 2.1 %shard_map.119 = f32[2,256,1024]{2,1,0:T(8,128)} custom-call(s32[16]{0:T(128)S(1)} %copy-done.4, f32[256,256]{1,0:T(8,128)S(1)} %convert_add_fusion.a0, f32[256,256]{1,0:T(8,128)S(1)} %collective-permute-done.33.a1, f32[256,256]{1,0:T(8,128)S(1)} %collective-permute-done.34.a2, f32[256,256]{1,0:T(8,128)S(1)} %collective-permute-done.35.a3, ...), custom_call_target="tpu_custom_call" | custom-call | bytes 1 | tf_op jit(solution)/shard_map/pallas_call | solution.py:99
  173.8 3.9 %collective-permute-done.28 = bf16[256,256]{1,0:T(8,128)(2,1)S(1)} collective-permute-done((bf16[256,256]{1,0:T(8,128)(2,1)S(1)}, bf16[256,256]{1,0:T(8,128)(2,1)S(1)}, u32[]{:S(2)}, u32[]{:S(2)}) %collective-permute-start.28) | collective-permute-done | bytes 131104 | tf_op jit(solution)/shard_map/ppermute | solution.py:449
  177.6 0.7 convert_add_fusion.1
  (55 shorter events, 1.6 us)
Async XLA Ops:
  0.6 7.7 %copy-start = (bf16[1024,256]{1,0:T(8,128)(2,1)S(1)}, bf16[1024,256]{1,0:T(8,128)(2,1)}, u32[]{:S(2)}) copy-start(bf16[1024,256]{1,0:T(8,128)(2,1)} %refs_1_.3) | copy-start | bytes 1572868
  0.6 21.8 %copy-start.2 = (bf16[2,1024,128]{2,1,0:T(8,128)(2,1)S(1)}, bf16[2,1024,128]{2,1,0:T(8,128)(2,1)}, u32[]{:S(2)}) copy-start(bf16[2,1024,128]{2,1,0:T(8,128)(2,1)} %gkv.1) | copy-start | bytes 1572868
  2.0 20.4 %copy-start.4 = (s32[16]{0:T(128)S(1)}, s32[16]{0:T(128)}, u32[]{:S(2)}) copy-start(s32[16]{0:T(128)} %dynamic-slice_bitcast_fusion.place.refs_0_) | copy-start | bytes 196
  5.4 15.5 %collective-permute-start.3 = (bf16[512,256]{1,0:T(8,128)(2,1)}, bf16[512,256]{1,0:T(8,128)(2,1)S(1)}, u32[]{:S(2)}, u32[]{:S(2)}) collective-permute-start(bf16[512,256]{1,0:T(8,128)(2,1)} %get-tuple-element.36), channel_id=1, source_target_pairs={{0,1},{1,0},{2,3},{3,2},{4,5},{5,4},{6,7},{7,6},{8,9},{9,8},{10,11... | collective-permute-start | bytes 786440 | tf_op jit(solution)/shard_map/ppermute | solution.py:63
  7.1 13.8 %collective-permute-start.4 = (bf16[512,256]{1,0:T(8,128)(2,1)}, bf16[512,256]{1,0:T(8,128)(2,1)S(1)}, u32[]{:S(2)}, u32[]{:S(2)}) collective-permute-start(bf16[512,256]{1,0:T(8,128)(2,1)} %get-tuple-element.37), channel_id=1, source_target_pairs={{0,4},{1,5},{2,6},{3,7},{4,0},{5,1},{6,2},{7,3},{8,12},{9,13},{10,... | collective-permute-start | bytes 786440 | tf_op jit(solution)/shard_map/ppermute | solution.py:63
  8.1 14.3 %collective-permute-start.5 = (bf16[512,256]{1,0:T(8,128)(2,1)}, bf16[512,256]{1,0:T(8,128)(2,1)S(1)}, u32[]{:S(2)}, u32[]{:S(2)}) collective-permute-start(bf16[512,256]{1,0:T(8,128)(2,1)} %get-tuple-element.38), channel_id=1, source_target_pairs={{0,5},{1,4},{2,7},{3,6},{4,1},{5,0},{6,3},{7,2},{8,13},{9,12},{10,... | collective-permute-start | bytes 786440 | tf_op jit(solution)/shard_map/ppermute | solution.py:63
  8.4 34.9 %collective-permute-start.1 = (bf16[1024,256]{1,0:T(8,128)(2,1)S(1)}, bf16[1024,256]{1,0:T(8,128)(2,1)S(1)}, u32[]{:S(2)}, u32[]{:S(2)}) collective-permute-start(bf16[1024,256]{1,0:T(8,128)(2,1)S(1)} %copy-done), channel_id=1, source_target_pairs={{0,4},{1,5},{2,6},{3,7},{4,0},{5,1},{6,2},{7,3},{8,12},{9,13},{10,... | collective-permute-start | bytes 1572872 | tf_op jit(solution)/shard_map/ppermute | solution.py:63
  9.4 11.5 %collective-permute-start.6 = (bf16[2,128,256]{2,1,0:T(8,128)(2,1)}, bf16[2,128,256]{2,1,0:T(8,128)(2,1)S(1)}, u32[]{:S(2)}, u32[]{:S(2)}) collective-permute-start(bf16[2,128,256]{2,1,0:T(8,128)(2,1)} %get-tuple-element.39), channel_id=1, source_target_pairs={{0,2},{1,3},{2,0},{3,1},{4,6},{5,7},{6,4},{7,5},{8,10},{9,11},{10,... | collective-permute-start | bytes 393224 | tf_op jit(solution)/shard_map/ppermute | solution.py:63
  22.4 1.0 copy-start.1
  23.4 0.8 copy-start.6
  24.8 23.9 %collective-permute-start.7 = (bf16[2,1024,128]{2,1,0:T(8,128)(2,1)S(1)}, bf16[2,1024,128]{2,1,0:T(8,128)(2,1)S(1)}, u32[]{:S(2)}, u32[]{:S(2)}) collective-permute-start(bf16[2,1024,128]{2,1,0:T(8,128)(2,1)S(1)} %get-tuple-element.41.own), channel_id=1, source_target_pairs={{0,1},{1,0},{2,3},{3,2},{4,5},{5,4},{6,7},{7,6},{8,9},{9,8},{10,11... | collective-permute-start | bytes 1572872 | tf_op jit(solution)/shard_map/ppermute | solution.py:63
  27.2 21.5 %collective-permute-start.9 = (bf16[256,1024]{1,0:T(8,128)(2,1)S(1)}, bf16[256,1024]{1,0:T(8,128)(2,1)S(1)}, u32[]{:S(2)}, u32[]{:S(2)}) collective-permute-start(bf16[256,1024]{1,0:T(8,128)(2,1)S(1)} %get-tuple-element.44.n0), channel_id=1, source_target_pairs={{0,2},{1,3},{2,0},{3,1},{4,6},{5,7},{6,4},{7,5},{8,10},{9,11},{10,... | collective-permute-start | bytes 1572872 | tf_op jit(solution)/shard_map/ppermute | solution.py:63
  29.2 19.5 %collective-permute-start.10 = (bf16[256,1024]{1,0:T(8,128)(2,1)S(1)}, bf16[256,1024]{1,0:T(8,128)(2,1)S(1)}, u32[]{:S(2)}, u32[]{:S(2)}) collective-permute-start(bf16[256,1024]{1,0:T(8,128)(2,1)S(1)} %get-tuple-element.44.n0), channel_id=1, source_target_pairs={{0,12},{1,13},{2,14},{3,15},{4,8},{5,9},{6,10},{7,11},{8,4},{9,5},... | collective-permute-start | bytes 1572872 | tf_op jit(solution)/shard_map/ppermute | solution.py:63
  29.2 14.1 %collective-permute-start.8 = (bf16[2,128,256]{2,1,0:T(8,128)(2,1)S(1)}, bf16[2,128,256]{2,1,0:T(8,128)(2,1)S(1)}, u32[]{:S(2)}, u32[]{:S(2)}) collective-permute-start(bf16[2,128,256]{2,1,0:T(8,128)(2,1)S(1)} %get-tuple-element.43), channel_id=1, source_target_pairs={{0,12},{1,13},{2,14},{3,15},{4,8},{5,9},{6,10},{7,11},{8,4},{9,5},... | collective-permute-start | bytes 393224 | tf_op jit(solution)/shard_map/ppermute | solution.py:63
  43.2 0.8 copy-start.5
  44.7 16.0 %collective-permute-start.12 = (bf16[4,384,256]{2,1,0:T(8,128)(2,1)S(1)}, bf16[4,384,256]{2,1,0:T(8,128)(2,1)S(1)}, u32[]{:S(2)}, u32[]{:S(2)}) collective-permute-start(bf16[4,384,256]{2,1,0:T(8,128)(2,1)S(1)} %shard_map.105.a0.w0), channel_id=1, source_target_pairs={{0,64},{16,80},{32,96},{48,112},{64,0},{80,16},{96,32},{112,48},{1... | collective-permute-start | bytes 2359304 | tf_op jit(solution)/shard_map/ppermute | solution.py:63
  46.0 14.6 %collective-permute-start = (bf16[1024,256]{1,0:T(8,128)(2,1)S(1)}, bf16[1024,256]{1,0:T(8,128)(2,1)S(1)}, u32[]{:S(2)}, u32[]{:S(2)}) collective-permute-start(bf16[1024,256]{1,0:T(8,128)(2,1)S(1)} %copy-done), channel_id=1, source_target_pairs={{0,1},{1,0},{2,3},{3,2},{4,5},{5,4},{6,7},{7,6},{8,9},{9,8},{10,11... | collective-permute-start | bytes 1572872 | tf_op jit(solution)/shard_map/ppermute | solution.py:63
  49.4 11.2 %collective-permute-start.11 = (bf16[2,1024,128]{2,1,0:T(8,128)(2,1)S(1)}, bf16[2,1024,128]{2,1,0:T(8,128)(2,1)S(1)}, u32[]{:S(2)}, u32[]{:S(2)}) collective-permute-start(bf16[2,1024,128]{2,1,0:T(8,128)(2,1)S(1)} %shard_map.106.kv0.refs_5_), channel_id=1, source_target_pairs={{0,4},{1,5},{2,6},{3,7},{4,0},{5,1},{6,2},{7,3},{8,12},{9,13},{10,... | collective-permute-start | bytes 1572872 | tf_op jit(solution)/shard_map/ppermute | solution.py:63
  50.1 10.6 %collective-permute-start.13 = (bf16[256,1024]{1,0:T(8,128)(2,1)S(1)}, bf16[256,1024]{1,0:T(8,128)(2,1)S(1)}, u32[]{:S(2)}, u32[]{:S(2)}) collective-permute-start(bf16[256,1024]{1,0:T(8,128)(2,1)S(1)} %collective-permute-done.9.a1.n1), channel_id=1, source_target_pairs={{0,12},{1,13},{2,14},{3,15},{4,8},{5,9},{6,10},{7,11},{8,4},{9,5},... | collective-permute-start | bytes 1572872 | tf_op jit(solution)/shard_map/ppermute | solution.py:63
  61.4 10.9 %collective-permute-start.14 = (bf16[4,128,1536]{2,1,0:T(8,128)(2,1)S(1)}, bf16[4,128,1536]{2,1,0:T(8,128)(2,1)S(1)}, u32[]{:S(2)}, u32[]{:S(2)}) collective-permute-start(bf16[4,128,1536]{2,1,0:T(8,128)(2,1)S(1)} %shard_map.107.mine.after), channel_id=1, source_target_pairs={{0,16},{16,0},{32,48},{48,32},{64,80},{80,64},{96,112},{112,96},{1... | collective-permute-start | bytes 4718600 | tf_op jit(solution)/shard_map/ppermute | solution.py:63
  67.4 2.7 %collective-permute-start.15 = (f32[1024,256]{1,0:T(8,128)S(1)}, f32[1024,256]{1,0:T(8,128)S(1)}, u32[]{:S(2)}, u32[]{:S(2)}) collective-permute-start(f32[1024,256]{1,0:T(8,128)S(1)} %get-tuple-element.46), channel_id=1, source_target_pairs={{0,16},{16,0},{32,48},{48,32},{64,80},{80,64},{96,112},{112,96},{1... | collective-permute-start | bytes 3145736 | tf_op jit(solution)/shard_map/ppermute | solution.py:63
  67.5 13.8 %collective-permute-start.2 = (bf16[1024,256]{1,0:T(8,128)(2,1)S(1)}, bf16[1024,256]{1,0:T(8,128)(2,1)S(1)}, u32[]{:S(2)}, u32[]{:S(2)}) collective-permute-start(bf16[1024,256]{1,0:T(8,128)(2,1)S(1)} %collective-permute-done.a1.refs_2_.g1), channel_id=1, source_target_pairs={{0,4},{1,5},{2,6},{3,7},{4,0},{5,1},{6,2},{7,3},{8,12},{9,13},{10,... | collective-permute-start | bytes 1572872 | tf_op jit(solution)/shard_map/ppermute | solution.py:63
  70.8 10.5 %collective-permute-start.16 = (f32[256,256]{1,0:T(8,128)S(1)}, f32[256,256]{1,0:T(8,128)S(1)}, u32[]{:S(2)}, u32[]{:S(2)}) collective-permute-start(f32[256,256]{1,0:T(8,128)S(1)} %get-tuple-element.47), channel_id=1, source_target_pairs={{0,64},{16,80},{32,96},{48,112},{64,0},{80,16},{96,32},{112,48},{1... | collective-permute-start | bytes 786440 | tf_op jit(solution)/shard_map/ppermute | solution.py:63
  86.8 6.1 %collective-permute-start.17 = (f32[2,1024,256]{2,1,0:T(8,128)S(1)}, f32[2,1024,256]{2,1,0:T(8,128)S(1)}, u32[]{:S(2)}, u32[]{:S(2)}) collective-permute-start(f32[2,1024,256]{2,1,0:T(8,128)S(1)} %get-tuple-element.50), channel_id=1, source_target_pairs={{0,16},{16,0},{32,48},{48,32},{64,80},{80,64},{96,112},{112,96},{1... | collective-permute-start | bytes 6291464 | tf_op jit(solution)/shard_map/ppermute | solution.py:63
  87.8 13.5 %collective-permute-start.19 = (bf16[256,1024]{1,0:T(8,128)(2,1)S(1)}, bf16[256,1024]{1,0:T(8,128)(2,1)S(1)}, u32[]{:S(2)}, u32[]{:S(2)}) collective-permute-start(bf16[256,1024]{1,0:T(8,128)(2,1)S(1)} %get-tuple-element.48.after), channel_id=1, source_target_pairs={{0,12},{1,13},{2,14},{3,15},{4,8},{5,9},{6,10},{7,11},{8,4},{9,5},... | collective-permute-start | bytes 1572872 | tf_op jit(solution)/shard_map/ppermute | solution.py:63
  87.9 16.4 %collective-permute-start.29 = (f32[256,256]{1,0:T(8,128)S(1)}, f32[256,256]{1,0:T(8,128)S(1)}, u32[]{:S(2)}, u32[]{:S(2)}) collective-permute-start(f32[256,256]{1,0:T(8,128)S(1)} %get-tuple-element.65), channel_id=1, source_target_pairs={{0,128},{16,144},{32,160},{48,176},{64,192},{80,208},{96,224},{112... | collective-permute-start | bytes 786440 | tf_op jit(solution)/shard_map/ppermute | solution.py:63
  90.6 13.6 %collective-permute-start.30 = (f32[256,256]{1,0:T(8,128)S(1)}, f32[256,256]{1,0:T(8,128)S(1)}, u32[]{:S(2)}, u32[]{:S(2)}) collective-permute-start(f32[256,256]{1,0:T(8,128)S(1)} %get-tuple-element.66), channel_id=1, source_target_pairs={{0,192},{16,208},{32,224},{48,240},{64,128},{80,144},{96,160},{112... | collective-permute-start | bytes 786440 | tf_op jit(solution)/shard_map/ppermute | solution.py:63
  91.5 45.8 %collective-permute-start.18 = (bf16[256,1024]{1,0:T(8,128)(2,1)S(1)}, bf16[256,1024]{1,0:T(8,128)(2,1)S(1)}, u32[]{:S(2)}, u32[]{:S(2)}) collective-permute-start(bf16[256,1024]{1,0:T(8,128)(2,1)S(1)} %get-tuple-element.54), channel_id=1, source_target_pairs={{0,12},{1,13},{2,14},{3,15},{4,8},{5,9},{6,10},{7,11},{8,4},{9,5},... | collective-permute-start | bytes 1572872 | tf_op jit(solution)/shard_map/ppermute | solution.py:63
  101.4 39.8 %collective-permute-start.20 = (bf16[256,1024]{1,0:T(8,128)(2,1)S(1)}, bf16[256,1024]{1,0:T(8,128)(2,1)S(1)}, u32[]{:S(2)}, u32[]{:S(2)}) collective-permute-start(bf16[256,1024]{1,0:T(8,128)(2,1)S(1)} %add_convert_fusion.after), channel_id=1, source_target_pairs={{0,2},{1,3},{2,0},{3,1},{4,6},{5,7},{6,4},{7,5},{8,10},{9,11},{10,... | collective-permute-start | bytes 1572872 | tf_op jit(solution)/shard_map/ppermute | solution.py:63
  104.9 22.5 %collective-permute-start.32 = (bf16[256,256]{1,0:T(8,128)(2,1)S(1)}, bf16[256,256]{1,0:T(8,128)(2,1)S(1)}, u32[]{:S(2)}, u32[]{:S(2)}) collective-permute-start(bf16[256,256]{1,0:T(8,128)(2,1)S(1)} %shard_map.118), channel_id=1, source_target_pairs={{0,32},{1,33},{2,96},{3,97},{4,36},{5,37},{6,100},{7,101},{8,164},... | collective-permute-start | bytes 393224 | tf_op jit(solution)/shard_map/ppermute | solution.py:423
  111.9 15.9 %collective-permute-start.31 = (bf16[256,256]{1,0:T(8,128)(2,1)S(1)}, bf16[256,256]{1,0:T(8,128)(2,1)S(1)}, u32[]{:S(2)}, u32[]{:S(2)}) collective-permute-start(bf16[256,256]{1,0:T(8,128)(2,1)S(1)} %shard_map.118), channel_id=1, source_target_pairs={{0,0},{1,1},{2,64},{3,65},{4,4},{5,5},{6,68},{7,69},{8,132},{9,133... | collective-permute-start | bytes 393224 | tf_op jit(solution)/shard_map/ppermute | solution.py:423
  115.0 22.4 %collective-permute-start.24 = (bf16[512,256]{1,0:T(8,128)(2,1)S(1)}, bf16[512,256]{1,0:T(8,128)(2,1)S(1)}, u32[]{:S(2)}, u32[]{:S(2)}) collective-permute-start(bf16[512,256]{1,0:T(8,128)(2,1)S(1)} %get-tuple-element.60), channel_id=1, source_target_pairs={{0,64},{16,80},{32,96},{48,112},{64,0},{80,16},{96,32},{112,48},{1... | collective-permute-start | bytes 786440 | tf_op jit(solution)/shard_map/ppermute | solution.py:63
  127.3 11.5 %collective-permute-start.25 = (bf16[512,256]{1,0:T(8,128)(2,1)S(1)}, bf16[512,256]{1,0:T(8,128)(2,1)S(1)}, u32[]{:S(2)}, u32[]{:S(2)}) collective-permute-start(bf16[512,256]{1,0:T(8,128)(2,1)S(1)} %get-tuple-element.61), channel_id=1, source_target_pairs={{0,128},{16,144},{32,160},{48,176},{64,192},{80,208},{96,224},{112... | collective-permute-start | bytes 786440 | tf_op jit(solution)/shard_map/ppermute | solution.py:63
  127.7 41.7 %copy-start.3 = (bf16[64,4096]{1,0:T(8,128)(2,1)S(1)}, bf16[64,4096]{1,0:T(8,128)(2,1)}, u32[]{:S(2)}) copy-start(bf16[64,4096]{1,0:T(8,128)(2,1)} %x_ref.1) | copy-start | bytes 1572868
  127.7 41.7 %copy-start.7 = (f32[4096]{0:T(1024)S(1)}, f32[4096]{0:T(1024)}, u32[]{:S(2)}) copy-start(f32[4096]{0:T(1024)} %param.10) | copy-start | bytes 49156
  127.7 41.7 %copy-start.8 = (bf16[64,4096]{1,0:T(8,128)(2,1)S(1)}, bf16[64,4096]{1,0:T(8,128)(2,1)}, u32[]{:S(2)}) copy-start(bf16[64,4096]{1,0:T(8,128)(2,1)} %og_ref.1) | copy-start | bytes 1572868
  127.7 17.8 %collective-permute-start.26 = (bf16[512,256]{1,0:T(8,128)(2,1)S(1)}, bf16[512,256]{1,0:T(8,128)(2,1)S(1)}, u32[]{:S(2)}, u32[]{:S(2)}) collective-permute-start(bf16[512,256]{1,0:T(8,128)(2,1)S(1)} %get-tuple-element.62), channel_id=1, source_target_pairs={{0,192},{16,208},{32,224},{48,240},{64,128},{80,144},{96,160},{112... | collective-permute-start | bytes 786440 | tf_op jit(solution)/shard_map/ppermute | solution.py:63
  137.3 8.3 %collective-permute-start.33 = (f32[256,256]{1,0:T(8,128)S(1)}, f32[256,256]{1,0:T(8,128)S(1)}, u32[]{:S(2)}, u32[]{:S(2)}) collective-permute-start(f32[256,256]{1,0:T(8,128)S(1)} %convert_add_fusion.a0), channel_id=1, source_target_pairs={{0,64},{16,80},{32,96},{48,112},{64,0},{80,16},{96,32},{112,48},{1... | collective-permute-start | bytes 786440 | tf_op jit(solution)/shard_map/ppermute | solution.py:63
  137.4 11.4 %collective-permute-start.34 = (f32[256,256]{1,0:T(8,128)S(1)}, f32[256,256]{1,0:T(8,128)S(1)}, u32[]{:S(2)}, u32[]{:S(2)}) collective-permute-start(f32[256,256]{1,0:T(8,128)S(1)} %convert_add_fusion.a0), channel_id=1, source_target_pairs={{0,128},{16,144},{32,160},{48,176},{64,192},{80,208},{96,224},{112... | collective-permute-start | bytes 786440 | tf_op jit(solution)/shard_map/ppermute | solution.py:63
  138.8 16.3 %collective-permute-start.35 = (f32[256,256]{1,0:T(8,128)S(1)}, f32[256,256]{1,0:T(8,128)S(1)}, u32[]{:S(2)}, u32[]{:S(2)}) collective-permute-start(f32[256,256]{1,0:T(8,128)S(1)} %convert_add_fusion.a0), channel_id=1, source_target_pairs={{0,192},{16,208},{32,224},{48,240},{64,128},{80,144},{96,160},{112... | collective-permute-start | bytes 786440 | tf_op jit(solution)/shard_map/ppermute | solution.py:63
  141.3 15.8 %collective-permute-start.36 = (f32[256,256]{1,0:T(8,128)S(1)}, f32[256,256]{1,0:T(8,128)S(1)}, u32[]{:S(2)}, u32[]{:S(2)}) collective-permute-start(f32[256,256]{1,0:T(8,128)S(1)} %convert_add_fusion.a0), channel_id=1, source_target_pairs={{0,16},{16,0},{32,48},{48,32},{64,80},{80,64},{96,112},{112,96},{1... | collective-permute-start | bytes 786440 | tf_op jit(solution)/shard_map/ppermute | solution.py:63
  145.5 11.7 %collective-permute-start.21 = (bf16[64,1024]{1,0:T(8,128)(2,1)S(1)}, bf16[64,1024]{1,0:T(8,128)(2,1)S(1)}, u32[]{:S(2)}, u32[]{:S(2)}) collective-permute-start(bf16[64,1024]{1,0:T(8,128)(2,1)S(1)} %get-tuple-element.57), channel_id=1, source_target_pairs={{0,1},{1,0},{2,3},{3,2},{4,5},{5,4},{6,7},{7,6},{8,9},{9,8},{10,11... | collective-permute-start | bytes 393224 | tf_op jit(solution)/shard_map/ppermute | solution.py:63
  145.6 13.0 %collective-permute-start.22 = (bf16[64,1024]{1,0:T(8,128)(2,1)S(1)}, bf16[64,1024]{1,0:T(8,128)(2,1)S(1)}, u32[]{:S(2)}, u32[]{:S(2)}) collective-permute-start(bf16[64,1024]{1,0:T(8,128)(2,1)S(1)} %get-tuple-element.58), channel_id=1, source_target_pairs={{0,4},{1,5},{2,6},{3,7},{4,0},{5,1},{6,2},{7,3},{8,12},{9,13},{10,... | collective-permute-start | bytes 393224 | tf_op jit(solution)/shard_map/ppermute | solution.py:63
  148.8 17.5 %collective-permute-start.23 = (bf16[64,1024]{1,0:T(8,128)(2,1)S(1)}, bf16[64,1024]{1,0:T(8,128)(2,1)S(1)}, u32[]{:S(2)}, u32[]{:S(2)}) collective-permute-start(bf16[64,1024]{1,0:T(8,128)(2,1)S(1)} %get-tuple-element.59), channel_id=1, source_target_pairs={{0,5},{1,4},{2,7},{3,6},{4,1},{5,0},{6,3},{7,2},{8,13},{9,12},{10,... | collective-permute-start | bytes 393224 | tf_op jit(solution)/shard_map/ppermute | solution.py:63
  155.1 16.5 %collective-permute-start.37 = (f32[256,256]{1,0:T(8,128)S(1)}, f32[256,256]{1,0:T(8,128)S(1)}, u32[]{:S(2)}, u32[]{:S(2)}) collective-permute-start(f32[256,256]{1,0:T(8,128)S(1)} %collective-permute-done.33.a1), channel_id=1, source_target_pairs={{0,16},{16,0},{32,48},{48,32},{64,80},{80,64},{96,112},{112,96},{1... | collective-permute-start | bytes 786440 | tf_op jit(solution)/shard_map/ppermute | solution.py:63
  157.0 14.6 %collective-permute-start.38 = (f32[256,256]{1,0:T(8,128)S(1)}, f32[256,256]{1,0:T(8,128)S(1)}, u32[]{:S(2)}, u32[]{:S(2)}) collective-permute-start(f32[256,256]{1,0:T(8,128)S(1)} %collective-permute-done.34.a2), channel_id=1, source_target_pairs={{0,16},{16,0},{32,48},{48,32},{64,80},{80,64},{96,112},{112,96},{1... | collective-permute-start | bytes 786440 | tf_op jit(solution)/shard_map/ppermute | solution.py:63
  157.2 14.5 %collective-permute-start.39 = (f32[256,256]{1,0:T(8,128)S(1)}, f32[256,256]{1,0:T(8,128)S(1)}, u32[]{:S(2)}, u32[]{:S(2)}) collective-permute-start(f32[256,256]{1,0:T(8,128)S(1)} %collective-permute-done.35.a3), channel_id=1, source_target_pairs={{0,16},{16,0},{32,48},{48,32},{64,80},{80,64},{96,112},{112,96},{1... | collective-permute-start | bytes 786440 | tf_op jit(solution)/shard_map/ppermute | solution.py:63
  158.7 19.0 %collective-permute-start.27 = (f32[256,256]{1,0:T(8,128)S(1)}, f32[256,256]{1,0:T(8,128)S(1)}, u32[]{:S(2)}, u32[]{:S(2)}) collective-permute-start(f32[256,256]{1,0:T(8,128)S(1)} %get-tuple-element.63), channel_id=1, source_target_pairs={{0,0},{1,16},{2,2},{3,18},{4,64},{5,80},{6,66},{7,82},{8,76},{9,92... | collective-permute-start | bytes 786440 | tf_op jit(solution)/shard_map/ppermute | solution.py:449
  166.3 11.3 %collective-permute-start.28 = (bf16[256,256]{1,0:T(8,128)(2,1)S(1)}, bf16[256,256]{1,0:T(8,128)(2,1)S(1)}, u32[]{:S(2)}, u32[]{:S(2)}) collective-permute-start(bf16[256,256]{1,0:T(8,128)(2,1)S(1)} %get-tuple-element.64), channel_id=1, source_target_pairs={{0,32},{1,48},{2,34},{3,50},{4,96},{5,112},{6,98},{7,114},{8,108},... | collective-permute-start | bytes 393224 | tf_op jit(solution)/shard_map/ppermute | solution.py:449

commit v4 on v3

--- a/solution.py
+++ b/solution.py
@@ -89,13 +89,21 @@
     return pairs
 
 
+COST = {
+    "owner_sum_kernel": 4 * 10**9,
+    "input_grad_kernel": 6 * 10**9,
+    "keyval_lay_kernel": 6 * 10**9,
+    "side_kernel": 20 * 10**9,
+    "rows1": 4 * 10**9,
+}
+
 SMEM = pl.BlockSpec(memory_space=pltpu.SMEM)
 VMEM = pl.BlockSpec(memory_space=pltpu.VMEM)
 ANY = pl.BlockSpec(memory_space=pl.ANY)
 HBM = pl.BlockSpec(memory_space=pltpu.HBM)
 
 
-def call(kernel, outs, place, args, scratch=(), spaces=None, limit=40, cost=0):
+def call(kernel, outs, place, args, scratch=(), spaces=None, limit=40, cost=None):
     return pl.pallas_call(
         kernel,
         out_shape=[jax.ShapeDtypeStruct(s, d) for s, d in outs],
@@ -103,7 +111,9 @@
         out_specs=[VMEM] * len(outs),
         scratch_shapes=list(scratch),
         compiler_params=pltpu.CompilerParams(vmem_limit_bytes=limit << 20),
-        cost_estimate=pl.CostEstimate(flops=cost, bytes_accessed=1, transcendentals=0),
+        cost_estimate=pl.CostEstimate(
+            flops=COST.get(kernel.__name__, 0) if cost is None else cost, bytes_accessed=1, transcendentals=0
+        ),
     )(place, *args)
 
 
@@ -183,9 +193,9 @@
             out[d, block(c ^ half, 128), :] = ref[d]
 
 
-def rows_grad_kernel(which, place, g0, g1, g2, g3, kv0, kv1, w, after, o0, o1, scr):
+def rows_grad_kernel(which, place, g0, g1, g2, g3, kv0, kv1, w, after, out, scr):
     t = place[1]
-    for j, out in zip(which, (o0, o1)):
+    for at, j in enumerate(which):
         for k in range(4):
             rows = block(t ^ (OUTER[j] ^ INNER[k]), 64)
             here = slice(64 * k, 64 * (k + 1))
@@ -193,12 +203,16 @@
                 scr[here, 256 * n : 256 * (n + 1)] = g[rows, :]
             for a, kv in enumerate((kv0, kv1)):
                 for p in range(2):
-                    at = 1024 + 128 * (2 * a + p)
-                    scr[here, at : at + 128] = kv[p, rows, :]
+                    lane = 1024 + 128 * (2 * a + p)
+                    scr[here, lane : lane + 128] = kv[p, rows, :]
         left = scr[...]
         for d in range(4):
             value = lax.dot_general(left, w[d], (((1,), (1,)), ((), ())), preferred_element_type=F32)
-            out[:, 256 * d : 256 * (d + 1)] = value.astype(out.dtype)
+            out[256 * at : 256 * (at + 1), 256 * d : 256 * (d + 1)] = value.astype(out.dtype)
+
+
+def side_kernel(place, mine, got, after, out):
+    out[...] = (mine[:256, :] + got[:256, :].astype(F32)).astype(BF)
 
 
 def rows_product(ns, d, right):
@@ -260,7 +274,7 @@
         out[...] = (keep[a, rows, :] + got[a, rows, :]).astype(out.dtype)
 
 
-def query_ring_kernel(place, own, r1, r2, r3, after, q_keep, q_send):
+def query_ring_kernel(place, own, r1, r2, r3, q_keep, q_send):
     h = place[8]
 
     def total(rows):
@@ -270,23 +284,28 @@
     q_send[...] = total(block(h ^ 1, 256)).astype(BF)
 
 
-def keyval_ring_kernel(place, own, r1, r2, r3, after, out):
+def keyval_ring_kernel(place, own, r1, r2, r3, out):
     out[...] = (own[...] + r1[...] + r2[...] + r3[...]).astype(BF)
 
 
-def keyval_lay_kernel(place, a0, a1, a2, a3, b0, b1, b2, b3, out):
+def stack_kernel(place, a0, a1, a2, a3, after, later, out):
+    for i, ref in enumerate((a0, a1, a2, a3)):
+        out[i] = ref[...]
+
+
+def keyval_lay_kernel(place, near, far, out):
     c, head = place[4], place[12]
-    for half, refs in ((0, (a0, a1, a2, a3)), (1, (b0, b1, b2, b3))):
-        for i, ref in enumerate(refs):
+    for half, ref in ((0, near), (1, far)):
+        for i in range(4):
             for a in range(2):
                 lanes = block(head ^ (HEAD_STEP[i] ^ (2 * a)), 128)
-                out[c ^ half, :, lanes] = ref[:, 128 * a : 128 * (a + 1)]
-
-
-def owner_sum_kernel(place, own, beta, side, o0, o1, o2, o3):
+                out[c ^ half, :, lanes] = ref[i, :, 128 * a : 128 * (a + 1)]
+
+
+def owner_sum_kernel(place, mine, far, side, o0, o1, o2, o3):
     for k, out in enumerate((o0, o1, o2, o3)):
-        rows = slice(64 * k, 64 * (k + 1))
-        out[...] = (own[rows, :] + beta[rows, :].astype(F32) + side[rows, :].astype(F32)).astype(out.dtype)
+        rows, own = slice(64 * k, 64 * (k + 1)), slice(256 + 64 * k, 256 + 64 * (k + 1))
+        out[...] = (mine[own, :] + far[own, :].astype(F32) + side[rows, :].astype(F32)).astype(out.dtype)
 
 
 def input_grad_kernel(place, x_ref, og_ref, gain_ref, p0, p1, p2, p3, out, scaled):
@@ -381,22 +400,22 @@
     def rows_grad(which, kind, after):
         return call(
             lambda *refs: rows_grad_kernel(which, *refs),
-            [((256, 1024), kind)] * 2,
+            [((512, 1024), kind)],
             place,
             (*g, kv_own, kv_far, w, after),
             [pltpu.VMEM((256, 1536), BF)],
             spaces=[VMEM] * 7 + [ANY],
+            cost=COST.get("rows" + str(which[0]), 0),
         )
 
     kv_got = [exchange(kv[i], "dp", 4 * i) for i in (1, 2, 3)]
-    both, beta = rows_grad((3, 2), BF, kv_got[0])
-    both_got = exchange(both, "tensor", 12)
-    beta_got = exchange(beta, "tensor", 12)
+    (far,) = rows_grad((3, 2), BF, kv_got[0])
+    far_got = exchange(far, "tensor", 12)
     q_keep, q_send = call(
         query_grad_kernel,
         [((2, 1024, 256), F32)] * 2,
         place,
-        (*n, *g, both),
+        (*n, *g, far),
         [pltpu.VMEM((1024, 1024), BF)],
         spaces=[VMEM] * 8 + [ANY],
     )
@@ -408,47 +427,45 @@
         (q_keep, q_got, kv[0]),
         spaces=[VMEM] * 2 + [ANY],
     )
-    side, own = rows_grad((1, 0), F32, q[0])
-    side = (side + both_got.astype(F32)).astype(BF)
-    side_got = exchange(side, "tensor", 2)
-
-    everywhere = ("dp", "tensor")
-    (kv,) = call(
+    (mine,) = rows_grad((1, 0), F32, q[0])
+    (kv_ring,) = call(
         keyval_ring_kernel,
         [((256, 256), BF)],
         place,
-        (kv[0], *kv_got, side),
-        spaces=[VMEM] * 4 + [ANY],
-    )
-    kv = [lax.ppermute(kv, everywhere, keyval_turn(over)).astype(F32) for over in (0, 1)]
+        (kv[0], *kv_got),
+    )
+    (side,) = call(side_kernel, [((256, 1024), BF)], place, (mine, far_got, kv_ring), spaces=[VMEM] * 2 + [ANY])
+    side_got = exchange(side, "tensor", 2)
+
+    everywhere = ("dp", "tensor")
+    kv = [lax.ppermute(kv_ring, everywhere, keyval_turn(over)).astype(F32) for over in (0, 1)]
     kv = kv[0] + kv[1]
     near = [kv] + [exchange(kv, "dp", 4 * i) for i in (1, 2, 3)]
-    far = [exchange(v, "dp", 1) for v in near]
-    (keyval_weight_grad,) = call(keyval_lay_kernel, [((2, 256, 1024), F32)], place, (*near, *far))
-
     parts = call(
-        owner_sum_kernel, [((64, 1024), F32)] + [((64, 1024), BF)] * 3, place, (own, beta_got, side_got)
-    )
-    parts = [parts[0]] + [exchange(parts[k], "tensor", INNER[k]) for k in (1, 2, 3)]
+        owner_sum_kernel, [((64, 1024), F32)] + [((64, 1024), BF)] * 3, place, (mine, far_got, side_got)
+    )
+    pieces = [parts[0]] + [exchange(parts[k], "tensor", INNER[k]) for k in (1, 2, 3)]
     (input_grad,) = call(
         input_grad_kernel,
         [((64, 4096), F32)],
         place,
-        (inputs, out_grad, gain_row, *parts),
+        (inputs, out_grad, gain_row, *pieces),
         [pltpu.VMEM((64, 4096), F32)],
-        cost=10**11,
     )
 
     q_keep, q_send = call(
         query_ring_kernel,
         [((256, 256), F32), ((256, 256), BF)],
         place,
-        (q[0], *(exchange(q[i], "dp", 4 * i) for i in (1, 2, 3)), parts[0]),
-        spaces=[VMEM] * 4 + [ANY],
+        (q[0], *(exchange(q[i], "dp", 4 * i) for i in (1, 2, 3))),
     )
     query_weight_grad = lax.ppermute(q_keep, everywhere, query_turn(0)) + lax.ppermute(
         q_send, everywhere, query_turn(1)
     ).astype(F32)
+    (near,) = call(stack_kernel, [((4, 256, 256), F32)], place, (*near, q_keep, q_keep), spaces=[VMEM] * 4 + [ANY] * 2)
+    (keyval_weight_grad,) = call(
+        keyval_lay_kernel, [((2, 256, 1024), F32)], place, (near, exchange(near, "dp", 1))
+    )
     return (input_grad, query_weight_grad, keyval_weight_grad)
 
 

time: 179 us -> 174 us (0.972)
  the two profiles are of different devices: /device:TPU:17 before, /device:TPU:160 now
where the time goes in v4:
time: 174 us
  waiting for transfers between devices  72.4 us (42%)
  starting transfers between devices  70.4 us (40%)
  Pallas kernels  25.3 us (15%)
  local copies, waits for them, and re-layouts  4.01 us (2%)
    ppermute x32, waiting for transfers between devices, exchange(): return lax.ppermute(v, axis, [(i, i ^ flip) for i in range(16)])  72.4 us
    ppermute x32, starting transfers between devices, exchange(): return lax.ppermute(v, axis, [(i, i ^ flip) for i in range(16)])  62.1 us
    pallas_call x19, Pallas kernels, call(): pl.pallas_call(kernel, out_shape=[jax.ShapeDtypeStruct(s, d) for s, d in...  25.3 us
    ppermute x1, starting transfers between devices, shards(): lax.ppermute(q_keep, everywhere, query_turn(0))  5.27 us
  transfers between devices with their start and end apart: 36, of which 16 were waited for; matrix products, arithmetic and copies ran while one was open for 0% of the time, Pallas kernels for 8%

profile of v4, /device:TPU:160, one launch (start us, length us, event | category | flops | bytes accessed | tf_op | source)
XLA Modules:
  0.0 173.9 jit_solution(15129044483734901409)
XLA Ops:
  0.7 1.4 dynamic-slice_bitcast_fusion.place.refs_0_
  2.0 3.3 %shard_map.103 = (bf16[512,256]{1,0:T(8,128)(2,1)}, bf16[512,256]{1,0:T(8,128)(2,1)}, bf16[512,256]{1,0:T(8,128)(2,1)}, bf16[512,256]{1,0:T(8,128)(2,1)}, bf16[1...) custom-call(s32[16]{0:T(128)} %dynamic-slice_bitcast_fusion.place.refs_0_, ...), custom_call_target="tpu_custom_call" | custom-call | bytes 1 | tf_op jit(solution)/shard_map/pallas_call | solution.py:107
  5.4 1.1 collective-permute-start.3
  6.5 1.6 collective-permute-start.4
  8.0 0.9 collective-permute-start.5
  8.9 1.6 collective-permute-start.1
  10.5 1.5 collective-permute-start.6
  12.0 10.6 %collective-permute-done.6.k1 = bf16[2,128,256]{2,1,0:T(8,128)(2,1)S(1)} collective-permute-done((bf16[2,128,256]{2,1,0:T(8,128)(2,1)}, bf16[2,128,256]{2,1,0:T(8,128)(2,1)S(1)}, u32[]{:S(2)}, u32[]{:S(2)}) %collective-permute-start.6) | collective-permute-done | bytes 131104 | tf_op jit(solution)/shard_map/ppermute | solution.py:63
  22.7 0.9 copy-done.1
  23.6 0.8 copy-done.6
  24.5 0.6 shard_map.104
  25.1 1.7 collective-permute-start.7
  26.8 0.9 collective-permute-start.9
  27.7 3.0 %collective-permute-start.10 = (bf16[256,1024]{1,0:T(8,128)(2,1)S(1)}, bf16[256,1024]{1,0:T(8,128)(2,1)S(1)}, u32[]{:S(2)}, u32[]{:S(2)}) collective-permute-start(bf16[256,1024]{1,0:T(8,128)(2,1)S(1)} %get-tuple-element.40.n0), channel_id=1, source_target_pairs={{0,12},{1,13},{2,14},{3,15},{4,8},{5,9},{6,10},{7,11},{8,4},{9,5},... | collective-permute-start | bytes 1572872 | tf_op jit(solution)/shard_map/ppermute | solution.py:63
  30.9 13.1 %collective-permute-done.8.k23 = bf16[2,128,256]{2,1,0:T(8,128)(2,1)S(1)} collective-permute-done((bf16[2,128,256]{2,1,0:T(8,128)(2,1)S(1)}, bf16[2,128,256]{2,1,0:T(8,128)(2,1)S(1)}, u32[]{:S(2)}, u32[]{:S(2)}) %collective-permute-start.8) | collective-permute-done | bytes 131104 | tf_op jit(solution)/shard_map/ppermute | solution.py:63
  44.0 0.8 copy-done.5
  45.4 1.6 collective-permute-start.12
  47.0 1.5 collective-permute-start
  48.5 1.0 collective-permute-done.7.got
  49.5 2.2 %collective-permute-done.9.a1.n1 = bf16[256,1024]{1,0:T(8,128)(2,1)S(1)} collective-permute-done((bf16[256,1024]{1,0:T(8,128)(2,1)S(1)}, bf16[256,1024]{1,0:T(8,128)(2,1)S(1)}, u32[]{:S(2)}, u32[]{:S(2)}) %collective-permute-start.9) | collective-permute-done | bytes 524320 | tf_op jit(solution)/shard_map/ppermute | solution.py:63
  51.8 0.7 shard_map.106.kv0.refs_5_
  52.4 1.7 collective-permute-start.11
  54.1 2.2 %collective-permute-start.13 = (bf16[256,1024]{1,0:T(8,128)(2,1)S(1)}, bf16[256,1024]{1,0:T(8,128)(2,1)S(1)}, u32[]{:S(2)}, u32[]{:S(2)}) collective-permute-start(bf16[256,1024]{1,0:T(8,128)(2,1)S(1)} %collective-permute-done.9.a1.n1), channel_id=1, source_target_pairs={{0,12},{1,13},{2,14},{3,15},{4,8},{5,9},{6,10},{7,11},{8,4},{9,5},... | collective-permute-start | bytes 1572872 | tf_op jit(solution)/shard_map/ppermute | solution.py:63
  56.3 4.2 %collective-permute-done.a1.refs_2_.g1 = bf16[1024,256]{1,0:T(8,128)(2,1)S(1)} collective-permute-done((bf16[1024,256]{1,0:T(8,128)(2,1)S(1)}, bf16[1024,256]{1,0:T(8,128)(2,1)S(1)}, u32[]{:S(2)}, u32[]{:S(2)}) %collective-permute-start) | collective-permute-done | bytes 524320 | tf_op jit(solution)/shard_map/ppermute | solution.py:63
  60.5 1.8 %collective-permute-done.11.a0.kv1.refs_6_ = bf16[2,1024,128]{2,1,0:T(8,128)(2,1)S(1)} collective-permute-done((bf16[2,1024,128]{2,1,0:T(8,128)(2,1)S(1)}, bf16[2,1024,128]{2,1,0:T(8,128)(2,1)S(1)}, u32[]{:S(2)}, u32[]{:S(2)}) %collective-permute-start.11) | collective-permute-done | bytes 524320 | tf_op jit(solution)/shard_map/ppermute | solution.py:63
  62.5 2.4 %collective-permute-done.13.a2.n3 = bf16[256,1024]{1,0:T(8,128)(2,1)S(1)} collective-permute-done((bf16[256,1024]{1,0:T(8,128)(2,1)S(1)}, bf16[256,1024]{1,0:T(8,128)(2,1)S(1)}, u32[]{:S(2)}, u32[]{:S(2)}) %collective-permute-start.13) | collective-permute-done | bytes 524320 | tf_op jit(solution)/shard_map/ppermute | solution.py:63
  64.8 0.7 shard_map.107.mine.after
  65.6 1.9 %shard_map.109 = (f32[1024,256]{1,0:T(8,128)S(1)}, f32[1024,256]{1,0:T(8,128)S(1)}) custom-call(s32[16]{0:T(128)S(1)} %copy-done.4, bf16[256,1024]{1,0:T(8,128)(2,1)S(1)} %get-tuple-element.40.n0, bf16[256,1024]{1,0:T(8,128)(2,1)S(1)} %collective-permute-done.9.a1.n1, bf16[256,1024]{1,0:T(8,128)(2,1)S(1)} %collective-permute-done.10.a2.n2, ...), custom_call_target="tpu_custom_call" | custom-call | bytes 1 | tf_op jit(solution)/shard_map/pallas_call | solution.py:107
  68.2 2.4 %collective-permute-done.15.got = f32[1024,256]{1,0:T(8,128)S(1)} collective-permute-done((f32[1024,256]{1,0:T(8,128)S(1)}, f32[1024,256]{1,0:T(8,128)S(1)}, u32[]{:S(2)}, u32[]{:S(2)}) %collective-permute-start.15) | collective-permute-done | bytes 1048608 | tf_op jit(solution)/shard_map/ppermute | solution.py:63
  70.5 0.7 shard_map.110
  71.2 1.8 %collective-permute-start.16 = (f32[256,256]{1,0:T(8,128)S(1)}, f32[256,256]{1,0:T(8,128)S(1)}, u32[]{:S(2)}, u32[]{:S(2)}) collective-permute-start(f32[256,256]{1,0:T(8,128)S(1)} %get-tuple-element.43), channel_id=1, source_target_pairs={{0,64},{16,80},{32,96},{48,112},{64,0},{80,16},{96,32},{112,48},{1... | collective-permute-start | bytes 786440 | tf_op jit(solution)/shard_map/ppermute | solution.py:63
  72.9 0.7 shard_map.108.refs_7_
  73.7 8.4 %collective-permute-done.2.refs_4_.g3 = bf16[1024,256]{1,0:T(8,128)(2,1)S(1)} collective-permute-done((bf16[1024,256]{1,0:T(8,128)(2,1)S(1)}, bf16[1024,256]{1,0:T(8,128)(2,1)S(1)}, u32[]{:S(2)}, u32[]{:S(2)}) %collective-permute-start.2) | collective-permute-done | bytes 524320 | tf_op jit(solution)/shard_map/ppermute | solution.py:63
  82.1 2.4 %shard_map.111.after = bf16[512,1024]{1,0:T(8,128)(2,1)S(1)} custom-call(s32[16]{0:T(128)S(1)} %copy-done.4, bf16[1024,256]{1,0:T(8,128)(2,1)S(1)} %copy-done, bf16[1024,256]{1,0:T(8,128)(2,1)S(1)} %collective-permute-done.a1.refs_2_.g1, bf16[1024,256]{1,0:T(8,128)(2,1)S(1)} %collective-permute-done.1.after.refs_3_.g2, ...), custom_call_target="tpu_custom_call" | custom-call | bytes 1 | tf_op jit(solution)/shard_map/pallas_call | solution.py:107
  84.5 3.0 %shard_map.112 = (f32[2,1024,256]{2,1,0:T(8,128)S(1)}, f32[2,1024,256]{2,1,0:T(8,128)S(1)}) custom-call(s32[16]{0:T(128)S(1)} %copy-done.4, bf16[256,1024]{1,0:T(8,128)(2,1)S(1)} %get-tuple-element.40.n0, bf16[256,1024]{1,0:T(8,128)(2,1)S(1)} %collective-permute-done.9.a1.n1, bf16[256,1024]{1,0:T(8,128)(2,1)S(1)} %collective-permute-done.10.a2.n2, ...), custom_call_target="tpu_custom_call" | custom-call | bytes 1 | tf_op jit(solution)/shard_map/pallas_call | solution.py:107
  87.6 2.3 %collective-permute-start.18 = (bf16[512,1024]{1,0:T(8,128)(2,1)S(1)}, bf16[512,1024]{1,0:T(8,128)(2,1)S(1)}, u32[]{:S(2)}, u32[]{:S(2)}) collective-permute-start(bf16[512,1024]{1,0:T(8,128)(2,1)S(1)} %shard_map.111.after), channel_id=1, source_target_pairs={{0,12},{1,13},{2,14},{3,15},{4,8},{5,9},{6,10},{7,11},{8,4},{9,5},... | collective-permute-start | bytes 3145736 | tf_op jit(solution)/shard_map/ppermute | solution.py:63
  89.9 3.0 %collective-permute-start.19 = (f32[256,256]{1,0:T(8,128)S(1)}, f32[256,256]{1,0:T(8,128)S(1)}, u32[]{:S(2)}, u32[]{:S(2)}) collective-permute-start(f32[256,256]{1,0:T(8,128)S(1)} %get-tuple-element.48), channel_id=1, source_target_pairs={{0,128},{16,144},{32,160},{48,176},{64,192},{80,208},{96,224},{112... | collective-permute-start | bytes 786440 | tf_op jit(solution)/shard_map/ppermute | solution.py:63
  92.9 1.1 collective-permute-start.20
  94.1 5.8 %collective-permute-done.19.r2 = f32[256,256]{1,0:T(8,128)S(1)} collective-permute-done((f32[256,256]{1,0:T(8,128)S(1)}, f32[256,256]{1,0:T(8,128)S(1)}, u32[]{:S(2)}, u32[]{:S(2)}) %collective-permute-start.19) | collective-permute-done | bytes 262176 | tf_op jit(solution)/shard_map/ppermute | solution.py:63
  99.9 5.5 %collective-permute-done.20.r3 = f32[256,256]{1,0:T(8,128)S(1)} collective-permute-done((f32[256,256]{1,0:T(8,128)S(1)}, f32[256,256]{1,0:T(8,128)S(1)}, u32[]{:S(2)}, u32[]{:S(2)}) %collective-permute-start.20) | collective-permute-done | bytes 262176 | tf_op jit(solution)/shard_map/ppermute | solution.py:63
  106.0 1.3 collective-permute-start.31
  107.2 0.7 collective-permute-start.30
  107.9 0.7 shard_map.113
  108.6 4.3 %collective-permute-start.25 = (bf16[512,256]{1,0:T(8,128)(2,1)S(1)}, bf16[512,256]{1,0:T(8,128)(2,1)S(1)}, u32[]{:S(2)}, u32[]{:S(2)}) collective-permute-start(bf16[512,256]{1,0:T(8,128)(2,1)S(1)} %get-tuple-element.54), channel_id=1, source_target_pairs={{0,64},{16,80},{32,96},{48,112},{64,0},{80,16},{96,32},{112,48},{1... | collective-permute-start | bytes 786440 | tf_op jit(solution)/shard_map/ppermute | solution.py:63
  112.9 6.1 %collective-permute-start.26 = (bf16[512,256]{1,0:T(8,128)(2,1)S(1)}, bf16[512,256]{1,0:T(8,128)(2,1)S(1)}, u32[]{:S(2)}, u32[]{:S(2)}) collective-permute-start(bf16[512,256]{1,0:T(8,128)(2,1)S(1)} %get-tuple-element.55), channel_id=1, source_target_pairs={{0,128},{16,144},{32,160},{48,176},{64,192},{80,208},{96,224},{112... | collective-permute-start | bytes 786440 | tf_op jit(solution)/shard_map/ppermute | solution.py:63
  119.0 2.4 %shard_map.114.mine = f32[512,1024]{1,0:T(8,128)S(1)} custom-call(s32[16]{0:T(128)S(1)} %copy-done.4, bf16[1024,256]{1,0:T(8,128)(2,1)S(1)} %copy-done, bf16[1024,256]{1,0:T(8,128)(2,1)S(1)} %collective-permute-done.a1.refs_2_.g1, bf16[1024,256]{1,0:T(8,128)(2,1)S(1)} %collective-permute-done.1.after.refs_3_.g2, ...), custom_call_target="tpu_custom_call" | custom-call | flops 4000000000 | bytes 1 | tf_op jit(solution)/shard_map/pallas_call | solution.py:107
  121.4 0.6 shard_map.116
  122.1 2.0 %collective-permute-start.21 = (bf16[256,1024]{1,0:T(8,128)(2,1)S(1)}, bf16[256,1024]{1,0:T(8,128)(2,1)S(1)}, u32[]{:S(2)}, u32[]{:S(2)}) collective-permute-start(bf16[256,1024]{1,0:T(8,128)(2,1)S(1)} %shard_map.116), channel_id=1, source_target_pairs={{0,2},{1,3},{2,0},{3,1},{4,6},{5,7},{6,4},{7,5},{8,10},{9,11},{10,... | collective-permute-start | bytes 1572872 | tf_op jit(solution)/shard_map/ppermute | solution.py:63
  124.0 4.5 %collective-permute-start.27 = (bf16[512,256]{1,0:T(8,128)(2,1)S(1)}, bf16[512,256]{1,0:T(8,128)(2,1)S(1)}, u32[]{:S(2)}, u32[]{:S(2)}) collective-permute-start(bf16[512,256]{1,0:T(8,128)(2,1)S(1)} %get-tuple-element.56), channel_id=1, source_target_pairs={{0,192},{16,208},{32,224},{48,240},{64,128},{80,144},{96,160},{112... | collective-permute-start | bytes 786440 | tf_op jit(solution)/shard_map/ppermute | solution.py:63
  128.6 7.9 %collective-permute-start.33 = (f32[256,256]{1,0:T(8,128)S(1)}, f32[256,256]{1,0:T(8,128)S(1)}, u32[]{:S(2)}, u32[]{:S(2)}) collective-permute-start(f32[256,256]{1,0:T(8,128)S(1)} %convert_add_fusion.a0), channel_id=1, source_target_pairs={{0,128},{16,144},{32,160},{48,176},{64,192},{80,208},{96,224},{112... | collective-permute-start | bytes 786440 | tf_op jit(solution)/shard_map/ppermute | solution.py:63
  136.6 1.6 collective-permute-done.27.r3
  138.1 0.7 shard_map.119
  138.8 5.3 %collective-permute-start.28 = (f32[256,256]{1,0:T(8,128)S(1)}, f32[256,256]{1,0:T(8,128)S(1)}, u32[]{:S(2)}, u32[]{:S(2)}) collective-permute-start(f32[256,256]{1,0:T(8,128)S(1)} %get-tuple-element.57.after.later), channel_id=1, source_target_pairs={{0,0},{1,16},{2,2},{3,18},{4,64},{5,80},{6,66},{7,82},{8,76},{9,92... | collective-permute-start | bytes 786440 | tf_op jit(solution)/shard_map/ppermute | solution.py:462
  144.1 1.2 collective-permute-start.29
  145.3 7.0 %collective-permute-done.33.a2 = f32[256,256]{1,0:T(8,128)S(1)} collective-permute-done((f32[256,256]{1,0:T(8,128)S(1)}, f32[256,256]{1,0:T(8,128)S(1)}, u32[]{:S(2)}, u32[]{:S(2)}) %collective-permute-start.33) | collective-permute-done | bytes 262176 | tf_op jit(solution)/shard_map/ppermute | solution.py:63
  152.3 0.6 shard_map.120.near
  153.1 0.7 shard_map.117
  153.8 7.4 %collective-permute-start.22 = (bf16[64,1024]{1,0:T(8,128)(2,1)S(1)}, bf16[64,1024]{1,0:T(8,128)(2,1)S(1)}, u32[]{:S(2)}, u32[]{:S(2)}) collective-permute-start(bf16[64,1024]{1,0:T(8,128)(2,1)S(1)} %get-tuple-element.51), channel_id=1, source_target_pairs={{0,1},{1,0},{2,3},{3,2},{4,5},{5,4},{6,7},{7,6},{8,9},{9,8},{10,11... | collective-permute-start | bytes 393224 | tf_op jit(solution)/shard_map/ppermute | solution.py:63
  161.1 1.6 collective-permute-start.24
  162.7 0.7 convert_add_fusion.1
  163.4 1.9 %collective-permute-done.22.p1 = bf16[64,1024]{1,0:T(8,128)(2,1)S(1)} collective-permute-done((bf16[64,1024]{1,0:T(8,128)(2,1)S(1)}, bf16[64,1024]{1,0:T(8,128)(2,1)S(1)}, u32[]{:S(2)}, u32[]{:S(2)}) %collective-permute-start.22) | collective-permute-done | bytes 131104 | tf_op jit(solution)/shard_map/ppermute | solution.py:63
  165.4 4.2 %collective-permute-done.23.p2 = bf16[64,1024]{1,0:T(8,128)(2,1)S(1)} collective-permute-done((bf16[64,1024]{1,0:T(8,128)(2,1)S(1)}, bf16[64,1024]{1,0:T(8,128)(2,1)S(1)}, u32[]{:S(2)}, u32[]{:S(2)}) %collective-permute-start.23) | collective-permute-done | bytes 131104 | tf_op jit(solution)/shard_map/ppermute | solution.py:63
  169.6 2.2 %shard_map.118 = f32[64,4096]{1,0:T(8,128)} custom-call(s32[16]{0:T(128)S(1)} %copy-done.4, bf16[64,4096]{1,0:T(8,128)(2,1)S(1)} %copy-done.3, bf16[64,4096]{1,0:T(8,128)(2,1)S(1)} %copy-done.8, f32[1,4096]{1,0:T(1,128)S(1)} %bitcast.4, f32[64,1024]{1,0:T(8,128)S(1)} %get-tuple-element.50.p0, bf16[64,1024]{1,0:T(8,128)(2,1)S(1)} %collective-permute-done.22.p1, ...), custom_call_target="tpu_custom_call" | custom-call | flops 6000000000 | bytes 1 | tf_op jit(solution)/shard_map/pallas_call | solution.py:107
  171.8 2.1 %shard_map.121 = f32[2,256,1024]{2,1,0:T(8,128)} custom-call(s32[16]{0:T(128)S(1)} %copy-done.4, f32[4,256,256]{2,1,0:T(8,128)S(1)} %shard_map.120.near, f32[4,256,256]{2,1,0:T(8,128)S(1)} %collective-permute-done.35.far), custom_call_target="tpu_custom_call" | custom-call | flops 6000000000 | bytes 1 | tf_op jit(solution)/shard_map/pallas_call | solution.py:107
  (48 shorter events, 2.6 us)
Async XLA Ops:
  0.6 8.3 %copy-start = (bf16[1024,256]{1,0:T(8,128)(2,1)S(1)}, bf16[1024,256]{1,0:T(8,128)(2,1)}, u32[]{:S(2)}) copy-start(bf16[1024,256]{1,0:T(8,128)(2,1)} %refs_1_.3) | copy-start | bytes 1572868
  0.6 22.0 %copy-start.2 = (bf16[2,1024,128]{2,1,0:T(8,128)(2,1)S(1)}, bf16[2,1024,128]{2,1,0:T(8,128)(2,1)}, u32[]{:S(2)}) copy-start(bf16[2,1024,128]{2,1,0:T(8,128)(2,1)} %gkv.1) | copy-start | bytes 1572868
  2.0 20.6 %copy-start.4 = (s32[16]{0:T(128)S(1)}, s32[16]{0:T(128)}, u32[]{:S(2)}) copy-start(s32[16]{0:T(128)} %dynamic-slice_bitcast_fusion.place.refs_0_) | copy-start | bytes 196
  5.4 17.3 %collective-permute-start.3 = (bf16[512,256]{1,0:T(8,128)(2,1)}, bf16[512,256]{1,0:T(8,128)(2,1)S(1)}, u32[]{:S(2)}, u32[]{:S(2)}) collective-permute-start(bf16[512,256]{1,0:T(8,128)(2,1)} %get-tuple-element.32), channel_id=1, source_target_pairs={{0,1},{1,0},{2,3},{3,2},{4,5},{5,4},{6,7},{7,6},{8,9},{9,8},{10,11... | collective-permute-start | bytes 786440 | tf_op jit(solution)/shard_map/ppermute | solution.py:63
  6.5 16.2 %collective-permute-start.4 = (bf16[512,256]{1,0:T(8,128)(2,1)}, bf16[512,256]{1,0:T(8,128)(2,1)S(1)}, u32[]{:S(2)}, u32[]{:S(2)}) collective-permute-start(bf16[512,256]{1,0:T(8,128)(2,1)} %get-tuple-element.33), channel_id=1, source_target_pairs={{0,4},{1,5},{2,6},{3,7},{4,0},{5,1},{6,2},{7,3},{8,12},{9,13},{10,... | collective-permute-start | bytes 786440 | tf_op jit(solution)/shard_map/ppermute | solution.py:63
  8.0 14.6 %collective-permute-start.5 = (bf16[512,256]{1,0:T(8,128)(2,1)}, bf16[512,256]{1,0:T(8,128)(2,1)S(1)}, u32[]{:S(2)}, u32[]{:S(2)}) collective-permute-start(bf16[512,256]{1,0:T(8,128)(2,1)} %get-tuple-element.34), channel_id=1, source_target_pairs={{0,5},{1,4},{2,7},{3,6},{4,1},{5,0},{6,3},{7,2},{8,13},{9,12},{10,... | collective-permute-start | bytes 786440 | tf_op jit(solution)/shard_map/ppermute | solution.py:63
  8.9 35.0 %collective-permute-start.1 = (bf16[1024,256]{1,0:T(8,128)(2,1)S(1)}, bf16[1024,256]{1,0:T(8,128)(2,1)S(1)}, u32[]{:S(2)}, u32[]{:S(2)}) collective-permute-start(bf16[1024,256]{1,0:T(8,128)(2,1)S(1)} %copy-done), channel_id=1, source_target_pairs={{0,4},{1,5},{2,6},{3,7},{4,0},{5,1},{6,2},{7,3},{8,12},{9,13},{10,... | collective-permute-start | bytes 1572872 | tf_op jit(solution)/shard_map/ppermute | solution.py:63
  10.5 12.1 %collective-permute-start.6 = (bf16[2,128,256]{2,1,0:T(8,128)(2,1)}, bf16[2,128,256]{2,1,0:T(8,128)(2,1)S(1)}, u32[]{:S(2)}, u32[]{:S(2)}) collective-permute-start(bf16[2,128,256]{2,1,0:T(8,128)(2,1)} %get-tuple-element.35), channel_id=1, source_target_pairs={{0,2},{1,3},{2,0},{3,1},{4,6},{5,7},{6,4},{7,5},{8,10},{9,11},{10,... | collective-permute-start | bytes 393224 | tf_op jit(solution)/shard_map/ppermute | solution.py:63
  22.7 1.0 copy-start.1
  23.6 0.8 copy-start.6
  25.1 24.4 %collective-permute-start.7 = (bf16[2,1024,128]{2,1,0:T(8,128)(2,1)S(1)}, bf16[2,1024,128]{2,1,0:T(8,128)(2,1)S(1)}, u32[]{:S(2)}, u32[]{:S(2)}) collective-permute-start(bf16[2,1024,128]{2,1,0:T(8,128)(2,1)S(1)} %get-tuple-element.37.own), channel_id=1, source_target_pairs={{0,1},{1,0},{2,3},{3,2},{4,5},{5,4},{6,7},{7,6},{8,9},{9,8},{10,11... | collective-permute-start | bytes 1572872 | tf_op jit(solution)/shard_map/ppermute | solution.py:63
  26.8 25.0 %collective-permute-start.9 = (bf16[256,1024]{1,0:T(8,128)(2,1)S(1)}, bf16[256,1024]{1,0:T(8,128)(2,1)S(1)}, u32[]{:S(2)}, u32[]{:S(2)}) collective-permute-start(bf16[256,1024]{1,0:T(8,128)(2,1)S(1)} %get-tuple-element.40.n0), channel_id=1, source_target_pairs={{0,2},{1,3},{2,0},{3,1},{4,6},{5,7},{6,4},{7,5},{8,10},{9,11},{10,... | collective-permute-start | bytes 1572872 | tf_op jit(solution)/shard_map/ppermute | solution.py:63
  27.7 24.1 %collective-permute-start.10 = (bf16[256,1024]{1,0:T(8,128)(2,1)S(1)}, bf16[256,1024]{1,0:T(8,128)(2,1)S(1)}, u32[]{:S(2)}, u32[]{:S(2)}) collective-permute-start(bf16[256,1024]{1,0:T(8,128)(2,1)S(1)} %get-tuple-element.40.n0), channel_id=1, source_target_pairs={{0,12},{1,13},{2,14},{3,15},{4,8},{5,9},{6,10},{7,11},{8,4},{9,5},... | collective-permute-start | bytes 1572872 | tf_op jit(solution)/shard_map/ppermute | solution.py:63
  30.7 13.3 %collective-permute-start.8 = (bf16[2,128,256]{2,1,0:T(8,128)(2,1)S(1)}, bf16[2,128,256]{2,1,0:T(8,128)(2,1)S(1)}, u32[]{:S(2)}, u32[]{:S(2)}) collective-permute-start(bf16[2,128,256]{2,1,0:T(8,128)(2,1)S(1)} %get-tuple-element.39), channel_id=1, source_target_pairs={{0,12},{1,13},{2,14},{3,15},{4,8},{5,9},{6,10},{7,11},{8,4},{9,5},... | collective-permute-start | bytes 393224 | tf_op jit(solution)/shard_map/ppermute | solution.py:63
  44.0 0.8 copy-start.5
  45.4 17.1 %collective-permute-start.12 = (bf16[4,384,256]{2,1,0:T(8,128)(2,1)S(1)}, bf16[4,384,256]{2,1,0:T(8,128)(2,1)S(1)}, u32[]{:S(2)}, u32[]{:S(2)}) collective-permute-start(bf16[4,384,256]{2,1,0:T(8,128)(2,1)S(1)} %shard_map.105.a0.w0), channel_id=1, source_target_pairs={{0,64},{16,80},{32,96},{48,112},{64,0},{80,16},{96,32},{112,48},{1... | collective-permute-start | bytes 2359304 | tf_op jit(solution)/shard_map/ppermute | solution.py:63
  47.0 13.5 %collective-permute-start = (bf16[1024,256]{1,0:T(8,128)(2,1)S(1)}, bf16[1024,256]{1,0:T(8,128)(2,1)S(1)}, u32[]{:S(2)}, u32[]{:S(2)}) collective-permute-start(bf16[1024,256]{1,0:T(8,128)(2,1)S(1)} %copy-done), channel_id=1, source_target_pairs={{0,1},{1,0},{2,3},{3,2},{4,5},{5,4},{6,7},{7,6},{8,9},{9,8},{10,11... | collective-permute-start | bytes 1572872 | tf_op jit(solution)/shard_map/ppermute | solution.py:63
  52.4 9.9 %collective-permute-start.11 = (bf16[2,1024,128]{2,1,0:T(8,128)(2,1)S(1)}, bf16[2,1024,128]{2,1,0:T(8,128)(2,1)S(1)}, u32[]{:S(2)}, u32[]{:S(2)}) collective-permute-start(bf16[2,1024,128]{2,1,0:T(8,128)(2,1)S(1)} %shard_map.106.kv0.refs_5_), channel_id=1, source_target_pairs={{0,4},{1,5},{2,6},{3,7},{4,0},{5,1},{6,2},{7,3},{8,12},{9,13},{10,... | collective-permute-start | bytes 1572872 | tf_op jit(solution)/shard_map/ppermute | solution.py:63
  54.1 10.7 %collective-permute-start.13 = (bf16[256,1024]{1,0:T(8,128)(2,1)S(1)}, bf16[256,1024]{1,0:T(8,128)(2,1)S(1)}, u32[]{:S(2)}, u32[]{:S(2)}) collective-permute-start(bf16[256,1024]{1,0:T(8,128)(2,1)S(1)} %collective-permute-done.9.a1.n1), channel_id=1, source_target_pairs={{0,12},{1,13},{2,14},{3,15},{4,8},{5,9},{6,10},{7,11},{8,4},{9,5},... | collective-permute-start | bytes 1572872 | tf_op jit(solution)/shard_map/ppermute | solution.py:63
  65.5 7.4 %collective-permute-start.14 = (bf16[4,128,1536]{2,1,0:T(8,128)(2,1)S(1)}, bf16[4,128,1536]{2,1,0:T(8,128)(2,1)S(1)}, u32[]{:S(2)}, u32[]{:S(2)}) collective-permute-start(bf16[4,128,1536]{2,1,0:T(8,128)(2,1)S(1)} %shard_map.107.mine.after), channel_id=1, source_target_pairs={{0,16},{16,0},{32,48},{48,32},{64,80},{80,64},{96,112},{112,96},{1... | collective-permute-start | bytes 4718600 | tf_op jit(solution)/shard_map/ppermute | solution.py:63
  67.6 3.0 %collective-permute-start.15 = (f32[1024,256]{1,0:T(8,128)S(1)}, f32[1024,256]{1,0:T(8,128)S(1)}, u32[]{:S(2)}, u32[]{:S(2)}) collective-permute-start(f32[1024,256]{1,0:T(8,128)S(1)} %get-tuple-element.42), channel_id=1, source_target_pairs={{0,16},{16,0},{32,48},{48,32},{64,80},{80,64},{96,112},{112,96},{1... | collective-permute-start | bytes 3145736 | tf_op jit(solution)/shard_map/ppermute | solution.py:63
  68.1 13.9 %collective-permute-start.2 = (bf16[1024,256]{1,0:T(8,128)(2,1)S(1)}, bf16[1024,256]{1,0:T(8,128)(2,1)S(1)}, u32[]{:S(2)}, u32[]{:S(2)}) collective-permute-start(bf16[1024,256]{1,0:T(8,128)(2,1)S(1)} %collective-permute-done.a1.refs_2_.g1), channel_id=1, source_target_pairs={{0,4},{1,5},{2,6},{3,7},{4,0},{5,1},{6,2},{7,3},{8,12},{9,13},{10,... | collective-permute-start | bytes 1572872 | tf_op jit(solution)/shard_map/ppermute | solution.py:63
  71.2 10.9 %collective-permute-start.16 = (f32[256,256]{1,0:T(8,128)S(1)}, f32[256,256]{1,0:T(8,128)S(1)}, u32[]{:S(2)}, u32[]{:S(2)}) collective-permute-start(f32[256,256]{1,0:T(8,128)S(1)} %get-tuple-element.43), channel_id=1, source_target_pairs={{0,64},{16,80},{32,96},{48,112},{64,0},{80,16},{96,32},{112,48},{1... | collective-permute-start | bytes 786440 | tf_op jit(solution)/shard_map/ppermute | solution.py:63
  87.5 20.4 %collective-permute-start.17 = (f32[2,1024,256]{2,1,0:T(8,128)S(1)}, f32[2,1024,256]{2,1,0:T(8,128)S(1)}, u32[]{:S(2)}, u32[]{:S(2)}) collective-permute-start(f32[2,1024,256]{2,1,0:T(8,128)S(1)} %get-tuple-element.45), channel_id=1, source_target_pairs={{0,16},{16,0},{32,48},{48,32},{64,80},{80,64},{96,112},{112,96},{1... | collective-permute-start | bytes 6291464 | tf_op jit(solution)/shard_map/ppermute | solution.py:63
  87.6 33.8 %collective-permute-start.18 = (bf16[512,1024]{1,0:T(8,128)(2,1)S(1)}, bf16[512,1024]{1,0:T(8,128)(2,1)S(1)}, u32[]{:S(2)}, u32[]{:S(2)}) collective-permute-start(bf16[512,1024]{1,0:T(8,128)(2,1)S(1)} %shard_map.111.after), channel_id=1, source_target_pairs={{0,12},{1,13},{2,14},{3,15},{4,8},{5,9},{6,10},{7,11},{8,4},{9,5},... | collective-permute-start | bytes 3145736 | tf_op jit(solution)/shard_map/ppermute | solution.py:63
  89.9 10.0 %collective-permute-start.19 = (f32[256,256]{1,0:T(8,128)S(1)}, f32[256,256]{1,0:T(8,128)S(1)}, u32[]{:S(2)}, u32[]{:S(2)}) collective-permute-start(f32[256,256]{1,0:T(8,128)S(1)} %get-tuple-element.48), channel_id=1, source_target_pairs={{0,128},{16,144},{32,160},{48,176},{64,192},{80,208},{96,224},{112... | collective-permute-start | bytes 786440 | tf_op jit(solution)/shard_map/ppermute | solution.py:63
  92.9 12.5 %collective-permute-start.20 = (f32[256,256]{1,0:T(8,128)S(1)}, f32[256,256]{1,0:T(8,128)S(1)}, u32[]{:S(2)}, u32[]{:S(2)}) collective-permute-start(f32[256,256]{1,0:T(8,128)S(1)} %get-tuple-element.49), channel_id=1, source_target_pairs={{0,192},{16,208},{32,224},{48,240},{64,128},{80,144},{96,160},{112... | collective-permute-start | bytes 786440 | tf_op jit(solution)/shard_map/ppermute | solution.py:63
  106.0 18.1 %collective-permute-start.31 = (bf16[256,256]{1,0:T(8,128)(2,1)S(1)}, bf16[256,256]{1,0:T(8,128)(2,1)S(1)}, u32[]{:S(2)}, u32[]{:S(2)}) collective-permute-start(bf16[256,256]{1,0:T(8,128)(2,1)S(1)} %shard_map.115.after), channel_id=1, source_target_pairs={{0,32},{1,33},{2,96},{3,97},{4,36},{5,37},{6,100},{7,101},{8,164},... | collective-permute-start | bytes 393224 | tf_op jit(solution)/shard_map/ppermute | solution.py:441
  107.2 21.3 %collective-permute-start.30 = (bf16[256,256]{1,0:T(8,128)(2,1)S(1)}, bf16[256,256]{1,0:T(8,128)(2,1)S(1)}, u32[]{:S(2)}, u32[]{:S(2)}) collective-permute-start(bf16[256,256]{1,0:T(8,128)(2,1)S(1)} %shard_map.115.after), channel_id=1, source_target_pairs={{0,0},{1,1},{2,64},{3,65},{4,4},{5,5},{6,68},{7,69},{8,132},{9,133... | collective-permute-start | bytes 393224 | tf_op jit(solution)/shard_map/ppermute | solution.py:441
  108.6 20.0 %collective-permute-start.25 = (bf16[512,256]{1,0:T(8,128)(2,1)S(1)}, bf16[512,256]{1,0:T(8,128)(2,1)S(1)}, u32[]{:S(2)}, u32[]{:S(2)}) collective-permute-start(bf16[512,256]{1,0:T(8,128)(2,1)S(1)} %get-tuple-element.54), channel_id=1, source_target_pairs={{0,64},{16,80},{32,96},{48,112},{64,0},{80,16},{96,32},{112,48},{1... | collective-permute-start | bytes 786440 | tf_op jit(solution)/shard_map/ppermute | solution.py:63
  112.9 23.6 %collective-permute-start.26 = (bf16[512,256]{1,0:T(8,128)(2,1)S(1)}, bf16[512,256]{1,0:T(8,128)(2,1)S(1)}, u32[]{:S(2)}, u32[]{:S(2)}) collective-permute-start(bf16[512,256]{1,0:T(8,128)(2,1)S(1)} %get-tuple-element.55), channel_id=1, source_target_pairs={{0,128},{16,144},{32,160},{48,176},{64,192},{80,208},{96,224},{112... | collective-permute-start | bytes 786440 | tf_op jit(solution)/shard_map/ppermute | solution.py:63
  122.1 31.0 %collective-permute-start.21 = (bf16[256,1024]{1,0:T(8,128)(2,1)S(1)}, bf16[256,1024]{1,0:T(8,128)(2,1)S(1)}, u32[]{:S(2)}, u32[]{:S(2)}) collective-permute-start(bf16[256,1024]{1,0:T(8,128)(2,1)S(1)} %shard_map.116), channel_id=1, source_target_pairs={{0,2},{1,3},{2,0},{3,1},{4,6},{5,7},{6,4},{7,5},{8,10},{9,11},{10,... | collective-permute-start | bytes 1572872 | tf_op jit(solution)/shard_map/ppermute | solution.py:63
  124.0 14.1 %collective-permute-start.27 = (bf16[512,256]{1,0:T(8,128)(2,1)S(1)}, bf16[512,256]{1,0:T(8,128)(2,1)S(1)}, u32[]{:S(2)}, u32[]{:S(2)}) collective-permute-start(bf16[512,256]{1,0:T(8,128)(2,1)S(1)} %get-tuple-element.56), channel_id=1, source_target_pairs={{0,192},{16,208},{32,224},{48,240},{64,128},{80,144},{96,160},{112... | collective-permute-start | bytes 786440 | tf_op jit(solution)/shard_map/ppermute | solution.py:63
  128.5 15.6 %collective-permute-start.32 = (f32[256,256]{1,0:T(8,128)S(1)}, f32[256,256]{1,0:T(8,128)S(1)}, u32[]{:S(2)}, u32[]{:S(2)}) collective-permute-start(f32[256,256]{1,0:T(8,128)S(1)} %convert_add_fusion.a0), channel_id=1, source_target_pairs={{0,64},{16,80},{32,96},{48,112},{64,0},{80,16},{96,32},{112,48},{1... | collective-permute-start | bytes 786440 | tf_op jit(solution)/shard_map/ppermute | solution.py:63
  128.6 23.7 %collective-permute-start.33 = (f32[256,256]{1,0:T(8,128)S(1)}, f32[256,256]{1,0:T(8,128)S(1)}, u32[]{:S(2)}, u32[]{:S(2)}) collective-permute-start(f32[256,256]{1,0:T(8,128)S(1)} %convert_add_fusion.a0), channel_id=1, source_target_pairs={{0,128},{16,144},{32,160},{48,176},{64,192},{80,208},{96,224},{112... | collective-permute-start | bytes 786440 | tf_op jit(solution)/shard_map/ppermute | solution.py:63
  136.6 15.8 %collective-permute-start.34 = (f32[256,256]{1,0:T(8,128)S(1)}, f32[256,256]{1,0:T(8,128)S(1)}, u32[]{:S(2)}, u32[]{:S(2)}) collective-permute-start(f32[256,256]{1,0:T(8,128)S(1)} %convert_add_fusion.a0), channel_id=1, source_target_pairs={{0,192},{16,208},{32,224},{48,240},{64,128},{80,144},{96,160},{112... | collective-permute-start | bytes 786440 | tf_op jit(solution)/shard_map/ppermute | solution.py:63
  138.8 23.9 %collective-permute-start.28 = (f32[256,256]{1,0:T(8,128)S(1)}, f32[256,256]{1,0:T(8,128)S(1)}, u32[]{:S(2)}, u32[]{:S(2)}) collective-permute-start(f32[256,256]{1,0:T(8,128)S(1)} %get-tuple-element.57.after.later), channel_id=1, source_target_pairs={{0,0},{1,16},{2,2},{3,18},{4,64},{5,80},{6,66},{7,82},{8,76},{9,92... | collective-permute-start | bytes 786440 | tf_op jit(solution)/shard_map/ppermute | solution.py:462
  144.1 17.1 %collective-permute-start.29 = (bf16[256,256]{1,0:T(8,128)(2,1)S(1)}, bf16[256,256]{1,0:T(8,128)(2,1)S(1)}, u32[]{:S(2)}, u32[]{:S(2)}) collective-permute-start(bf16[256,256]{1,0:T(8,128)(2,1)S(1)} %get-tuple-element.58), channel_id=1, source_target_pairs={{0,32},{1,48},{2,34},{3,50},{4,96},{5,112},{6,98},{7,114},{8,108},... | collective-permute-start | bytes 393224 | tf_op jit(solution)/shard_map/ppermute | solution.py:462
  152.9 16.6 %copy-start.3 = (bf16[64,4096]{1,0:T(8,128)(2,1)S(1)}, bf16[64,4096]{1,0:T(8,128)(2,1)}, u32[]{:S(2)}) copy-start(bf16[64,4096]{1,0:T(8,128)(2,1)} %x_ref.1) | copy-start | bytes 1572868
  152.9 16.6 %copy-start.7 = (f32[4096]{0:T(1024)S(1)}, f32[4096]{0:T(1024)}, u32[]{:S(2)}) copy-start(f32[4096]{0:T(1024)} %param.10) | copy-start | bytes 49156
  153.0 16.6 %copy-start.8 = (bf16[64,4096]{1,0:T(8,128)(2,1)S(1)}, bf16[64,4096]{1,0:T(8,128)(2,1)}, u32[]{:S(2)}) copy-start(bf16[64,4096]{1,0:T(8,128)(2,1)} %og_ref.1) | copy-start | bytes 1572868
  153.0 18.8 %collective-permute-start.35 = (f32[4,256,256]{2,1,0:T(8,128)S(1)}, f32[4,256,256]{2,1,0:T(8,128)S(1)}, u32[]{:S(2)}, u32[]{:S(2)}) collective-permute-start(f32[4,256,256]{2,1,0:T(8,128)S(1)} %shard_map.120.near), channel_id=1, source_target_pairs={{0,16},{16,0},{32,48},{48,32},{64,80},{80,64},{96,112},{112,96},{1... | collective-permute-start | bytes 3145736 | tf_op jit(solution)/shard_map/ppermute | solution.py:63
  153.8 11.6 %collective-permute-start.22 = (bf16[64,1024]{1,0:T(8,128)(2,1)S(1)}, bf16[64,1024]{1,0:T(8,128)(2,1)S(1)}, u32[]{:S(2)}, u32[]{:S(2)}) collective-permute-start(bf16[64,1024]{1,0:T(8,128)(2,1)S(1)} %get-tuple-element.51), channel_id=1, source_target_pairs={{0,1},{1,0},{2,3},{3,2},{4,5},{5,4},{6,7},{7,6},{8,9},{9,8},{10,11... | collective-permute-start | bytes 393224 | tf_op jit(solution)/shard_map/ppermute | solution.py:63
  161.1 8.4 %collective-permute-start.23 = (bf16[64,1024]{1,0:T(8,128)(2,1)S(1)}, bf16[64,1024]{1,0:T(8,128)(2,1)S(1)}, u32[]{:S(2)}, u32[]{:S(2)}) collective-permute-start(bf16[64,1024]{1,0:T(8,128)(2,1)S(1)} %get-tuple-element.52), channel_id=1, source_target_pairs={{0,4},{1,5},{2,6},{3,7},{4,0},{5,1},{6,2},{7,3},{8,12},{9,13},{10,... | collective-permute-start | bytes 393224 | tf_op jit(solution)/shard_map/ppermute | solution.py:63
  161.1 8.4 %collective-permute-start.24 = (bf16[64,1024]{1,0:T(8,128)(2,1)S(1)}, bf16[64,1024]{1,0:T(8,128)(2,1)S(1)}, u32[]{:S(2)}, u32[]{:S(2)}) collective-permute-start(bf16[64,1024]{1,0:T(8,128)(2,1)S(1)} %get-tuple-element.53), channel_id=1, source_target_pairs={{0,5},{1,4},{2,7},{3,6},{4,1},{5,0},{6,3},{7,2},{8,13},{9,12},{10,... | collective-permute-start | bytes 393224 | tf_op jit(solution)/shard_map/ppermute | solution.py:63

commit v5 on v4

--- a/solution.py
+++ b/solution.py
@@ -95,6 +95,9 @@
     "keyval_lay_kernel": 6 * 10**9,
     "side_kernel": 20 * 10**9,
     "rows1": 4 * 10**9,
+    "keyval_ring_kernel": 10**11,
+    "turn_sum_kernel": 10**11,
+    "keyval_pair_kernel": 20 * 10**9,
 }
 
 SMEM = pl.BlockSpec(memory_space=pltpu.SMEM)

time: 174 us -> 164 us (0.943)
  the two profiles are of different devices: /device:TPU:160 before, /device:TPU:17 now
where the time goes in v5:
time: 164 us; the launch traced here: 163 us
  waiting for transfers between devices  66.3 us (40%)
  starting transfers between devices  66 us (40%)
  Pallas kernels  25.3 us (15%)
  local copies, waits for them, and re-layouts  4.02 us (2%)
    ppermute x32, waiting for transfers between devices, exchange(): return lax.ppermute(v, axis, [(i, i ^ flip) for i in range(16)])  59.7 us
    ppermute x32, starting transfers between devices, exchange(): return lax.ppermute(v, axis, [(i, i ^ flip) for i in range(16)])  36.4 us
    pallas_call x19, Pallas kernels, call(): pl.pallas_call(kernel, out_shape=[jax.ShapeDtypeStruct(s, d) for s, d in...  25.3 us
    ppermute x1, starting transfers between devices, shards(): lax.ppermute(q_keep, everywhere, query_turn(0))  15.3 us
    ppermute x2, starting transfers between devices, shards(): lax.ppermute(kv_ring, everywhere, keyval_turn(over)).astype(F32)  11.2 us
    ppermute x1, waiting for transfers between devices, shards(): lax.ppermute(q_send, everywhere, query_turn(1)).astype(F32)  6.53 us
  transfers between devices with their start and end apart: 36, of which 13 were waited for; matrix products, arithmetic and copies ran while one was open for 0% of the time, Pallas kernels for 11%

profile of v5, /device:TPU:17, one launch (start us, length us, event | category | flops | bytes accessed | tf_op | source)
XLA Modules:
  0.0 163.3 jit_solution(17176354054496342186)
XLA Ops:
  0.7 1.4 dynamic-slice_bitcast_fusion.place.refs_0_
  2.0 3.3 %shard_map.103 = (bf16[512,256]{1,0:T(8,128)(2,1)}, bf16[512,256]{1,0:T(8,128)(2,1)}, bf16[512,256]{1,0:T(8,128)(2,1)}, bf16[512,256]{1,0:T(8,128)(2,1)}, bf16[1...) custom-call(s32[16]{0:T(128)} %dynamic-slice_bitcast_fusion.place.refs_0_, ...), custom_call_target="tpu_custom_call" | custom-call | bytes 1 | tf_op jit(solution)/shard_map/pallas_call | solution.py:110
  5.4 1.7 %collective-permute-start.3 = (bf16[512,256]{1,0:T(8,128)(2,1)}, bf16[512,256]{1,0:T(8,128)(2,1)S(1)}, u32[]{:S(2)}, u32[]{:S(2)}) collective-permute-start(bf16[512,256]{1,0:T(8,128)(2,1)} %get-tuple-element.32), channel_id=1, source_target_pairs={{0,1},{1,0},{2,3},{3,2},{4,5},{5,4},{6,7},{7,6},{8,9},{9,8},{10,11... | collective-permute-start | bytes 786440 | tf_op jit(solution)/shard_map/ppermute | solution.py:63
  7.1 1.0 collective-permute-start.4
  8.1 0.3 collective-permute-start.5
  8.4 1.0 collective-permute-start.1
  9.4 3.0 %collective-permute-start.6 = (bf16[2,128,256]{2,1,0:T(8,128)(2,1)}, bf16[2,128,256]{2,1,0:T(8,128)(2,1)S(1)}, u32[]{:S(2)}, u32[]{:S(2)}) collective-permute-start(bf16[2,128,256]{2,1,0:T(8,128)(2,1)} %get-tuple-element.35), channel_id=1, source_target_pairs={{0,2},{1,3},{2,0},{3,1},{4,6},{5,7},{6,4},{7,5},{8,10},{9,11},{10,... | collective-permute-start | bytes 393224 | tf_op jit(solution)/shard_map/ppermute | solution.py:63
  12.4 8.5 %collective-permute-done.6.k1 = bf16[2,128,256]{2,1,0:T(8,128)(2,1)S(1)} collective-permute-done((bf16[2,128,256]{2,1,0:T(8,128)(2,1)}, bf16[2,128,256]{2,1,0:T(8,128)(2,1)S(1)}, u32[]{:S(2)}, u32[]{:S(2)}) %collective-permute-start.6) | collective-permute-done | bytes 131104 | tf_op jit(solution)/shard_map/ppermute | solution.py:63
  20.9 1.5 collective-permute-done.5.m3
  22.4 0.9 copy-done.1
  23.4 0.8 copy-done.6
  24.2 0.6 shard_map.104
  24.8 2.4 %collective-permute-start.7 = (bf16[2,1024,128]{2,1,0:T(8,128)(2,1)S(1)}, bf16[2,1024,128]{2,1,0:T(8,128)(2,1)S(1)}, u32[]{:S(2)}, u32[]{:S(2)}) collective-permute-start(bf16[2,1024,128]{2,1,0:T(8,128)(2,1)S(1)} %get-tuple-element.37.own), channel_id=1, source_target_pairs={{0,1},{1,0},{2,3},{3,2},{4,5},{5,4},{6,7},{7,6},{8,9},{9,8},{10,11... | collective-permute-start | bytes 1572872 | tf_op jit(solution)/shard_map/ppermute | solution.py:63
  27.2 2.0 %collective-permute-start.9 = (bf16[256,1024]{1,0:T(8,128)(2,1)S(1)}, bf16[256,1024]{1,0:T(8,128)(2,1)S(1)}, u32[]{:S(2)}, u32[]{:S(2)}) collective-permute-start(bf16[256,1024]{1,0:T(8,128)(2,1)S(1)} %get-tuple-element.40.n0), channel_id=1, source_target_pairs={{0,2},{1,3},{2,0},{3,1},{4,6},{5,7},{6,4},{7,5},{8,10},{9,11},{10,... | collective-permute-start | bytes 1572872 | tf_op jit(solution)/shard_map/ppermute | solution.py:63
  29.2 1.5 collective-permute-start.8
  30.6 12.6 %collective-permute-done.8.k23 = bf16[2,128,256]{2,1,0:T(8,128)(2,1)S(1)} collective-permute-done((bf16[2,128,256]{2,1,0:T(8,128)(2,1)S(1)}, bf16[2,128,256]{2,1,0:T(8,128)(2,1)S(1)}, u32[]{:S(2)}, u32[]{:S(2)}) %collective-permute-start.8) | collective-permute-done | bytes 131104 | tf_op jit(solution)/shard_map/ppermute | solution.py:63
  43.2 0.8 copy-done.5
  44.1 0.6 shard_map.105.a0.w0
  44.7 1.3 collective-permute-start.12
  46.0 0.4 collective-permute-start
  46.4 2.3 %collective-permute-done.7.got = bf16[2,1024,128]{2,1,0:T(8,128)(2,1)S(1)} collective-permute-done((bf16[2,1024,128]{2,1,0:T(8,128)(2,1)S(1)}, bf16[2,1024,128]{2,1,0:T(8,128)(2,1)S(1)}, u32[]{:S(2)}, u32[]{:S(2)}) %collective-permute-start.7) | collective-permute-done | bytes 524320 | tf_op jit(solution)/shard_map/ppermute | solution.py:63
  48.7 0.7 shard_map.106.kv0.refs_5_
  49.4 0.8 collective-permute-start.11
  50.1 10.4 %collective-permute-done.a1.refs_2_.g1 = bf16[1024,256]{1,0:T(8,128)(2,1)S(1)} collective-permute-done((bf16[1024,256]{1,0:T(8,128)(2,1)S(1)}, bf16[1024,256]{1,0:T(8,128)(2,1)S(1)}, u32[]{:S(2)}, u32[]{:S(2)}) %collective-permute-start) | collective-permute-done | bytes 524320 | tf_op jit(solution)/shard_map/ppermute | solution.py:63
  60.7 0.7 shard_map.107.mine.after
  61.4 1.9 %shard_map.109 = (f32[1024,256]{1,0:T(8,128)S(1)}, f32[1024,256]{1,0:T(8,128)S(1)}) custom-call(s32[16]{0:T(128)S(1)} %copy-done.4, bf16[256,1024]{1,0:T(8,128)(2,1)S(1)} %get-tuple-element.40.n0, bf16[256,1024]{1,0:T(8,128)(2,1)S(1)} %collective-permute-done.9.a1.n1, bf16[256,1024]{1,0:T(8,128)(2,1)S(1)} %collective-permute-done.10.a2.n2, ...), custom_call_target="tpu_custom_call" | custom-call | bytes 1 | tf_op jit(solution)/shard_map/pallas_call | solution.py:110
  63.3 4.1 %collective-permute-start.15 = (f32[1024,256]{1,0:T(8,128)S(1)}, f32[1024,256]{1,0:T(8,128)S(1)}, u32[]{:S(2)}, u32[]{:S(2)}) collective-permute-start(f32[1024,256]{1,0:T(8,128)S(1)} %get-tuple-element.42), channel_id=1, source_target_pairs={{0,16},{16,0},{32,48},{48,32},{64,80},{80,64},{96,112},{112,96},{1... | collective-permute-start | bytes 3145736 | tf_op jit(solution)/shard_map/ppermute | solution.py:63
  67.4 1.8 %collective-permute-start.2 = (bf16[1024,256]{1,0:T(8,128)(2,1)S(1)}, bf16[1024,256]{1,0:T(8,128)(2,1)S(1)}, u32[]{:S(2)}, u32[]{:S(2)}) collective-permute-start(bf16[1024,256]{1,0:T(8,128)(2,1)S(1)} %collective-permute-done.a1.refs_2_.g1), channel_id=1, source_target_pairs={{0,4},{1,5},{2,6},{3,7},{4,0},{5,1},{6,2},{7,3},{8,12},{9,13},{10,... | collective-permute-start | bytes 1572872 | tf_op jit(solution)/shard_map/ppermute | solution.py:63
  69.2 0.4 collective-permute-start.14
  69.7 0.7 shard_map.110
  70.4 1.3 collective-permute-start.16
  71.7 2.5 %collective-permute-start.19 = (f32[256,256]{1,0:T(8,128)S(1)}, f32[256,256]{1,0:T(8,128)S(1)}, u32[]{:S(2)}, u32[]{:S(2)}) collective-permute-start(f32[256,256]{1,0:T(8,128)S(1)} %get-tuple-element.48), channel_id=1, source_target_pairs={{0,128},{16,144},{32,160},{48,176},{64,192},{80,208},{96,224},{112... | collective-permute-start | bytes 786440 | tf_op jit(solution)/shard_map/ppermute | solution.py:63
  74.2 0.2 collective-permute-start.20
  74.4 0.7 shard_map.108.refs_7_
  75.1 6.2 %collective-permute-done.2.refs_4_.g3 = bf16[1024,256]{1,0:T(8,128)(2,1)S(1)} collective-permute-done((bf16[1024,256]{1,0:T(8,128)(2,1)S(1)}, bf16[1024,256]{1,0:T(8,128)(2,1)S(1)}, u32[]{:S(2)}, u32[]{:S(2)}) %collective-permute-start.2) | collective-permute-done | bytes 524320 | tf_op jit(solution)/shard_map/ppermute | solution.py:63
  81.4 2.4 %shard_map.111.after = bf16[512,1024]{1,0:T(8,128)(2,1)S(1)} custom-call(s32[16]{0:T(128)S(1)} %copy-done.4, bf16[1024,256]{1,0:T(8,128)(2,1)S(1)} %copy-done, bf16[1024,256]{1,0:T(8,128)(2,1)S(1)} %collective-permute-done.a1.refs_2_.g1, bf16[1024,256]{1,0:T(8,128)(2,1)S(1)} %collective-permute-done.1.after.refs_3_.g2, ...), custom_call_target="tpu_custom_call" | custom-call | bytes 1 | tf_op jit(solution)/shard_map/pallas_call | solution.py:110
  83.9 3.0 %shard_map.112 = (f32[2,1024,256]{2,1,0:T(8,128)S(1)}, f32[2,1024,256]{2,1,0:T(8,128)S(1)}) custom-call(s32[16]{0:T(128)S(1)} %copy-done.4, bf16[256,1024]{1,0:T(8,128)(2,1)S(1)} %get-tuple-element.40.n0, bf16[256,1024]{1,0:T(8,128)(2,1)S(1)} %collective-permute-done.9.a1.n1, bf16[256,1024]{1,0:T(8,128)(2,1)S(1)} %collective-permute-done.10.a2.n2, ...), custom_call_target="tpu_custom_call" | custom-call | bytes 1 | tf_op jit(solution)/shard_map/pallas_call | solution.py:110
  86.9 1.1 collective-permute-start.17
  88.1 0.6 shard_map.115.after
  88.7 9.3 %collective-permute-start.31 = (bf16[256,256]{1,0:T(8,128)(2,1)S(1)}, bf16[256,256]{1,0:T(8,128)(2,1)S(1)}, u32[]{:S(2)}, u32[]{:S(2)}) collective-permute-start(bf16[256,256]{1,0:T(8,128)(2,1)S(1)} %shard_map.115.after), channel_id=1, source_target_pairs={{0,32},{1,33},{2,96},{3,97},{4,36},{5,37},{6,100},{7,101},{8,164},... | collective-permute-start | bytes 393224 | tf_op jit(solution)/shard_map/ppermute | solution.py:444
  98.0 1.9 %collective-permute-start.30 = (bf16[256,256]{1,0:T(8,128)(2,1)S(1)}, bf16[256,256]{1,0:T(8,128)(2,1)S(1)}, u32[]{:S(2)}, u32[]{:S(2)}) collective-permute-start(bf16[256,256]{1,0:T(8,128)(2,1)S(1)} %shard_map.115.after), channel_id=1, source_target_pairs={{0,0},{1,1},{2,64},{3,65},{4,4},{5,5},{6,68},{7,69},{8,132},{9,133... | collective-permute-start | bytes 393224 | tf_op jit(solution)/shard_map/ppermute | solution.py:444
  99.9 0.7 shard_map.113
  100.8 0.9 collective-permute-start.26
  101.7 2.4 %shard_map.114.mine = f32[512,1024]{1,0:T(8,128)S(1)} custom-call(s32[16]{0:T(128)S(1)} %copy-done.4, bf16[1024,256]{1,0:T(8,128)(2,1)S(1)} %copy-done, bf16[1024,256]{1,0:T(8,128)(2,1)S(1)} %collective-permute-done.a1.refs_2_.g1, bf16[1024,256]{1,0:T(8,128)(2,1)S(1)} %collective-permute-done.1.after.refs_3_.g2, ...), custom_call_target="tpu_custom_call" | custom-call | flops 4000000000 | bytes 1 | tf_op jit(solution)/shard_map/pallas_call | solution.py:110
  104.1 9.5 %collective-permute-done.18.got.far = bf16[512,1024]{1,0:T(8,128)(2,1)S(1)} collective-permute-done((bf16[512,1024]{1,0:T(8,128)(2,1)S(1)}, bf16[512,1024]{1,0:T(8,128)(2,1)S(1)}, u32[]{:S(2)}, u32[]{:S(2)}) %collective-permute-start.18) | collective-permute-done | bytes 1048608 | tf_op jit(solution)/shard_map/ppermute | solution.py:63
  113.6 0.6 shard_map.116
  114.2 2.9 %collective-permute-start.21 = (bf16[256,1024]{1,0:T(8,128)(2,1)S(1)}, bf16[256,1024]{1,0:T(8,128)(2,1)S(1)}, u32[]{:S(2)}, u32[]{:S(2)}) collective-permute-start(bf16[256,1024]{1,0:T(8,128)(2,1)S(1)} %shard_map.116), channel_id=1, source_target_pairs={{0,2},{1,3},{2,0},{3,1},{4,6},{5,7},{6,4},{7,5},{8,10},{9,11},{10,... | collective-permute-start | bytes 1572872 | tf_op jit(solution)/shard_map/ppermute | solution.py:63
  117.1 0.4 collective-permute-start.27
  117.5 0.9 collective-permute-start.32
  118.4 2.7 %collective-permute-start.33 = (f32[256,256]{1,0:T(8,128)S(1)}, f32[256,256]{1,0:T(8,128)S(1)}, u32[]{:S(2)}, u32[]{:S(2)}) collective-permute-start(f32[256,256]{1,0:T(8,128)S(1)} %convert_add_fusion.a0), channel_id=1, source_target_pairs={{0,128},{16,144},{32,160},{48,176},{64,192},{80,208},{96,224},{112... | collective-permute-start | bytes 786440 | tf_op jit(solution)/shard_map/ppermute | solution.py:63
  121.1 0.4 collective-permute-start.34
  121.5 2.8 %collective-permute-done.27.r3 = bf16[512,256]{1,0:T(8,128)(2,1)S(1)} collective-permute-done((bf16[512,256]{1,0:T(8,128)(2,1)S(1)}, bf16[512,256]{1,0:T(8,128)(2,1)S(1)}, u32[]{:S(2)}, u32[]{:S(2)}) %collective-permute-start.27) | collective-permute-done | bytes 262176 | tf_op jit(solution)/shard_map/ppermute | solution.py:63
  124.3 0.7 shard_map.119
  125.0 15.3 %collective-permute-start.28 = (f32[256,256]{1,0:T(8,128)S(1)}, f32[256,256]{1,0:T(8,128)S(1)}, u32[]{:S(2)}, u32[]{:S(2)}) collective-permute-start(f32[256,256]{1,0:T(8,128)S(1)} %get-tuple-element.57.after.later), channel_id=1, source_target_pairs={{0,0},{1,16},{2,2},{3,18},{4,64},{5,80},{6,66},{7,82},{8,76},{9,92... | collective-permute-start | bytes 786440 | tf_op jit(solution)/shard_map/ppermute | solution.py:465
  140.3 3.1 %collective-permute-start.29 = (bf16[256,256]{1,0:T(8,128)(2,1)S(1)}, bf16[256,256]{1,0:T(8,128)(2,1)S(1)}, u32[]{:S(2)}, u32[]{:S(2)}) collective-permute-start(bf16[256,256]{1,0:T(8,128)(2,1)S(1)} %get-tuple-element.58), channel_id=1, source_target_pairs={{0,32},{1,48},{2,34},{3,50},{4,96},{5,112},{6,98},{7,114},{8,108},... | collective-permute-start | bytes 393224 | tf_op jit(solution)/shard_map/ppermute | solution.py:465
  143.4 0.6 shard_map.120.near
  144.0 1.3 collective-permute-start.35
  145.4 0.7 shard_map.117
  146.3 6.5 %collective-permute-done.29 = bf16[256,256]{1,0:T(8,128)(2,1)S(1)} collective-permute-done((bf16[256,256]{1,0:T(8,128)(2,1)S(1)}, bf16[256,256]{1,0:T(8,128)(2,1)S(1)}, u32[]{:S(2)}, u32[]{:S(2)}) %collective-permute-start.29) | collective-permute-done | bytes 131104 | tf_op jit(solution)/shard_map/ppermute | solution.py:465
  152.8 0.7 convert_add_fusion.1
  153.6 2.2 %collective-permute-done.23.p2 = bf16[64,1024]{1,0:T(8,128)(2,1)S(1)} collective-permute-done((bf16[64,1024]{1,0:T(8,128)(2,1)S(1)}, bf16[64,1024]{1,0:T(8,128)(2,1)S(1)}, u32[]{:S(2)}, u32[]{:S(2)}) %collective-permute-start.23) | collective-permute-done | bytes 131104 | tf_op jit(solution)/shard_map/ppermute | solution.py:63
  155.7 3.3 %collective-permute-done.24.p3 = bf16[64,1024]{1,0:T(8,128)(2,1)S(1)} collective-permute-done((bf16[64,1024]{1,0:T(8,128)(2,1)S(1)}, bf16[64,1024]{1,0:T(8,128)(2,1)S(1)}, u32[]{:S(2)}, u32[]{:S(2)}) %collective-permute-start.24) | collective-permute-done | bytes 131104 | tf_op jit(solution)/shard_map/ppermute | solution.py:63
  159.0 2.2 %shard_map.118 = f32[64,4096]{1,0:T(8,128)} custom-call(s32[16]{0:T(128)S(1)} %copy-done.4, bf16[64,4096]{1,0:T(8,128)(2,1)S(1)} %copy-done.3, bf16[64,4096]{1,0:T(8,128)(2,1)S(1)} %copy-done.8, f32[1,4096]{1,0:T(1,128)S(1)} %bitcast.4, f32[64,1024]{1,0:T(8,128)S(1)} %get-tuple-element.50.p0, bf16[64,1024]{1,0:T(8,128)(2,1)S(1)} %collective-permute-done.22.p1, ...), custom_call_target="tpu_custom_call" | custom-call | flops 6000000000 | bytes 1 | tf_op jit(solution)/shard_map/pallas_call | solution.py:110
  161.2 2.1 %shard_map.121 = f32[2,256,1024]{2,1,0:T(8,128)} custom-call(s32[16]{0:T(128)S(1)} %copy-done.4, f32[4,256,256]{2,1,0:T(8,128)S(1)} %shard_map.120.near, f32[4,256,256]{2,1,0:T(8,128)S(1)} %collective-permute-done.35.far), custom_call_target="tpu_custom_call" | custom-call | flops 6000000000 | bytes 1 | tf_op jit(solution)/shard_map/pallas_call | solution.py:110
  (48 shorter events, 0.8 us)
Async XLA Ops:
  0.6 7.7 %copy-start = (bf16[1024,256]{1,0:T(8,128)(2,1)S(1)}, bf16[1024,256]{1,0:T(8,128)(2,1)}, u32[]{:S(2)}) copy-start(bf16[1024,256]{1,0:T(8,128)(2,1)} %refs_1_.3) | copy-start | bytes 1572868
  0.6 21.8 %copy-start.2 = (bf16[2,1024,128]{2,1,0:T(8,128)(2,1)S(1)}, bf16[2,1024,128]{2,1,0:T(8,128)(2,1)}, u32[]{:S(2)}) copy-start(bf16[2,1024,128]{2,1,0:T(8,128)(2,1)} %gkv.1) | copy-start | bytes 1572868
  2.0 20.4 %copy-start.4 = (s32[16]{0:T(128)S(1)}, s32[16]{0:T(128)}, u32[]{:S(2)}) copy-start(s32[16]{0:T(128)} %dynamic-slice_bitcast_fusion.place.refs_0_) | copy-start | bytes 196
  5.4 15.5 %collective-permute-start.3 = (bf16[512,256]{1,0:T(8,128)(2,1)}, bf16[512,256]{1,0:T(8,128)(2,1)S(1)}, u32[]{:S(2)}, u32[]{:S(2)}) collective-permute-start(bf16[512,256]{1,0:T(8,128)(2,1)} %get-tuple-element.32), channel_id=1, source_target_pairs={{0,1},{1,0},{2,3},{3,2},{4,5},{5,4},{6,7},{7,6},{8,9},{9,8},{10,11... | collective-permute-start | bytes 786440 | tf_op jit(solution)/shard_map/ppermute | solution.py:63
  7.1 13.8 %collective-permute-start.4 = (bf16[512,256]{1,0:T(8,128)(2,1)}, bf16[512,256]{1,0:T(8,128)(2,1)S(1)}, u32[]{:S(2)}, u32[]{:S(2)}) collective-permute-start(bf16[512,256]{1,0:T(8,128)(2,1)} %get-tuple-element.33), channel_id=1, source_target_pairs={{0,4},{1,5},{2,6},{3,7},{4,0},{5,1},{6,2},{7,3},{8,12},{9,13},{10,... | collective-permute-start | bytes 786440 | tf_op jit(solution)/shard_map/ppermute | solution.py:63
  8.1 14.3 %collective-permute-start.5 = (bf16[512,256]{1,0:T(8,128)(2,1)}, bf16[512,256]{1,0:T(8,128)(2,1)S(1)}, u32[]{:S(2)}, u32[]{:S(2)}) collective-permute-start(bf16[512,256]{1,0:T(8,128)(2,1)} %get-tuple-element.34), channel_id=1, source_target_pairs={{0,5},{1,4},{2,7},{3,6},{4,1},{5,0},{6,3},{7,2},{8,13},{9,12},{10,... | collective-permute-start | bytes 786440 | tf_op jit(solution)/shard_map/ppermute | solution.py:63
  8.4 34.9 %collective-permute-start.1 = (bf16[1024,256]{1,0:T(8,128)(2,1)S(1)}, bf16[1024,256]{1,0:T(8,128)(2,1)S(1)}, u32[]{:S(2)}, u32[]{:S(2)}) collective-permute-start(bf16[1024,256]{1,0:T(8,128)(2,1)S(1)} %copy-done), channel_id=1, source_target_pairs={{0,4},{1,5},{2,6},{3,7},{4,0},{5,1},{6,2},{7,3},{8,12},{9,13},{10,... | collective-permute-start | bytes 1572872 | tf_op jit(solution)/shard_map/ppermute | solution.py:63
  9.4 11.5 %collective-permute-start.6 = (bf16[2,128,256]{2,1,0:T(8,128)(2,1)}, bf16[2,128,256]{2,1,0:T(8,128)(2,1)S(1)}, u32[]{:S(2)}, u32[]{:S(2)}) collective-permute-start(bf16[2,128,256]{2,1,0:T(8,128)(2,1)} %get-tuple-element.35), channel_id=1, source_target_pairs={{0,2},{1,3},{2,0},{3,1},{4,6},{5,7},{6,4},{7,5},{8,10},{9,11},{10,... | collective-permute-start | bytes 393224 | tf_op jit(solution)/shard_map/ppermute | solution.py:63
  22.4 1.0 copy-start.1
  23.4 0.8 copy-start.6
  24.8 23.9 %collective-permute-start.7 = (bf16[2,1024,128]{2,1,0:T(8,128)(2,1)S(1)}, bf16[2,1024,128]{2,1,0:T(8,128)(2,1)S(1)}, u32[]{:S(2)}, u32[]{:S(2)}) collective-permute-start(bf16[2,1024,128]{2,1,0:T(8,128)(2,1)S(1)} %get-tuple-element.37.own), channel_id=1, source_target_pairs={{0,1},{1,0},{2,3},{3,2},{4,5},{5,4},{6,7},{7,6},{8,9},{9,8},{10,11... | collective-permute-start | bytes 1572872 | tf_op jit(solution)/shard_map/ppermute | solution.py:63
  27.2 21.5 %collective-permute-start.9 = (bf16[256,1024]{1,0:T(8,128)(2,1)S(1)}, bf16[256,1024]{1,0:T(8,128)(2,1)S(1)}, u32[]{:S(2)}, u32[]{:S(2)}) collective-permute-start(bf16[256,1024]{1,0:T(8,128)(2,1)S(1)} %get-tuple-element.40.n0), channel_id=1, source_target_pairs={{0,2},{1,3},{2,0},{3,1},{4,6},{5,7},{6,4},{7,5},{8,10},{9,11},{10,... | collective-permute-start | bytes 1572872 | tf_op jit(solution)/shard_map/ppermute | solution.py:63
  29.2 19.5 %collective-permute-start.10 = (bf16[256,1024]{1,0:T(8,128)(2,1)S(1)}, bf16[256,1024]{1,0:T(8,128)(2,1)S(1)}, u32[]{:S(2)}, u32[]{:S(2)}) collective-permute-start(bf16[256,1024]{1,0:T(8,128)(2,1)S(1)} %get-tuple-element.40.n0), channel_id=1, source_target_pairs={{0,12},{1,13},{2,14},{3,15},{4,8},{5,9},{6,10},{7,11},{8,4},{9,5},... | collective-permute-start | bytes 1572872 | tf_op jit(solution)/shard_map/ppermute | solution.py:63
  29.2 14.1 %collective-permute-start.8 = (bf16[2,128,256]{2,1,0:T(8,128)(2,1)S(1)}, bf16[2,128,256]{2,1,0:T(8,128)(2,1)S(1)}, u32[]{:S(2)}, u32[]{:S(2)}) collective-permute-start(bf16[2,128,256]{2,1,0:T(8,128)(2,1)S(1)} %get-tuple-element.39), channel_id=1, source_target_pairs={{0,12},{1,13},{2,14},{3,15},{4,8},{5,9},{6,10},{7,11},{8,4},{9,5},... | collective-permute-start | bytes 393224 | tf_op jit(solution)/shard_map/ppermute | solution.py:63
  43.2 0.8 copy-start.5
  44.7 16.0 %collective-permute-start.12 = (bf16[4,384,256]{2,1,0:T(8,128)(2,1)S(1)}, bf16[4,384,256]{2,1,0:T(8,128)(2,1)S(1)}, u32[]{:S(2)}, u32[]{:S(2)}) collective-permute-start(bf16[4,384,256]{2,1,0:T(8,128)(2,1)S(1)} %shard_map.105.a0.w0), channel_id=1, source_target_pairs={{0,64},{16,80},{32,96},{48,112},{64,0},{80,16},{96,32},{112,48},{1... | collective-permute-start | bytes 2359304 | tf_op jit(solution)/shard_map/ppermute | solution.py:63
  46.0 14.6 %collective-permute-start = (bf16[1024,256]{1,0:T(8,128)(2,1)S(1)}, bf16[1024,256]{1,0:T(8,128)(2,1)S(1)}, u32[]{:S(2)}, u32[]{:S(2)}) collective-permute-start(bf16[1024,256]{1,0:T(8,128)(2,1)S(1)} %copy-done), channel_id=1, source_target_pairs={{0,1},{1,0},{2,3},{3,2},{4,5},{5,4},{6,7},{7,6},{8,9},{9,8},{10,11... | collective-permute-start | bytes 1572872 | tf_op jit(solution)/shard_map/ppermute | solution.py:63
  49.4 11.2 %collective-permute-start.11 = (bf16[2,1024,128]{2,1,0:T(8,128)(2,1)S(1)}, bf16[2,1024,128]{2,1,0:T(8,128)(2,1)S(1)}, u32[]{:S(2)}, u32[]{:S(2)}) collective-permute-start(bf16[2,1024,128]{2,1,0:T(8,128)(2,1)S(1)} %shard_map.106.kv0.refs_5_), channel_id=1, source_target_pairs={{0,4},{1,5},{2,6},{3,7},{4,0},{5,1},{6,2},{7,3},{8,12},{9,13},{10,... | collective-permute-start | bytes 1572872 | tf_op jit(solution)/shard_map/ppermute | solution.py:63
  50.1 10.6 %collective-permute-start.13 = (bf16[256,1024]{1,0:T(8,128)(2,1)S(1)}, bf16[256,1024]{1,0:T(8,128)(2,1)S(1)}, u32[]{:S(2)}, u32[]{:S(2)}) collective-permute-start(bf16[256,1024]{1,0:T(8,128)(2,1)S(1)} %collective-permute-done.9.a1.n1), channel_id=1, source_target_pairs={{0,12},{1,13},{2,14},{3,15},{4,8},{5,9},{6,10},{7,11},{8,4},{9,5},... | collective-permute-start | bytes 1572872 | tf_op jit(solution)/shard_map/ppermute | solution.py:63
  63.3 6.4 %collective-permute-start.15 = (f32[1024,256]{1,0:T(8,128)S(1)}, f32[1024,256]{1,0:T(8,128)S(1)}, u32[]{:S(2)}, u32[]{:S(2)}) collective-permute-start(f32[1024,256]{1,0:T(8,128)S(1)} %get-tuple-element.42), channel_id=1, source_target_pairs={{0,16},{16,0},{32,48},{48,32},{64,80},{80,64},{96,112},{112,96},{1... | collective-permute-start | bytes 3145736 | tf_op jit(solution)/shard_map/ppermute | solution.py:63
  67.4 14.0 %collective-permute-start.2 = (bf16[1024,256]{1,0:T(8,128)(2,1)S(1)}, bf16[1024,256]{1,0:T(8,128)(2,1)S(1)}, u32[]{:S(2)}, u32[]{:S(2)}) collective-permute-start(bf16[1024,256]{1,0:T(8,128)(2,1)S(1)} %collective-permute-done.a1.refs_2_.g1), channel_id=1, source_target_pairs={{0,4},{1,5},{2,6},{3,7},{4,0},{5,1},{6,2},{7,3},{8,12},{9,13},{10,... | collective-permute-start | bytes 1572872 | tf_op jit(solution)/shard_map/ppermute | solution.py:63
  69.2 5.2 %collective-permute-start.14 = (bf16[4,128,1536]{2,1,0:T(8,128)(2,1)S(1)}, bf16[4,128,1536]{2,1,0:T(8,128)(2,1)S(1)}, u32[]{:S(2)}, u32[]{:S(2)}) collective-permute-start(bf16[4,128,1536]{2,1,0:T(8,128)(2,1)S(1)} %shard_map.107.mine.after), channel_id=1, source_target_pairs={{0,16},{16,0},{32,48},{48,32},{64,80},{80,64},{96,112},{112,96},{1... | collective-permute-start | bytes 4718600 | tf_op jit(solution)/shard_map/ppermute | solution.py:63
  70.4 11.0 %collective-permute-start.16 = (f32[256,256]{1,0:T(8,128)S(1)}, f32[256,256]{1,0:T(8,128)S(1)}, u32[]{:S(2)}, u32[]{:S(2)}) collective-permute-start(f32[256,256]{1,0:T(8,128)S(1)} %get-tuple-element.43), channel_id=1, source_target_pairs={{0,64},{16,80},{32,96},{48,112},{64,0},{80,16},{96,32},{112,48},{1... | collective-permute-start | bytes 786440 | tf_op jit(solution)/shard_map/ppermute | solution.py:63
  71.7 16.3 %collective-permute-start.19 = (f32[256,256]{1,0:T(8,128)S(1)}, f32[256,256]{1,0:T(8,128)S(1)}, u32[]{:S(2)}, u32[]{:S(2)}) collective-permute-start(f32[256,256]{1,0:T(8,128)S(1)} %get-tuple-element.48), channel_id=1, source_target_pairs={{0,128},{16,144},{32,160},{48,176},{64,192},{80,208},{96,224},{112... | collective-permute-start | bytes 786440 | tf_op jit(solution)/shard_map/ppermute | solution.py:63
  74.2 13.9 %collective-permute-start.20 = (f32[256,256]{1,0:T(8,128)S(1)}, f32[256,256]{1,0:T(8,128)S(1)}, u32[]{:S(2)}, u32[]{:S(2)}) collective-permute-start(f32[256,256]{1,0:T(8,128)S(1)} %get-tuple-element.49), channel_id=1, source_target_pairs={{0,192},{16,208},{32,224},{48,240},{64,128},{80,144},{96,160},{112... | collective-permute-start | bytes 786440 | tf_op jit(solution)/shard_map/ppermute | solution.py:63
  83.8 29.7 %collective-permute-start.18 = (bf16[512,1024]{1,0:T(8,128)(2,1)S(1)}, bf16[512,1024]{1,0:T(8,128)(2,1)S(1)}, u32[]{:S(2)}, u32[]{:S(2)}) collective-permute-start(bf16[512,1024]{1,0:T(8,128)(2,1)S(1)} %shard_map.111.after), channel_id=1, source_target_pairs={{0,12},{1,13},{2,14},{3,15},{4,8},{5,9},{6,10},{7,11},{8,4},{9,5},... | collective-permute-start | bytes 3145736 | tf_op jit(solution)/shard_map/ppermute | solution.py:63
  86.9 12.9 %collective-permute-start.17 = (f32[2,1024,256]{2,1,0:T(8,128)S(1)}, f32[2,1024,256]{2,1,0:T(8,128)S(1)}, u32[]{:S(2)}, u32[]{:S(2)}) collective-permute-start(f32[2,1024,256]{2,1,0:T(8,128)S(1)} %get-tuple-element.45), channel_id=1, source_target_pairs={{0,16},{16,0},{32,48},{48,32},{64,80},{80,64},{96,112},{112,96},{1... | collective-permute-start | bytes 6291464 | tf_op jit(solution)/shard_map/ppermute | solution.py:63
  88.7 28.5 %collective-permute-start.31 = (bf16[256,256]{1,0:T(8,128)(2,1)S(1)}, bf16[256,256]{1,0:T(8,128)(2,1)S(1)}, u32[]{:S(2)}, u32[]{:S(2)}) collective-permute-start(bf16[256,256]{1,0:T(8,128)(2,1)S(1)} %shard_map.115.after), channel_id=1, source_target_pairs={{0,32},{1,33},{2,96},{3,97},{4,36},{5,37},{6,100},{7,101},{8,164},... | collective-permute-start | bytes 393224 | tf_op jit(solution)/shard_map/ppermute | solution.py:444
  98.0 19.5 %collective-permute-start.30 = (bf16[256,256]{1,0:T(8,128)(2,1)S(1)}, bf16[256,256]{1,0:T(8,128)(2,1)S(1)}, u32[]{:S(2)}, u32[]{:S(2)}) collective-permute-start(bf16[256,256]{1,0:T(8,128)(2,1)S(1)} %shard_map.115.after), channel_id=1, source_target_pairs={{0,0},{1,1},{2,64},{3,65},{4,4},{5,5},{6,68},{7,69},{8,132},{9,133... | collective-permute-start | bytes 393224 | tf_op jit(solution)/shard_map/ppermute | solution.py:444
  100.7 17.8 %collective-permute-start.25 = (bf16[512,256]{1,0:T(8,128)(2,1)S(1)}, bf16[512,256]{1,0:T(8,128)(2,1)S(1)}, u32[]{:S(2)}, u32[]{:S(2)}) collective-permute-start(bf16[512,256]{1,0:T(8,128)(2,1)S(1)} %get-tuple-element.54), channel_id=1, source_target_pairs={{0,64},{16,80},{32,96},{48,112},{64,0},{80,16},{96,32},{112,48},{1... | collective-permute-start | bytes 786440 | tf_op jit(solution)/shard_map/ppermute | solution.py:63
  100.8 20.3 %collective-permute-start.26 = (bf16[512,256]{1,0:T(8,128)(2,1)S(1)}, bf16[512,256]{1,0:T(8,128)(2,1)S(1)}, u32[]{:S(2)}, u32[]{:S(2)}) collective-permute-start(bf16[512,256]{1,0:T(8,128)(2,1)S(1)} %get-tuple-element.55), channel_id=1, source_target_pairs={{0,128},{16,144},{32,160},{48,176},{64,192},{80,208},{96,224},{112... | collective-permute-start | bytes 786440 | tf_op jit(solution)/shard_map/ppermute | solution.py:63
  114.2 31.2 %collective-permute-start.21 = (bf16[256,1024]{1,0:T(8,128)(2,1)S(1)}, bf16[256,1024]{1,0:T(8,128)(2,1)S(1)}, u32[]{:S(2)}, u32[]{:S(2)}) collective-permute-start(bf16[256,1024]{1,0:T(8,128)(2,1)S(1)} %shard_map.116), channel_id=1, source_target_pairs={{0,2},{1,3},{2,0},{3,1},{4,6},{5,7},{6,4},{7,5},{8,10},{9,11},{10,... | collective-permute-start | bytes 1572872 | tf_op jit(solution)/shard_map/ppermute | solution.py:63
  117.1 7.2 %collective-permute-start.27 = (bf16[512,256]{1,0:T(8,128)(2,1)S(1)}, bf16[512,256]{1,0:T(8,128)(2,1)S(1)}, u32[]{:S(2)}, u32[]{:S(2)}) collective-permute-start(bf16[512,256]{1,0:T(8,128)(2,1)S(1)} %get-tuple-element.56), channel_id=1, source_target_pairs={{0,192},{16,208},{32,224},{48,240},{64,128},{80,144},{96,160},{112... | collective-permute-start | bytes 786440 | tf_op jit(solution)/shard_map/ppermute | solution.py:63
  117.5 22.8 %collective-permute-start.32 = (f32[256,256]{1,0:T(8,128)S(1)}, f32[256,256]{1,0:T(8,128)S(1)}, u32[]{:S(2)}, u32[]{:S(2)}) collective-permute-start(f32[256,256]{1,0:T(8,128)S(1)} %convert_add_fusion.a0), channel_id=1, source_target_pairs={{0,64},{16,80},{32,96},{48,112},{64,0},{80,16},{96,32},{112,48},{1... | collective-permute-start | bytes 786440 | tf_op jit(solution)/shard_map/ppermute | solution.py:63
  118.4 24.9 %collective-permute-start.33 = (f32[256,256]{1,0:T(8,128)S(1)}, f32[256,256]{1,0:T(8,128)S(1)}, u32[]{:S(2)}, u32[]{:S(2)}) collective-permute-start(f32[256,256]{1,0:T(8,128)S(1)} %convert_add_fusion.a0), channel_id=1, source_target_pairs={{0,128},{16,144},{32,160},{48,176},{64,192},{80,208},{96,224},{112... | collective-permute-start | bytes 786440 | tf_op jit(solution)/shard_map/ppermute | solution.py:63
  121.1 22.3 %collective-permute-start.34 = (f32[256,256]{1,0:T(8,128)S(1)}, f32[256,256]{1,0:T(8,128)S(1)}, u32[]{:S(2)}, u32[]{:S(2)}) collective-permute-start(f32[256,256]{1,0:T(8,128)S(1)} %convert_add_fusion.a0), channel_id=1, source_target_pairs={{0,192},{16,208},{32,224},{48,240},{64,128},{80,144},{96,160},{112... | collective-permute-start | bytes 786440 | tf_op jit(solution)/shard_map/ppermute | solution.py:63
  125.0 27.8 %collective-permute-start.28 = (f32[256,256]{1,0:T(8,128)S(1)}, f32[256,256]{1,0:T(8,128)S(1)}, u32[]{:S(2)}, u32[]{:S(2)}) collective-permute-start(f32[256,256]{1,0:T(8,128)S(1)} %get-tuple-element.57.after.later), channel_id=1, source_target_pairs={{0,0},{1,16},{2,2},{3,18},{4,64},{5,80},{6,66},{7,82},{8,76},{9,92... | collective-permute-start | bytes 786440 | tf_op jit(solution)/shard_map/ppermute | solution.py:465
  140.3 12.5 %collective-permute-start.29 = (bf16[256,256]{1,0:T(8,128)(2,1)S(1)}, bf16[256,256]{1,0:T(8,128)(2,1)S(1)}, u32[]{:S(2)}, u32[]{:S(2)}) collective-permute-start(bf16[256,256]{1,0:T(8,128)(2,1)S(1)} %get-tuple-element.58), channel_id=1, source_target_pairs={{0,32},{1,48},{2,34},{3,50},{4,96},{5,112},{6,98},{7,114},{8,108},... | collective-permute-start | bytes 393224 | tf_op jit(solution)/shard_map/ppermute | solution.py:465
  144.0 15.0 %copy-start.3 = (bf16[64,4096]{1,0:T(8,128)(2,1)S(1)}, bf16[64,4096]{1,0:T(8,128)(2,1)}, u32[]{:S(2)}) copy-start(bf16[64,4096]{1,0:T(8,128)(2,1)} %x_ref.1) | copy-start | bytes 1572868
  144.0 15.0 %copy-start.7 = (f32[4096]{0:T(1024)S(1)}, f32[4096]{0:T(1024)}, u32[]{:S(2)}) copy-start(f32[4096]{0:T(1024)} %param.10) | copy-start | bytes 49156
  144.0 15.0 %copy-start.8 = (bf16[64,4096]{1,0:T(8,128)(2,1)S(1)}, bf16[64,4096]{1,0:T(8,128)(2,1)}, u32[]{:S(2)}) copy-start(bf16[64,4096]{1,0:T(8,128)(2,1)} %og_ref.1) | copy-start | bytes 1572868
  144.0 17.2 %collective-permute-start.35 = (f32[4,256,256]{2,1,0:T(8,128)S(1)}, f32[4,256,256]{2,1,0:T(8,128)S(1)}, u32[]{:S(2)}, u32[]{:S(2)}) collective-permute-start(f32[4,256,256]{2,1,0:T(8,128)S(1)} %shard_map.120.near), channel_id=1, source_target_pairs={{0,16},{16,0},{32,48},{48,32},{64,80},{80,64},{96,112},{112,96},{1... | collective-permute-start | bytes 3145736 | tf_op jit(solution)/shard_map/ppermute | solution.py:63
  146.1 7.5 %collective-permute-start.22 = (bf16[64,1024]{1,0:T(8,128)(2,1)S(1)}, bf16[64,1024]{1,0:T(8,128)(2,1)S(1)}, u32[]{:S(2)}, u32[]{:S(2)}) collective-permute-start(bf16[64,1024]{1,0:T(8,128)(2,1)S(1)} %get-tuple-element.51), channel_id=1, source_target_pairs={{0,1},{1,0},{2,3},{3,2},{4,5},{5,4},{6,7},{7,6},{8,9},{9,8},{10,11... | collective-permute-start | bytes 393224 | tf_op jit(solution)/shard_map/ppermute | solution.py:63
  146.2 9.5 %collective-permute-start.23 = (bf16[64,1024]{1,0:T(8,128)(2,1)S(1)}, bf16[64,1024]{1,0:T(8,128)(2,1)S(1)}, u32[]{:S(2)}, u32[]{:S(2)}) collective-permute-start(bf16[64,1024]{1,0:T(8,128)(2,1)S(1)} %get-tuple-element.52), channel_id=1, source_target_pairs={{0,4},{1,5},{2,6},{3,7},{4,0},{5,1},{6,2},{7,3},{8,12},{9,13},{10,... | collective-permute-start | bytes 393224 | tf_op jit(solution)/shard_map/ppermute | solution.py:63
  152.8 6.2 %collective-permute-start.24 = (bf16[64,1024]{1,0:T(8,128)(2,1)S(1)}, bf16[64,1024]{1,0:T(8,128)(2,1)S(1)}, u32[]{:S(2)}, u32[]{:S(2)}) collective-permute-start(bf16[64,1024]{1,0:T(8,128)(2,1)S(1)} %get-tuple-element.53), channel_id=1, source_target_pairs={{0,5},{1,4},{2,7},{3,6},{4,1},{5,0},{6,3},{7,2},{8,13},{9,12},{10,... | collective-permute-start | bytes 393224 | tf_op jit(solution)/shard_map/ppermute | solution.py:63
